TPU v7x, 128 devices: a whole 4x4x4 slice. The times are simulated.
128 devices in a mesh: row: 16 (over z_hi, y, core), col: 8 (over z_lo, x).
Axes of the slice: x: 4, y: 4, z: 4 (z_hi: 2, z_lo: 2; z = z_hi * 2 + z_lo), core: 2. Of those that a mesh axis runs over, the one named last changes fastest.
Arguments:
- tiles: bfloat16 [128, 128, 1536], P('row', 'col'), may hold values from -6 to 6
- tissue: int32 [128, 128], P('row', 'col'), may hold values from 0 to 1, as said below
- project_in: bfloat16 [1536, 2304], P(('row', 'col')), as said below
- project_out: bfloat16 [768, 1536], P(('row', 'col')), may hold values from -0.21875 to 0.21875
- grad_layer: bfloat16 [128, 128, 1536], P('row', 'col'), may hold values from -6 to 6
Outputs:
- layer_out: bfloat16 [128, 128, 1536], P('row', 'col')
- grad_tiles: bfloat16 [128, 128, 1536], P('row', 'col')
- grad_project_in: float32 [1536, 2304], P(('row', 'col'))
- grad_project_out: float32 [768, 1536], P(('row', 'col'))
Inputs may be any that keep to these rules, and one draw needn't show every extreme that they name: 1 marks a tissue tile, 0 a background tile; tissue lies in patches. `project_in`: query, key and value projections side by side along the second dimension.
All inputs are finite; a program needn't handle non-finite values.
Results may differ from a plain program's by a relative error of at most 0.009.
Values may be sent and summed in bfloat16 or wider, within the bound.
No kernel may reach another device: no remote copies, remote signals or barrier semaphores. Data moves between devices by JAX's collectives and lax.ppermute only.
A program may use at most 128 MiB of HBM per device.

v0:
```python
import jax
import jax.numpy as jnp
from jax import lax
from jax.experimental import pallas as pl
from jax.experimental.pallas import tpu as pltpu
from jax.sharding import Mesh, PartitionSpec as P

HEAD_DIM = 64
WINDOW = 7
D = 1536
DH = 768
HALF = DH // 2
GRID = 128
SIDE = 16
KEY_ROWS = 28
KEY_COLS = 32
QUERY_ROWS = 22
QUERY_COLS = 24
LANE = 128
WIDE = D + LANE

AXES = ("zh", "y", "c", "zl", "x")
STAGES = (("y", "z", "x"), ("z", "x", "y"))

epsilon = 1e-05
masked_score = -1e30
outside_score = -3e30
open_score = 3e38

f32 = jnp.float32
bf16 = jnp.bfloat16


def device(x, y, z, c):
    return (((z // 2 * 4 + y) * 2 + c) * 2 + z % 2) * 4 + x


def stage_pairs(axes, shift):
    pairs = []
    for x in range(4):
        for y in range(4):
            for z in range(4):
                for c in range(2):
                    place = {"x": x, "y": y, "z": z}
                    place[axes[c]] = (place[axes[c]] + shift) % 4
                    pairs.append((device(x, y, z, c), device(place["x"], place["y"], place["z"], c)))
    return pairs


def shifted(value, axes, shift):
    return lax.ppermute(value, AXES, stage_pairs(axes, shift))


def swap_cores(value):
    return lax.ppermute(value, "c", [(0, 1), (1, 0)])


def row_neighbour(value):
    pairs = [(r, r + 1 if r % 2 else r - 1) for r in range(16)]
    return lax.ppermute(value, ("zh", "y", "c"), [(a, b) for a, b in pairs if 0 <= b < 16])


def col_neighbour(value, step):
    pairs = [(i, i + step) for i in range(8)]
    return lax.ppermute(value, ("zl", "x"), [(a, b) for a, b in pairs if 0 <= b < 8])


def gather_stage(block, stage):
    axes = (STAGES[0][stage], STAGES[1][stage])
    far = shifted(block, axes, 2)
    near = shifted(block, axes, 1)
    back = shifted(block, axes, 3)
    return [block, near, far, back]


def scatter_stage(chunks, stage):
    axes = (STAGES[0][stage], STAGES[1][stage])
    far = shifted(chunks[2], axes, 2)
    near = shifted(chunks[1], axes, 3)
    back = shifted(chunks[3], axes, 1)
    return (chunks[0].astype(f32) + near.astype(f32)) + (far.astype(f32) + back.astype(f32))


def by_core(core, mine, other, axis):
    return jnp.where(
        core == 0,
        jnp.concatenate([mine, other], axis=axis),
        jnp.concatenate([other, mine], axis=axis),
    )


def on_chip(kernel, place, arrays, outs, scratch=(), megabytes=14):
    vmem = pl.BlockSpec(memory_space=pltpu.VMEM)
    return pl.pallas_call(
        kernel,
        out_shape=tuple(jax.ShapeDtypeStruct(shape, kind) for shape, kind in outs),
        in_specs=[pl.BlockSpec(memory_space=pltpu.SMEM)] + [vmem] * len(arrays),
        out_specs=(vmem,) * len(outs),
        scratch_shapes=[pltpu.VMEM(shape, kind) for shape, kind in scratch],
        compiler_params=pltpu.CompilerParams(vmem_limit_bytes=megabytes * 1024 * 1024),
        cost_estimate=pl.CostEstimate(flops=1000, bytes_accessed=1000, transcendentals=0),
    )(place, *arrays)


def normalize(values):
    center = values - jnp.mean(values, axis=-1, keepdims=True)
    inverse = lax.rsqrt(jnp.mean(center * center, axis=-1, keepdims=True) + epsilon)
    return (center * inverse, inverse)


def prepare_kernel(place_ref, tiles_ref, grad_ref, live_ref, hidden_out, grad_out, sent_out):
    core = place_ref[1]
    for r in range(8):
        at = pl.ds(r * SIDE, SIDE)
        normed, inverse = normalize(tiles_ref[at, :].astype(f32))
        live = live_ref[at, :]
        lanes = live.astype(bf16)
        hidden_out[at, :D] = normed.astype(bf16)
        hidden_out[at, D:] = lanes
        grad_out[at, :D] = (grad_ref[at, :].astype(f32) * live[:, :1]).astype(bf16)
        grad_out[at, D:] = lanes
    sent_out[:96, :] = hidden_out[pl.ds(pl.multiple_of(core * 32, 16), 96), :]
    sent_out[96:, :] = grad_out[pl.ds(pl.multiple_of(core * 80, 16), 48), :]


def columns_kernel(place_ref, hidden_ref, grad_ref, got_ref, a_out, b_out, right_out, left_out):
    core = place_ref[1]
    a_out[pl.ds(pl.multiple_of(core * 128, 32), 96), :] = got_ref[:96, :]
    a_out[pl.ds(pl.multiple_of((1 - core) * 96, 32), 128), :] = hidden_ref[...]
    b_out[pl.ds(pl.multiple_of(core * 128, 16), 48), :] = got_ref[96:, :]
    b_out[pl.ds(pl.multiple_of((1 - core) * 48, 16), 128), :] = grad_ref[...]
    b_out[176:, :] = jnp.zeros((SIDE, WIDE), bf16)
    upper = lax.broadcasted_iota(jnp.int32, (8, WIDE), 0) < 4
    for m in range(7):
        lines = a_out[32 * m : 32 * m + 32, :].astype(f32)
        right = [pltpu.roll(lines[16 * i + 8 : 16 * i + 16], 4, 0) for i in range(2)]
        right_out[16 * m : 16 * m + 16, :] = jnp.concatenate(right, axis=0).astype(bf16)
        left_out[16 * m : 16 * m + 16, :] = jnp.concatenate([lines[:8], lines[16:24]], axis=0).astype(bf16)
    for m in range(3):
        lines = b_out[64 * m : 64 * m + 64, :].astype(f32)
        right, left = [], []
        for i in (0, 32):
            right.append(jnp.where(upper, pltpu.roll(lines[i + 8 : i + 16], 4, 0), lines[i + 24 : i + 32]))
            left.append(jnp.where(upper, lines[i : i + 8], pltpu.roll(lines[i + 16 : i + 24], 4, 0)))
        at = slice(112 + 16 * m, 128 + 16 * m)
        right_out[at, :] = jnp.concatenate(right, axis=0).astype(bf16)
        left_out[at, :] = jnp.concatenate(left, axis=0).astype(bf16)


def widen_kernel(place_ref, a_ref, b_ref, left_ref, right_ref, a_out, b_out):
    upper = lax.broadcasted_iota(jnp.int32, (8, WIDE), 0) < 4
    for m in range(7):
        left = left_ref[16 * m : 16 * m + 16, :].astype(f32)
        right = right_ref[16 * m : 16 * m + 16, :].astype(f32)
        for i in range(2):
            at = KEY_COLS * (2 * m + i)
            a_out[at : at + SIDE, :] = a_ref[SIDE * (2 * m + i) : SIDE * (2 * m + i + 1), :]
            both = [left[8 * i : 8 * i + 8], right[8 * i : 8 * i + 8]]
            a_out[at + SIDE : at + KEY_COLS, :] = jnp.concatenate(both, axis=0).astype(bf16)
    for m in range(3):
        left = left_ref[112 + 16 * m : 128 + 16 * m, :].astype(f32)
        right = right_ref[112 + 16 * m : 128 + 16 * m, :].astype(f32)
        for i in range(2):
            lines = b_ref[64 * m + 32 * i : 64 * m + 32 * i + 32, :].astype(f32)
            left8, right8 = left[8 * i : 8 * i + 8], right[8 * i : 8 * i + 8]
            pieces = [
                lines[:SIDE],
                jnp.where(upper, left8, pltpu.roll(right8, 4, 0)),
                lines[SIDE:],
                jnp.where(upper, pltpu.roll(left8, 4, 0), right8),
            ]
            at = 2 * QUERY_COLS * (2 * m + i)
            b_out[at : at + 2 * QUERY_COLS, :] = jnp.concatenate(pieces, axis=0).astype(bf16)


def one_hot(hit):
    return jnp.where(hit, 1.0, 0.0).astype(bf16)


def permute_kernel(place_ref, tokens_ref, feature_ref, out):
    def part(n, carry):
        lanes = pl.ds(pl.multiple_of(n * 256, 256), 256)
        feature = lax.broadcasted_iota(jnp.int32, (D, 256), 0)
        order = one_hot(feature == feature_ref[:, lanes])
        out[:, lanes] = jnp.dot(tokens_ref[:, :D], order, preferred_element_type=f32).astype(bf16)
        return carry

    lax.fori_loop(0, D // 256, part, 0)


def out_rows_kernel(place_ref, r0, r1, r2, r3, row_ref, half_out, sent_out):
    core = place_ref[1]

    def part(n, carry):
        first = pl.multiple_of(n * 128, 128)
        for h in range(2):
            row = lax.broadcasted_iota(jnp.int32, (128, D // 4), 0) + (first + h * DH)
            total = jnp.zeros((128, HALF), f32)
            for k, ref in enumerate((r0, r1, r2, r3)):
                order = one_hot(row == row_ref[:, k * 384 : (k + 1) * 384])
                total += jnp.dot(order, ref[...], preferred_element_type=f32)
            half_out[pl.ds(first, 128), h * HALF : (h + 1) * HALF] = total.astype(bf16)
        return carry

    lax.fori_loop(0, DH // 128, part, 0)
    sent_out[...] = half_out[pl.ds(pl.multiple_of((1 - core) * HALF, HALF), HALF), :]


def out_grads_kernel(place_ref, mine_ref, other_ref, grad_ref, row_ref, c0, c1, c2, c3, grads):
    core = place_ref[1]
    over = (((0,), (0,)), ((), ()))
    for attn, side in ((mine_ref, core), (other_ref, 1 - core)):
        for h in range(2):
            to = pl.ds(pl.multiple_of(h * DH + side * HALF, HALF), HALF)
            grads[to, :] = lax.dot_general(
                attn[...], grad_ref[:, h * HALF : (h + 1) * HALF], over, preferred_element_type=f32
            ).astype(bf16)
    lane = lax.broadcasted_iota(jnp.int32, (LANE, LANE), 1).astype(f32)
    for k, chunk in enumerate((c0, c1, c2, c3)):

        def part(n, carry, k=k, chunk=chunk):
            first = pl.multiple_of(n * LANE, LANE)
            row = row_ref[:, pl.ds(k * 384 + first, LANE)].astype(f32)
            row = jnp.transpose(jnp.broadcast_to(row, (LANE, LANE)))
            order = jnp.concatenate([one_hot(lane + m * LANE == row) for m in range(2 * DH // LANE)], axis=1)
            chunk[pl.ds(first, LANE), :] = jnp.dot(order, grads[...], preferred_element_type=f32).astype(bf16)
            return carry

        lax.fori_loop(0, 3, part, 0)


def grad_hidden_kernel(place_ref, grads_ref, w0, w1, w2, w3, feature_ref, mine_out, sent_out, rel):
    core = place_ref[1]
    contract = (((1,), (1,)), ((), ()))
    for k, ref in enumerate((w0, w1, w2, w3)):
        rel[:, k * 384 : (k + 1) * 384] = lax.dot_general(
            grads_ref[...], ref[...], contract, preferred_element_type=f32
        ).astype(bf16)

    def part(n, carry):
        first = pl.multiple_of(n * 256, 256)
        feature = lax.broadcasted_iota(jnp.int32, (256, D), 0) + first
        order = one_hot(feature == feature_ref[...])
        lanes = pl.ds(first, 256)
        for side, out in ((core, mine_out), (1 - core, sent_out)):
            rows = rel[pl.ds(pl.multiple_of(side * 128, 128), 128), :]
            out[:, lanes] = lax.dot_general(rows, order, contract, preferred_element_type=f32).astype(bf16)
        return carry

    lax.fori_loop(0, D // 256, part, 0)


def project_kernel(place_ref, mine_ref, other_ref, half_ref, mine_out, sent_out):
    core = place_ref[1]
    for side, out in ((core, mine_out), (1 - core, sent_out)):
        rows = pl.ds(pl.multiple_of(side * 128, 128), 128)
        total = jnp.dot(
            mine_ref[rows, :],
            half_ref[pl.ds(pl.multiple_of(core * HALF, HALF), HALF), :],
            preferred_element_type=f32,
        )
        total += jnp.dot(
            other_ref[rows, :],
            half_ref[pl.ds(pl.multiple_of((1 - core) * HALF, HALF), HALF), :],
            preferred_element_type=f32,
        )
        out[...] = total


def finish_kernel(
    place_ref, tiles_ref, grad_ref, live_ref, pmine_ref, pother_ref, gmine_ref, gother_ref, layer_out, tiles_out
):
    first = place_ref[1] == 0
    for r in range(8):
        at = pl.ds(r * SIDE, SIDE)
        tiles = tiles_ref[at, :].astype(f32)
        normed, inverse = normalize(tiles)
        live = live_ref[at, :][:, :1]
        mine, other = pmine_ref[at, :], pother_ref[at, :]
        low, high = jnp.where(first, mine, other), jnp.where(first, other, mine)
        layer_out[at, :DH] = (tiles[:, :DH] + low * live).astype(bf16)
        layer_out[at, DH:] = (tiles[:, DH:] + high * live).astype(bf16)
        grad_hidden = gmine_ref[at, :].astype(f32) + gother_ref[at, :].astype(f32)
        grad_norm = inverse * (
            grad_hidden
            - jnp.mean(grad_hidden, axis=-1, keepdims=True)
            - normed * jnp.mean(grad_hidden * normed, axis=-1, keepdims=True)
        )
        tiles_out[at, :] = (grad_ref[at, :].astype(f32) + grad_norm).astype(bf16)


def layer_kernel(
    place_ref, mine_ref, other_ref, w0, w1, w2, w3, amine_ref, aother_ref, gmine_ref, gother_ref, rmine_ref, rother_ref,
    attn_out, grads_out, c0, c1, c2, c3, grad_own,
    packed, hidden, grad_attn, dk, dv, attn, dq, tissue, lines_f32,
):
    base, core, column = place_ref[0], place_ref[1], place_ref[2]
    width = 2 * QUERY_COLS
    span = 8 * KEY_COLS
    half = KEY_ROWS // 2 * KEY_COLS
    half_q = QUERY_ROWS // 2 * QUERY_COLS
    contract = (((1,), (1,)), ((), ()))
    over = (((0,), (0,)), ((), ()))
    chunks = (w0, w1, w2, w3)
    part = D // 4

    dk[...] = jnp.zeros_like(dk)
    dv[...] = jnp.zeros_like(dv)

    for source, side in ((mine_ref, core), (other_ref, 1 - core)):
        own_at = pl.multiple_of((1 - side) * 6 * KEY_COLS, KEY_COLS)
        for r in range(8):
            to = pl.ds(pl.multiple_of((side * 8 + r) * SIDE, SIDE), SIDE)
            hidden[to, :] = source[pl.ds(own_at + r * KEY_COLS, SIDE), :]

        def project(t, carry, source=source, side=side):
            rows = pl.ds(pl.multiple_of(t * 112, 112), 112)
            to = pl.ds(pl.multiple_of(side * half + t * 112, 112), 112)
            total = jnp.dot(source[rows, :part], w0[...], preferred_element_type=f32)
            for k in range(1, 4):
                total += jnp.dot(
                    source[rows, k * part : (k + 1) * part], chunks[k][...], preferred_element_type=f32
                )
            packed[to, :] = total.astype(bf16)
            return carry

        lax.fori_loop(0, 4, project, 0)

    mine_lanes = pl.ds(pl.multiple_of(core * DH, DH), DH)
    other_lanes = pl.ds(pl.multiple_of((1 - core) * DH, DH), DH)
    rmine = rmine_ref[pl.ds(pl.multiple_of(core * HALF, HALF), HALF), :]
    for source, side in ((gmine_ref, core), (gother_ref, 1 - core)):
        to = pl.ds(pl.multiple_of(side * half_q, 8), half_q)
        total = lax.dot_general(source[:, mine_lanes], rmine, contract, preferred_element_type=f32)
        total += lax.dot_general(source[:, other_lanes], rother_ref[...], contract, preferred_element_type=f32)
        grad_attn[to, :] = total[:half_q].astype(bf16).astype(f32)

    for source, side in ((gmine_ref, core), (gother_ref, 1 - core)):
        lines_f32[...] = source[:, mine_lanes].astype(f32)
        for r in range(8):
            own = lines_f32[pl.ds(pl.multiple_of((1 - side) * 72 + 24 * r, 8), SIDE), :]
            grad_own[pl.ds(pl.multiple_of((side * 8 + r) * SIDE, SIDE), SIDE), :] = own.astype(bf16)

    for source, side in ((amine_ref, core), (aother_ref, 1 - core)):
        tissue[pl.ds(pl.multiple_of(side * half, 64), half), :] = source[:, D:].astype(f32)
    alive_line = jnp.concatenate(
        [jnp.transpose(tissue[m * LANE : (m + 1) * LANE, :])[:8] for m in range(7)] + [jnp.zeros((8, LANE), f32)], axis=1
    )
    alive_line = jnp.where(alive_line > 0, open_score, masked_score)
    spot = lax.broadcasted_iota(jnp.int32, (QUERY_COLS, span), 1) % KEY_COLS
    key_col = jnp.where(spot < 16, spot, jnp.where(spot < 20, spot - 20, jnp.where(spot < 24, spot - 28, spot - 8)))
    spot = lax.broadcasted_iota(jnp.int32, (QUERY_COLS, span), 0)
    query_col = jnp.where(spot < 16, spot, jnp.where(spot < 20, spot - 20, spot - 4))
    col_start = jnp.clip(query_col + column - 3, 0, GRID - WINDOW)
    key_col = key_col + column
    col_in = jnp.logical_and(key_col >= col_start, key_col < col_start + WINDOW)
    col_cap = jnp.where(col_in, open_score, outside_score)

    key_line = lax.broadcasted_iota(jnp.int32, (1, span), 1) // KEY_COLS
    low = lax.broadcasted_iota(jnp.int32, (width, LANE), 1) < HEAD_DIM
    low2 = jnp.concatenate([low, jnp.logical_not(low)], axis=0)
    upper = lax.broadcasted_iota(jnp.int32, (8, LANE), 0) < 4

    def block(i, carry):
        row = base - 3 + 2 * i
        start = jnp.clip(row - 3, 0, GRID - 8)
        local = start - (base - 6)
        alive = pltpu.roll(alive_line, lax.rem((32 - local) * KEY_COLS, 32 * KEY_COLS), 1)[:1, :span]
        key_row = key_line + start
        caps = []
        for step in range(2):
            first = jnp.clip(row + step - 3, 0, GRID - WINDOW)
            inside = jnp.logical_and(key_row >= first, key_row < first + WINDOW)
            caps.append(jnp.minimum(col_cap, jnp.where(inside, alive, outside_score)))
        cap = jnp.concatenate(caps + caps, axis=0)
        keys_at = pl.ds(pl.multiple_of(local * KEY_COLS, KEY_COLS), span)
        query_at = pl.multiple_of((3 + 2 * i) * KEY_COLS, KEY_COLS)
        block_at = pl.ds(pl.multiple_of(i * width, width), width)
        groups = range(3)
        lanes = [pl.ds(g * LANE, LANE) for g in groups]
        key = [packed[keys_at, pl.ds(HALF + g * LANE, LANE)] for g in groups]
        value = [packed[keys_at, pl.ds(2 * HALF + g * LANE, LANE)] for g in groups]
        query2, grad2f = [], []
        for g in groups:
            lines = packed[pl.ds(query_at, 2 * KEY_COLS), lanes[g]].astype(f32) * HEAD_DIM ** (-0.5)
            pieces = []
            for step in range(2):
                line = lines[step * KEY_COLS : (step + 1) * KEY_COLS]
                pieces += [line[:SIDE], jnp.where(upper, line[16:24], pltpu.roll(line[24:32], 4, 0))]
            query2.append(jnp.where(low2, jnp.concatenate(pieces + pieces, axis=0), 0.0).astype(bf16))
            grad = grad_attn[block_at, lanes[g]]
            grad2f.append(jnp.where(low2, jnp.concatenate([grad, grad], axis=0), 0.0))
        grad2 = [g.astype(bf16) for g in grad2f]
        raw = [lax.dot_general(query2[g], key[g], contract, preferred_element_type=f32) for g in groups]
        grad_prob = [lax.dot_general(grad2[g], value[g], contract, preferred_element_type=f32) for g in groups]
        prob = []
        for g in groups:
            scores = jnp.minimum(raw[g], cap)
            expon = jnp.exp(scores - jnp.max(scores, axis=1, keepdims=True))
            prob.append(expon * (1.0 / jnp.sum(expon, axis=1, keepdims=True)))
        weights = [p.astype(bf16) for p in prob]
        mixed = [jnp.dot(weights[g], value[g], preferred_element_type=f32).astype(bf16).astype(f32) for g in groups]
        value_sum = [lax.dot_general(weights[g], grad2[g], over, preferred_element_type=f32) for g in groups]
        delta = [jnp.sum(grad2f[g] * mixed[g], axis=1, keepdims=True) for g in groups]
        grad_score = [(prob[g] * (grad_prob[g] - delta[g])).astype(bf16) for g in groups]
        grad_q = [jnp.dot(grad_score[g], key[g], preferred_element_type=f32) for g in groups]
        key_sum = [lax.dot_general(grad_score[g], query2[g], over, preferred_element_type=f32) for g in groups]
        for g in groups:
            attn[block_at, lanes[g]] = jnp.where(low, mixed[g][:width], mixed[g][width:])
            dq[block_at, lanes[g]] = jnp.where(low, grad_q[g][:width], grad_q[g][width:])
            dv[keys_at, lanes[g]] += value_sum[g]
            dk[keys_at, lanes[g]] += key_sum[g]
        return carry

    lax.fori_loop(0, QUERY_ROWS // 2, block, 0)
    for r in range(SIDE):
        own = pl.ds(r * SIDE, SIDE)
        at_query = pl.ds((r + 3) * QUERY_COLS, SIDE)
        at_key = pl.ds((r + 6) * KEY_COLS, SIDE)
        attn_out[own, :] = attn[at_query, :].astype(bf16)
        grads_out[own, :HALF] = (dq[at_query, :] * HEAD_DIM ** (-0.5)).astype(bf16)
        grads_out[own, HALF : 2 * HALF] = dk[at_key, :].astype(bf16)
        grads_out[own, 2 * HALF :] = dv[at_key, :].astype(bf16)
    for k, chunk in enumerate((c0, c1, c2, c3)):
        chunk[...] = lax.dot_general(
            hidden[:, k * part : (k + 1) * part], grads_out[...], over, preferred_element_type=f32
        ).astype(bf16)


def layer(place, *arrays):
    keys, queries = KEY_ROWS * KEY_COLS, QUERY_ROWS * QUERY_COLS
    return on_chip(
        layer_kernel,
        place,
        arrays,
        [((SIDE * SIDE, HALF), bf16), ((SIDE * SIDE, 3 * HALF), bf16)] + [((D // 4, 3 * HALF), bf16)] * 4 + [((SIDE * SIDE, DH), bf16)],
        [
            ((keys, 3 * HALF), bf16),
            ((SIDE * SIDE, D), bf16),
            ((queries, HALF), f32),
            ((keys, HALF), f32),
            ((keys, HALF), f32),
            ((queries, HALF), f32),
            ((queries, HALF), f32),
            ((keys, LANE), f32),
            ((288, DH), f32),
        ],
        30,
    )


def found_places(core, here, place):
    step = [(place // 24) % 4, (place // 96) % 4, place // 384]
    found = {}
    for name in ("x", "y", "z"):
        mine = [lax.rem(here[name] - step[STAGES[c].index(name)] + 4, 4) for c in range(2)]
        found[name] = jnp.where(core == 0, mine[0], mine[1])
    return found


def orders(core, here, place):
    found, inner = found_places(core, here, place), place % 24

    def owner(side):
        return (((found["z"] // 2 * 4 + found["y"]) * 2 + side) * 2 + found["z"] % 2) * 4 + found["x"]

    feature = owner(inner // 12) * 12 + inner % 12
    row = owner(inner % 12 // 6) * 6 + inner % 6 + inner // 12 * DH
    return feature, row


def body(tiles, tissue, project_in, project_out, grad_layer):
    zh, y, core, zl, x = [lax.axis_index(name) for name in AXES]
    z = zh * 2 + zl
    tokens = 8 * SIDE
    place = jnp.stack([(zh * 4 + y) * SIDE, core, (zl * 4 + x) * SIDE]).astype(jnp.int32)

    halves = project_in.reshape(12, 3, 2, HALF)
    first, second = halves[:, :, 0].reshape(12, 3 * HALF), halves[:, :, 1].reshape(12, 3 * HALF)

    def shard(of_in, of_out):
        return jnp.concatenate([of_in, of_out.reshape(6, 2, HALF).transpose(1, 0, 2).reshape(12, HALF)], axis=1)

    shard_first, shard_second = shard(first, project_out[:, :DH]), shard(second, project_out[:, DH:])
    mine = jnp.where(core == 0, shard_first, shard_second)
    theirs = jnp.where(core == 0, shard_second, shard_first)
    flat_tiles, flat_grad = tiles.reshape(tokens, D), grad_layer.reshape(tokens, D)
    live = jnp.broadcast_to(tissue.reshape(tokens, 1).astype(f32), (tokens, LANE))
    own_hidden, own_grad, sent = on_chip(
        prepare_kernel,
        place,
        [flat_tiles, flat_grad, live],
        [((tokens, WIDE), bf16), ((tokens, WIDE), bf16), ((144, WIDE), bf16)],
    )
    here = {"x": x, "y": y, "z": z}
    feature_line, row_line = orders(core, here, lax.broadcasted_iota(jnp.int32, (1, D), 1))

    other, got = swap_cores(theirs), row_neighbour(sent)
    other, got, feature_line, row_line = lax.optimization_barrier((other, got, feature_line, row_line))
    block_in = by_core(core, mine[:, : 3 * HALF], other[:, : 3 * HALF], 0)
    mine_out, other_out = mine[:, 3 * HALF :].reshape(2, 6, HALF), other[:, 3 * HALF :].reshape(2, 6, HALF)
    block_out = by_core(core, mine_out, other_out, 1).reshape(24, HALF)
    block = jnp.concatenate([block_in, block_out], axis=1)
    a, b, to_right, to_left = on_chip(
        columns_kernel,
        place,
        [own_hidden, own_grad, got],
        [((224, WIDE), bf16), ((192, WIDE), bf16), ((160, WIDE), bf16), ((160, WIDE), bf16)],
    )
    block, to_right, to_left = lax.optimization_barrier((block, to_right, to_left))

    parts = gather_stage(block, 0)
    left, right = col_neighbour(to_right, 1), col_neighbour(to_left, -1)
    *parts, left, right = lax.optimization_barrier((*parts, left, right))
    wide_a, wide_b = on_chip(
        widen_kernel, place, [a, b, left, right], [((14 * KEY_COLS, WIDE), bf16), ((12 * QUERY_COLS, WIDE), bf16)]
    )
    block, wide_a, wide_b = lax.optimization_barrier((jnp.concatenate(parts, axis=0), wide_a, wide_b))

    parts = gather_stage(block, 1)
    other_a, other_b = swap_cores(wide_a), swap_cores(wide_b)
    *parts, other_a, other_b = lax.optimization_barrier((*parts, other_a, other_b))
    block_out = jnp.concatenate([part[:, 3 * HALF :] for part in parts], axis=0)
    block_in = jnp.concatenate([part[:, : 3 * HALF] for part in parts], axis=0)
    block_out, block_in = lax.optimization_barrier((block_out, block_in))

    rows_out = gather_stage(block_out, 2)
    weights = gather_stage(block_in, 2)
    permuted = [((14 * KEY_COLS, D), bf16)]
    (hidden_mine,) = on_chip(permute_kernel, place, [wide_a, feature_line], permuted)
    (hidden_other,) = on_chip(permute_kernel, place, [other_a, feature_line], permuted)

    half_out, sent_rows = on_chip(
        out_rows_kernel, place, rows_out + [row_line], [((DH, DH), bf16), ((HALF, DH), bf16)]
    )
    other_rows = swap_cores(sent_rows)

    attention, grad_packed, *chunks_in, grad_own = layer(
        place, hidden_mine, hidden_other, *weights, wide_a, other_a, wide_b, other_b, half_out, other_rows
    )
    total_in = scatter_stage(chunks_in, 2)

    attention_other = swap_cores(attention)
    hidden_kept, hidden_sent = on_chip(
        grad_hidden_kernel,
        place,
        [grad_packed, *weights, feature_line],
        [((tokens, D), bf16)] * 2,
        [((2 * tokens, D), bf16)],
    )
    attention_other, hidden_kept, hidden_sent = lax.optimization_barrier((attention_other, hidden_kept, hidden_sent))
    chunks_out = on_chip(
        out_grads_kernel,
        place,
        [attention, attention_other, grad_own, row_line],
        [((D // 4, HALF), bf16)] * 4,
        [((2 * DH, HALF), bf16)],
    )
    projected, projected_sent = on_chip(
        project_kernel, place, [attention, attention_other, half_out], [((tokens, DH), f32)] * 2
    )
    total = jnp.concatenate([total_in, scatter_stage(chunks_out, 2)], axis=1).astype(bf16)
    total, hidden_kept, hidden_sent, projected, projected_sent = lax.optimization_barrier(
        (total, hidden_kept, hidden_sent, projected, projected_sent)
    )
    total = scatter_stage([total[k * 96 : (k + 1) * 96] for k in range(4)], 1).astype(bf16)
    layer_out, grad_tiles = on_chip(
        finish_kernel,
        place,
        [flat_tiles, flat_grad, live, projected, swap_cores(projected_sent), hidden_kept, swap_cores(hidden_sent)],
        [((tokens, D), bf16)] * 2,
    )
    total, layer_out, grad_tiles = lax.optimization_barrier((total, layer_out, grad_tiles))
    total = scatter_stage([total[k * 24 : (k + 1) * 24] for k in range(4)], 0)

    sums_in = total[:, : 3 * HALF].reshape(2, 12, 3 * HALF)
    sums_out = total[:, 3 * HALF :].reshape(2, 2, 6, HALF).transpose(1, 0, 2, 3).reshape(2, 12, HALF)
    sums = jnp.concatenate([sums_in, sums_out], axis=2)
    kept = jnp.where(core == 0, sums[0], sums[1])
    gotten = swap_cores(jnp.where(core == 0, sums[1], sums[0]))
    grad_project_in = by_core(
        core, kept[:, : 3 * HALF].reshape(12, 3, 1, HALF), gotten[:, : 3 * HALF].reshape(12, 3, 1, HALF), 2
    ).reshape(12, 3 * DH)
    kept_out = kept[:, 3 * HALF :].reshape(2, 6, HALF).transpose(1, 0, 2).reshape(6, DH)
    gotten_out = gotten[:, 3 * HALF :].reshape(2, 6, HALF).transpose(1, 0, 2).reshape(6, DH)
    grad_project_out = by_core(core, kept_out, gotten_out, 1)

    return (
        layer_out.reshape(8, SIDE, D),
        grad_tiles.reshape(8, SIDE, D),
        grad_project_in,
        grad_project_out,
    )


def solution(mesh):
    fine = Mesh(mesh.devices.reshape(2, 4, 2, 2, 4), AXES)
    grid = P(("zh", "y", "c"), ("zl", "x"), None)
    rows = P(AXES, None)
    return jax.shard_map(
        body,
        mesh=fine,
        in_specs=(grid, P(("zh", "y", "c"), ("zl", "x")), rows, rows, grid),
        out_specs=(grid, grid, rows, rows),
        check_vma=False,
    )
```

profile of v0, /device:TPU:1, one launch (start us, length us, event | category | flops | bytes accessed | tf_op | source)
XLA Modules:
  0.0 169.8 jit_solution(15486986280105228690)
XLA Ops:
  4.5 4.6 %collective-permute-start.1 = (bf16[144,1664]{1,0:T(8,128)(2,1)S(1)}, bf16[144,1664]{1,0:T(8,128)(2,1)S(1)}, u32[]{:S(2)}, u32[]{:S(2)}) collective-permute-start(bf16[144,1664]{1,0:T(8,128)(2,1)S(1)} %get-tuple-element.67), channel_id=1, source_target_pairs={{8,16},{16,8},{24,32},{32,24},{40,48},{48,40},{56,64},{64,56},{72,... | collective-permute-start | bytes 1437704 | tf_op jit(solution)/shard_map/ppermute | solution.py:60
  12.6 2.9 %collective-permute-done.1.got_ref = bf16[144,1664]{1,0:T(8,128)(2,1)S(1)} collective-permute-done((bf16[144,1664]{1,0:T(8,128)(2,1)S(1)}, bf16[144,1664]{1,0:T(8,128)(2,1)S(1)}, u32[]{:S(2)}, u32[]{:S(2)}) %collective-permute-start.1) | collective-permute-done | bytes 479264 | tf_op jit(solution)/shard_map/ppermute | solution.py:60
  16.4 3.1 %collective-permute-start.5 = (bf16[160,1664]{1,0:T(8,128)(2,1)S(1)}, bf16[160,1664]{1,0:T(8,128)(2,1)S(1)}, u32[]{:S(2)}, u32[]{:S(2)}) collective-permute-start(bf16[160,1664]{1,0:T(8,128)(2,1)S(1)} %get-tuple-element.75), channel_id=1, source_target_pairs={{0,1},{1,2},{2,3},{3,4},{4,5},{5,6},{6,7},{8,9},{9,10},{10,11},{11... | collective-permute-start | bytes 1597448 | tf_op jit(solution)/shard_map/ppermute | solution.py:65
  20.9 7.1 %collective-permute-start.4 = (bf16[24,1536]{1,0:T(8,128)(2,1)S(1)}, bf16[24,1536]{1,0:T(8,128)(2,1)S(1)}, u32[]{:S(2)}, u32[]{:S(2)}) collective-permute-start(bf16[24,1536]{1,0:T(8,128)(2,1)S(1)} %pad_maximum_fusion.4), channel_id=1, source_target_pairs={{0,48},{8,76},{4,52},{12,8},{64,112},{72,12},{68,116},{76,72},{16,... | collective-permute-start | bytes 221192 | tf_op jit(solution)/shard_map/ppermute | solution.py:51
  30.0 8.8 %collective-permute-done.3 = bf16[24,1536]{1,0:T(8,128)(2,1)S(1)} collective-permute-done((bf16[24,1536]{1,0:T(8,128)(2,1)S(1)}, bf16[24,1536]{1,0:T(8,128)(2,1)S(1)}, u32[]{:S(2)}, u32[]{:S(2)}) %collective-permute-start.3) | collective-permute-done | bytes 73760 | tf_op jit(solution)/shard_map/ppermute | solution.py:51
  41.6 4.4 %collective-permute-done.9 = bf16[96,1536]{1,0:T(8,128)(2,1)S(1)} collective-permute-done((bf16[96,1536]{1,0:T(8,128)(2,1)S(1)}, bf16[96,1536]{1,0:T(8,128)(2,1)S(1)}, u32[]{:S(2)}, u32[]{:S(2)}) %collective-permute-start.9) | collective-permute-done | bytes 294944 | tf_op jit(solution)/shard_map/ppermute | solution.py:51
  47.8 3.1 %collective-permute-done.7 = bf16[96,1536]{1,0:T(8,128)(2,1)S(1)} collective-permute-done((bf16[96,1536]{1,0:T(8,128)(2,1)S(1)}, bf16[96,1536]{1,0:T(8,128)(2,1)S(1)}, u32[]{:S(2)}, u32[]{:S(2)}) %collective-permute-start.7) | collective-permute-done | bytes 294944 | tf_op jit(solution)/shard_map/ppermute | solution.py:51
  51.2 5.5 %collective-permute-start.17 = (bf16[384,384]{1,0:T(8,128)(2,1)S(1)}, bf16[384,384]{1,0:T(8,128)(2,1)S(1)}, u32[]{:S(2)}, u32[]{:S(2)}) collective-permute-start(bf16[384,384]{1,0:T(8,128)(2,1)S(1)} %pad_maximum_fusion.3.r0), channel_id=1, source_target_pairs={{0,3},{8,56},{4,7},{12,60},{64,67},{72,120},{68,71},{76,124},{16,1... | collective-permute-start | bytes 884744 | tf_op jit(solution)/shard_map/ppermute | solution.py:51
  61.1 2.4 %collective-permute-done.17.r3 = bf16[384,384]{1,0:T(8,128)(2,1)S(1)} collective-permute-done((bf16[384,384]{1,0:T(8,128)(2,1)S(1)}, bf16[384,384]{1,0:T(8,128)(2,1)S(1)}, u32[]{:S(2)}, u32[]{:S(2)}) %collective-permute-start.17) | collective-permute-done | bytes 294944 | tf_op jit(solution)/shard_map/ppermute | solution.py:51
  63.9 3.0 %collective-permute-done.15.r1 = bf16[384,384]{1,0:T(8,128)(2,1)S(1)} collective-permute-done((bf16[384,384]{1,0:T(8,128)(2,1)S(1)}, bf16[384,384]{1,0:T(8,128)(2,1)S(1)}, u32[]{:S(2)}, u32[]{:S(2)}) %collective-permute-start.15) | collective-permute-done | bytes 294944 | tf_op jit(solution)/shard_map/ppermute | solution.py:51
  66.9 4.6 %shard_map.89 = (bf16[768,768]{1,0:T(8,128)(2,1)S(1)}, bf16[384,768]{1,0:T(8,128)(2,1)S(1)}) custom-call(s32[3]{0:T(128)S(1)} %pad_add_fusion.place_ref, bf16[384,384]{1,0:T(8,128)(2,1)S(1)} %pad_maximum_fusion.3.r0, bf16[384,384]{1,0:T(8,128)(2,1)S(1)} %collective-permute-done.15.r1, bf16[384,384]{1,0:T(8,128)(2,1)S(1)} %collective-permute-done.16.r2, ...), custom_call_target="tpu_custom_call" | custom-call | flops 1000 | bytes 1000 | tf_op jit(solution)/shard_map/pallas_call | solution.py:94
  72.2 3.7 %shard_map.87.mine_ref = bf16[448,1536]{1,0:T(8,128)(2,1)S(1)} custom-call(s32[3]{0:T(128)S(1)} %pad_add_fusion.place_ref, bf16[448,1664]{1,0:T(8,128)(2,1)S(1)} %get-tuple-element.87.tokens_ref.amine_ref, s32[1,1536]{1,0:T(1,128)S(1)} %get-tuple-element.88.feature_ref), custom_call_target="tpu_custom_call" | custom-call | flops 1000 | bytes 1000 | tf_op jit(solution)/shard_map/pallas_call | solution.py:94
  75.9 3.7 %shard_map.88.other_ref = bf16[448,1536]{1,0:T(8,128)(2,1)S(1)} custom-call(s32[3]{0:T(128)S(1)} %pad_add_fusion.place_ref, bf16[448,1664]{1,0:T(8,128)(2,1)S(1)} %collective-permute-done.10.tokens_ref.aother_ref, s32[1,1536]{1,0:T(1,128)S(1)} %get-tuple-element.88.feature_ref), custom_call_target="tpu_custom_call" | custom-call | flops 1000 | bytes 1000 | tf_op jit(solution)/shard_map/pallas_call | solution.py:94
  79.6 2.9 %collective-permute-done.14.w3 = bf16[384,1152]{1,0:T(8,128)(2,1)S(1)} collective-permute-done((bf16[384,1152]{1,0:T(8,128)(2,1)S(1)}, bf16[384,1152]{1,0:T(8,128)(2,1)S(1)}, u32[]{:S(2)}, u32[]{:S(2)}) %collective-permute-start.14) | collective-permute-done | bytes 884768 | tf_op jit(solution)/shard_map/ppermute | solution.py:51
  82.5 3.4 %collective-permute-done.12.w1 = bf16[384,1152]{1,0:T(8,128)(2,1)S(1)} collective-permute-done((bf16[384,1152]{1,0:T(8,128)(2,1)S(1)}, bf16[384,1152]{1,0:T(8,128)(2,1)S(1)}, u32[]{:S(2)}, u32[]{:S(2)}) %collective-permute-start.12) | collective-permute-done | bytes 884768 | tf_op jit(solution)/shard_map/ppermute | solution.py:51
  85.9 19.1 %shard_map.90 = (bf16[256,384]{1,0:T(8,128)(2,1)S(1)}, bf16[256,1152]{1,0:T(8,128)(2,1)S(1)}, bf16[384,1152]{1,0:T(8,128)(2,1)S(1)}, bf16[384,1152]{1,0:T(8,128)...) custom-call(s32[3]{0:T(128)S(1)} %pad_add_fusion.place_ref, ...), custom_call_target="tpu_custom_call" | custom-call | flops 1000 | bytes 1000 | tf_op jit(solution)/shard_map/pallas_call | solution.py:94
  105.5 5.8 %collective-permute-start.19 = (bf16[384,1152]{1,0:T(8,128)(2,1)S(1)}, bf16[384,1152]{1,0:T(8,128)(2,1)S(1)}, u32[]{:S(2)}, u32[]{:S(2)}) collective-permute-start(bf16[384,1152]{1,0:T(8,128)(2,1)S(1)} %get-tuple-element.103), channel_id=1, source_target_pairs={{0,3},{8,56},{4,7},{12,60},{64,67},{72,120},{68,71},{76,124},{16,1... | collective-permute-start | bytes 2654216 | tf_op jit(solution)/shard_map/ppermute | solution.py:51
  111.9 5.9 %shard_map.91 = (bf16[128,1536]{1,0:T(8,128)(2,1)S(1)}, bf16[128,1536]{1,0:T(8,128)(2,1)S(1)}) custom-call(s32[3]{0:T(128)S(1)} %pad_add_fusion.place_ref, bf16[256,1152]{1,0:T(8,128)(2,1)S(1)} %get-tuple-element.107.grads_ref, bf16[384,1152]{1,0:T(8,128)(2,1)S(1)} %pad_maximum_fusion.1.w0, bf16[384,1152]{1,0:T(8,128)(2,1)S(1)} %collective-permute-done.12.w1, ...), custom_call_target="tpu_custom_call" | custom-call | flops 1000 | bytes 1000 | tf_op jit(solution)/shard_map/pallas_call | solution.py:94
  117.8 6.6 %shard_map.92 = (bf16[384,384]{1,0:T(8,128)(2,1)S(1)}, bf16[384,384]{1,0:T(8,128)(2,1)S(1)}, bf16[384,384]{1,0:T(8,128)(2,1)S(1)}, bf16[384,384]{1,0:T(8,128)(2,1)S(1)}) custom-call(s32[3]{0:T(128)S(1)} %pad_add_fusion.place_ref, bf16[256,384]{1,0:T(8,128)(2,1)S(1)} %get-tuple-element.106.mine_ref, bf16[256,384]{1,0:T(8,128)(2,1)S(1)} %collective-permute-done.22.other_ref, ...), custom_call_target="tpu_custom_call" | custom-call | flops 1000 | bytes 1000 | tf_op jit(solution)/shard_map/pallas_call | solution.py:94
  128.3 8.8 %collective-permute-done.23 = bf16[384,384]{1,0:T(8,128)(2,1)S(1)} collective-permute-done((bf16[384,384]{1,0:T(8,128)(2,1)S(1)}, bf16[384,384]{1,0:T(8,128)(2,1)S(1)}, u32[]{:S(2)}, u32[]{:S(2)}) %collective-permute-start.23) | collective-permute-done | bytes 294944 | tf_op jit(solution)/shard_map/ppermute | solution.py:51
  138.2 6.1 %collective-permute-done.25 = bf16[384,384]{1,0:T(8,128)(2,1)S(1)} collective-permute-done((bf16[384,384]{1,0:T(8,128)(2,1)S(1)}, bf16[384,384]{1,0:T(8,128)(2,1)S(1)}, u32[]{:S(2)}, u32[]{:S(2)}) %collective-permute-start.25) | collective-permute-done | bytes 294944 | tf_op jit(solution)/shard_map/ppermute | solution.py:51
  147.8 3.5 %collective-permute-done.26 = bf16[96,1536]{1,0:T(8,128)(2,1)S(1)} collective-permute-done((bf16[96,1536]{1,0:T(8,128)(2,1)S(1)}, bf16[96,1536]{1,0:T(8,128)(2,1)S(1)}, u32[]{:S(2)}, u32[]{:S(2)}) %collective-permute-start.26) | collective-permute-done | bytes 294944 | tf_op jit(solution)/shard_map/ppermute | solution.py:51
  151.3 4.7 %collective-permute-done.28 = bf16[96,1536]{1,0:T(8,128)(2,1)S(1)} collective-permute-done((bf16[96,1536]{1,0:T(8,128)(2,1)S(1)}, bf16[96,1536]{1,0:T(8,128)(2,1)S(1)}, u32[]{:S(2)}, u32[]{:S(2)}) %collective-permute-start.28) | collective-permute-done | bytes 294944 | tf_op jit(solution)/shard_map/ppermute | solution.py:51
  164.7 2.7 %collective-permute-start.34 = (f32[12,1536]{1,0:T(8,128)S(1)}, f32[12,1536]{1,0:T(8,128)S(1)}, u32[]{:S(2)}, u32[]{:S(2)}) collective-permute-start(f32[12,1536]{1,0:T(8,128)S(1)} %get-tuple-element.139), channel_id=1, source_target_pairs={{0,8},{8,0},{1,9},{9,1},{2,10},{10,2},{3,11},{11,3},{4,12},{12,4},... | collective-permute-start | bytes 221192 | tf_op jit(solution)/shard_map/ppermute | solution.py:55
  (131 shorter events, 42.2 us)
Async XLA Ops:
  4.5 11.0 %collective-permute-start.1 = (bf16[144,1664]{1,0:T(8,128)(2,1)S(1)}, bf16[144,1664]{1,0:T(8,128)(2,1)S(1)}, u32[]{:S(2)}, u32[]{:S(2)}) collective-permute-start(bf16[144,1664]{1,0:T(8,128)(2,1)S(1)} %get-tuple-element.67), channel_id=1, source_target_pairs={{8,16},{16,8},{24,32},{32,24},{40,48},{48,40},{56,64},{64,56},{72,... | collective-permute-start | bytes 1437704 | tf_op jit(solution)/shard_map/ppermute | solution.py:60
  16.4 22.4 %collective-permute-start.5 = (bf16[160,1664]{1,0:T(8,128)(2,1)S(1)}, bf16[160,1664]{1,0:T(8,128)(2,1)S(1)}, u32[]{:S(2)}, u32[]{:S(2)}) collective-permute-start(bf16[160,1664]{1,0:T(8,128)(2,1)S(1)} %get-tuple-element.75), channel_id=1, source_target_pairs={{0,1},{1,2},{2,3},{3,4},{4,5},{5,6},{6,7},{8,9},{9,10},{10,11},{11... | collective-permute-start | bytes 1597448 | tf_op jit(solution)/shard_map/ppermute | solution.py:65
  19.6 19.2 %collective-permute-start.6 = (bf16[160,1664]{1,0:T(8,128)(2,1)S(1)}, bf16[160,1664]{1,0:T(8,128)(2,1)S(1)}, u32[]{:S(2)}, u32[]{:S(2)}) collective-permute-start(bf16[160,1664]{1,0:T(8,128)(2,1)S(1)} %get-tuple-element.76), channel_id=1, source_target_pairs={{1,0},{2,1},{3,2},{4,3},{5,4},{6,5},{7,6},{9,8},{10,9},{11,10},{12... | collective-permute-start | bytes 1597448 | tf_op jit(solution)/shard_map/ppermute | solution.py:65
  20.9 9.2 %collective-permute-start.4 = (bf16[24,1536]{1,0:T(8,128)(2,1)S(1)}, bf16[24,1536]{1,0:T(8,128)(2,1)S(1)}, u32[]{:S(2)}, u32[]{:S(2)}) collective-permute-start(bf16[24,1536]{1,0:T(8,128)(2,1)S(1)} %pad_maximum_fusion.4), channel_id=1, source_target_pairs={{0,48},{8,76},{4,52},{12,8},{64,112},{72,12},{68,116},{76,72},{16,... | collective-permute-start | bytes 221192 | tf_op jit(solution)/shard_map/ppermute | solution.py:51
  27.9 10.9 %collective-permute-start.3 = (bf16[24,1536]{1,0:T(8,128)(2,1)S(1)}, bf16[24,1536]{1,0:T(8,128)(2,1)S(1)}, u32[]{:S(2)}, u32[]{:S(2)}) collective-permute-start(bf16[24,1536]{1,0:T(8,128)(2,1)S(1)} %pad_maximum_fusion.4), channel_id=1, source_target_pairs={{0,32},{8,72},{4,36},{12,76},{64,96},{72,8},{68,100},{76,12},{16,4... | collective-permute-start | bytes 221192 | tf_op jit(solution)/shard_map/ppermute | solution.py:51
  27.9 10.9 %collective-permute-start.2 = (bf16[24,1536]{1,0:T(8,128)(2,1)S(1)}, bf16[24,1536]{1,0:T(8,128)(2,1)S(1)}, u32[]{:S(2)}, u32[]{:S(2)}) collective-permute-start(bf16[24,1536]{1,0:T(8,128)(2,1)S(1)} %pad_maximum_fusion.4), channel_id=1, source_target_pairs={{0,16},{8,12},{4,20},{12,72},{64,80},{72,76},{68,84},{76,8},{16,32... | collective-permute-start | bytes 221192 | tf_op jit(solution)/shard_map/ppermute | solution.py:51
  39.6 11.3 %collective-permute-start.10 = (bf16[448,1664]{1,0:T(8,128)(2,1)S(1)}, bf16[448,1664]{1,0:T(8,128)(2,1)S(1)}, u32[]{:S(2)}, u32[]{:S(2)}) collective-permute-start(bf16[448,1664]{1,0:T(8,128)(2,1)S(1)} %get-tuple-element.87.tokens_ref.amine_ref), channel_id=1, source_target_pairs={{0,8},{8,0},{1,9},{9,1},{2,10},{10,2},{3,11},{11,3},{4,12},{12,4},... | collective-permute-start | bytes 4472840 | tf_op jit(solution)/shard_map/ppermute | solution.py:55
  39.7 11.2 %collective-permute-start.11 = (bf16[288,1664]{1,0:T(8,128)(2,1)S(1)}, bf16[288,1664]{1,0:T(8,128)(2,1)S(1)}, u32[]{:S(2)}, u32[]{:S(2)}) collective-permute-start(bf16[288,1664]{1,0:T(8,128)(2,1)S(1)} %get-tuple-element.90.gmine_ref), channel_id=1, source_target_pairs={{0,8},{8,0},{1,9},{9,1},{2,10},{10,2},{3,11},{11,3},{4,12},{12,4},... | collective-permute-start | bytes 2875400 | tf_op jit(solution)/shard_map/ppermute | solution.py:55
  40.4 10.5 %collective-permute-start.7 = (bf16[96,1536]{1,0:T(8,128)(2,1)S(1)}, bf16[96,1536]{1,0:T(8,128)(2,1)S(1)}, u32[]{:S(2)}, u32[]{:S(2)}) collective-permute-start(bf16[96,1536]{1,0:T(8,128)(2,1)S(1)} %pad_maximum_fusion.2), channel_id=1, source_target_pairs={{0,4},{8,9},{4,64},{12,13},{64,68},{72,73},{68,0},{76,77},{16,20},... | collective-permute-start | bytes 884744 | tf_op jit(solution)/shard_map/ppermute | solution.py:51
  51.2 12.4 %collective-permute-start.17 = (bf16[384,384]{1,0:T(8,128)(2,1)S(1)}, bf16[384,384]{1,0:T(8,128)(2,1)S(1)}, u32[]{:S(2)}, u32[]{:S(2)}) collective-permute-start(bf16[384,384]{1,0:T(8,128)(2,1)S(1)} %pad_maximum_fusion.3.r0), channel_id=1, source_target_pairs={{0,3},{8,56},{4,7},{12,60},{64,67},{72,120},{68,71},{76,124},{16,1... | collective-permute-start | bytes 884744 | tf_op jit(solution)/shard_map/ppermute | solution.py:51
  56.7 10.2 %collective-permute-start.15 = (bf16[384,384]{1,0:T(8,128)(2,1)S(1)}, bf16[384,384]{1,0:T(8,128)(2,1)S(1)}, u32[]{:S(2)}, u32[]{:S(2)}) collective-permute-start(bf16[384,384]{1,0:T(8,128)(2,1)S(1)} %pad_maximum_fusion.3.r0), channel_id=1, source_target_pairs={{0,1},{8,24},{4,5},{12,28},{64,65},{72,88},{68,69},{76,92},{16,17}... | collective-permute-start | bytes 884744 | tf_op jit(solution)/shard_map/ppermute | solution.py:51
  57.4 25.1 %collective-permute-start.14 = (bf16[384,1152]{1,0:T(8,128)(2,1)S(1)}, bf16[384,1152]{1,0:T(8,128)(2,1)S(1)}, u32[]{:S(2)}, u32[]{:S(2)}) collective-permute-start(bf16[384,1152]{1,0:T(8,128)(2,1)S(1)} %pad_maximum_fusion.1.w0), channel_id=1, source_target_pairs={{0,3},{8,56},{4,7},{12,60},{64,67},{72,120},{68,71},{76,124},{16,1... | collective-permute-start | bytes 2654216 | tf_op jit(solution)/shard_map/ppermute | solution.py:51
  59.4 23.1 %collective-permute-start.13 = (bf16[384,1152]{1,0:T(8,128)(2,1)S(1)}, bf16[384,1152]{1,0:T(8,128)(2,1)S(1)}, u32[]{:S(2)}, u32[]{:S(2)}) collective-permute-start(bf16[384,1152]{1,0:T(8,128)(2,1)S(1)} %pad_maximum_fusion.1.w0), channel_id=1, source_target_pairs={{0,2},{8,40},{4,6},{12,44},{64,66},{72,104},{68,70},{76,108},{16,1... | collective-permute-start | bytes 2654216 | tf_op jit(solution)/shard_map/ppermute | solution.py:51
  63.5 22.4 %collective-permute-start.12 = (bf16[384,1152]{1,0:T(8,128)(2,1)S(1)}, bf16[384,1152]{1,0:T(8,128)(2,1)S(1)}, u32[]{:S(2)}, u32[]{:S(2)}) collective-permute-start(bf16[384,1152]{1,0:T(8,128)(2,1)S(1)} %pad_maximum_fusion.1.w0), channel_id=1, source_target_pairs={{0,1},{8,24},{4,5},{12,28},{64,65},{72,88},{68,69},{76,92},{16,17}... | collective-permute-start | bytes 2654216 | tf_op jit(solution)/shard_map/ppermute | solution.py:51
  105.1 12.7 %collective-permute-start.22 = (bf16[256,384]{1,0:T(8,128)(2,1)S(1)}, bf16[256,384]{1,0:T(8,128)(2,1)S(1)}, u32[]{:S(2)}, u32[]{:S(2)}) collective-permute-start(bf16[256,384]{1,0:T(8,128)(2,1)S(1)} %get-tuple-element.106.mine_ref), channel_id=1, source_target_pairs={{0,8},{8,0},{1,9},{9,1},{2,10},{10,2},{3,11},{11,3},{4,12},{12,4},... | collective-permute-start | bytes 589832 | tf_op jit(solution)/shard_map/ppermute | solution.py:55
  105.5 38.9 %collective-permute-start.19 = (bf16[384,1152]{1,0:T(8,128)(2,1)S(1)}, bf16[384,1152]{1,0:T(8,128)(2,1)S(1)}, u32[]{:S(2)}, u32[]{:S(2)}) collective-permute-start(bf16[384,1152]{1,0:T(8,128)(2,1)S(1)} %get-tuple-element.103), channel_id=1, source_target_pairs={{0,3},{8,56},{4,7},{12,60},{64,67},{72,120},{68,71},{76,124},{16,1... | collective-permute-start | bytes 2654216 | tf_op jit(solution)/shard_map/ppermute | solution.py:51
  111.3 33.2 %collective-permute-start.20 = (bf16[384,1152]{1,0:T(8,128)(2,1)S(1)}, bf16[384,1152]{1,0:T(8,128)(2,1)S(1)}, u32[]{:S(2)}, u32[]{:S(2)}) collective-permute-start(bf16[384,1152]{1,0:T(8,128)(2,1)S(1)} %get-tuple-element.104), channel_id=1, source_target_pairs={{0,2},{8,40},{4,6},{12,44},{64,66},{72,104},{68,70},{76,108},{16,1... | collective-permute-start | bytes 2654216 | tf_op jit(solution)/shard_map/ppermute | solution.py:51
  111.3 33.2 %collective-permute-start.21 = (bf16[384,1152]{1,0:T(8,128)(2,1)S(1)}, bf16[384,1152]{1,0:T(8,128)(2,1)S(1)}, u32[]{:S(2)}, u32[]{:S(2)}) collective-permute-start(bf16[384,1152]{1,0:T(8,128)(2,1)S(1)} %get-tuple-element.105), channel_id=1, source_target_pairs={{0,1},{8,24},{4,5},{12,28},{64,65},{72,88},{68,69},{76,92},{16,17}... | collective-permute-start | bytes 2654216 | tf_op jit(solution)/shard_map/ppermute | solution.py:51
  124.4 12.7 %collective-permute-start.23 = (bf16[384,384]{1,0:T(8,128)(2,1)S(1)}, bf16[384,384]{1,0:T(8,128)(2,1)S(1)}, u32[]{:S(2)}, u32[]{:S(2)}) collective-permute-start(bf16[384,384]{1,0:T(8,128)(2,1)S(1)} %get-tuple-element.113), channel_id=1, source_target_pairs={{0,3},{8,56},{4,7},{12,60},{64,67},{72,120},{68,71},{76,124},{16,1... | collective-permute-start | bytes 884744 | tf_op jit(solution)/shard_map/ppermute | solution.py:51
  126.5 11.7 %collective-permute-start.24 = (bf16[384,384]{1,0:T(8,128)(2,1)S(1)}, bf16[384,384]{1,0:T(8,128)(2,1)S(1)}, u32[]{:S(2)}, u32[]{:S(2)}) collective-permute-start(bf16[384,384]{1,0:T(8,128)(2,1)S(1)} %get-tuple-element.114), channel_id=1, source_target_pairs={{0,2},{8,40},{4,6},{12,44},{64,66},{72,104},{68,70},{76,108},{16,1... | collective-permute-start | bytes 884744 | tf_op jit(solution)/shard_map/ppermute | solution.py:51
  146.0 9.9 %collective-permute-start.28 = (bf16[96,1536]{1,0:T(8,128)(2,1)S(1)}, bf16[96,1536]{1,0:T(8,128)(2,1)S(1)}, u32[]{:S(2)}, u32[]{:S(2)}) collective-permute-start(bf16[96,1536]{1,0:T(8,128)(2,1)S(1)} %get-tuple-element.133), channel_id=1, source_target_pairs={{0,4},{8,9},{4,64},{12,13},{64,68},{72,73},{68,0},{76,77},{16,20},... | collective-permute-start | bytes 884744 | tf_op jit(solution)/shard_map/ppermute | solution.py:51
  146.9 9.1 %collective-permute-start.27 = (bf16[96,1536]{1,0:T(8,128)(2,1)S(1)}, bf16[96,1536]{1,0:T(8,128)(2,1)S(1)}, u32[]{:S(2)}, u32[]{:S(2)}) collective-permute-start(bf16[96,1536]{1,0:T(8,128)(2,1)S(1)} %get-tuple-element.134), channel_id=1, source_target_pairs={{0,64},{8,10},{4,68},{12,14},{64,0},{72,74},{68,4},{76,78},{16,80}... | collective-permute-start | bytes 884744 | tf_op jit(solution)/shard_map/ppermute | solution.py:51
  147.3 8.8 %collective-permute-start.29 = (f32[128,768]{1,0:T(8,128)S(1)}, f32[128,768]{1,0:T(8,128)S(1)}, u32[]{:S(2)}, u32[]{:S(2)}) collective-permute-start(f32[128,768]{1,0:T(8,128)S(1)} %get-tuple-element.122), channel_id=1, source_target_pairs={{0,8},{8,0},{1,9},{9,1},{2,10},{10,2},{3,11},{11,3},{4,12},{12,4},... | collective-permute-start | bytes 1179656 | tf_op jit(solution)/shard_map/ppermute | solution.py:55
  147.3 8.8 %collective-permute-start.30 = (bf16[128,1536]{1,0:T(8,128)(2,1)S(1)}, bf16[128,1536]{1,0:T(8,128)(2,1)S(1)}, u32[]{:S(2)}, u32[]{:S(2)}) collective-permute-start(bf16[128,1536]{1,0:T(8,128)(2,1)S(1)} %get-tuple-element.124), channel_id=1, source_target_pairs={{0,8},{8,0},{1,9},{9,1},{2,10},{10,2},{3,11},{11,3},{4,12},{12,4},... | collective-permute-start | bytes 1179656 | tf_op jit(solution)/shard_map/ppermute | solution.py:55
  (15 other events, 83.5 us)
where the time goes:
time: 170 us
  waiting for transfers between devices  63.6 us (37%)
  Pallas kernels  49.2 us (29%)
  starting transfers between devices  47.6 us (28%)
  local copies, waits for them, and re-layouts  5.39 us (3%)
  other arithmetic  2.84 us (2%)
    ppermute x24, waiting for transfers between devices, shifted(): return lax.ppermute(value, AXES, stage_pairs(axes, shift))  58.9 us
    pallas_call x11, Pallas kernels, on_chip(): pl.pallas_call(kernel, out_shape=tuple((jax.ShapeDtypeStruct(shape, kind)...  49.2 us
    ppermute x24, starting transfers between devices, shifted(): return lax.ppermute(value, AXES, stage_pairs(axes, shift))  33.5 us
    ppermute x8, starting transfers between devices, swap_cores(): return lax.ppermute(value, 'c', [(0, 1), (1, 0)])  4.99 us
    ppermute x1, starting transfers between devices, row_neighbour(): lax.ppermute(value, ('zh', 'y', 'c'), [(a, b) for a, b in pairs if 0 <= b...  4.59 us
    ppermute x2, starting transfers between devices, col_neighbour(): lax.ppermute(value, ('zl', 'x'), [(a, b) for a, b in pairs if 0 <= b < 8])  4.44 us
  transfers between devices with their start and end apart: 35, of which 20 were waited for; matrix products, arithmetic and copies ran while one was open for 2% of the time, Pallas kernels for 15%

commit v1 on v0

--- a/solution.py
+++ b/solution.py
@@ -20,7 +20,7 @@
 WIDE = D + LANE
 
 AXES = ("zh", "y", "c", "zl", "x")
-STAGES = (("y", "z", "x"), ("z", "x", "y"))
+STAGES = (("z", "y", "x"), ("x", "z", "y"))
 
 epsilon = 1e-05
 masked_score = -1e30
@@ -71,6 +71,16 @@
     near = shifted(block, axes, 1)
     back = shifted(block, axes, 3)
     return [block, near, far, back]
+
+
+def gather_ring(block):
+    axes = (STAGES[0][2], STAGES[1][2])
+    return shifted(block, axes, 1), shifted(block, axes, 3)
+
+
+def relay_ring(near, back):
+    axes = (STAGES[0][2], STAGES[1][2])
+    return shifted(near[:192], axes, 1), shifted(back[192:], axes, 3)
 
 
 def scatter_stage(chunks, stage):
@@ -188,53 +198,92 @@
     lax.fori_loop(0, D // 256, part, 0)
 
 
-def out_rows_kernel(place_ref, r0, r1, r2, r3, row_ref, half_out, sent_out):
-    core = place_ref[1]
-
+def out_rows_product(row_ref, part, h, first, chunk):
+    row = lax.broadcasted_iota(jnp.int32, (128, D // 4), 0) + (first + h * DH)
+    order = one_hot(row == row_ref[:, part * 384 : (part + 1) * 384])
+    return jnp.dot(order, chunk, preferred_element_type=f32)
+
+
+def near_rows_kernel(place_ref, r0, r1, r3, row_ref, sums_out):
     def part(n, carry):
         first = pl.multiple_of(n * 128, 128)
         for h in range(2):
-            row = lax.broadcasted_iota(jnp.int32, (128, D // 4), 0) + (first + h * DH)
-            total = jnp.zeros((128, HALF), f32)
-            for k, ref in enumerate((r0, r1, r2, r3)):
-                order = one_hot(row == row_ref[:, k * 384 : (k + 1) * 384])
-                total += jnp.dot(order, ref[...], preferred_element_type=f32)
-            half_out[pl.ds(first, 128), h * HALF : (h + 1) * HALF] = total.astype(bf16)
+            total = out_rows_product(row_ref, 0, h, first, r0[:, 3 * HALF :])
+            total += out_rows_product(row_ref, 1, h, first, r1[:, 3 * HALF :])
+            total += out_rows_product(row_ref, 3, h, first, r3[:, 3 * HALF :])
+            sums_out[pl.ds(first, 128), h * HALF : (h + 1) * HALF] = total
+        return carry
+
+    lax.fori_loop(0, DH // 128, part, 0)
+
+
+def out_rows_kernel(place_ref, sums_ref, r2_top, r2_low, row_ref, half_out, sent_out):
+    core = place_ref[1]
+    far = jnp.concatenate([r2_top[:, 3 * HALF :], r2_low[:, 3 * HALF :]], axis=0)
+
+    def part(n, carry):
+        first = pl.multiple_of(n * 128, 128)
+        for h in range(2):
+            lanes = slice(h * HALF, (h + 1) * HALF)
+            total = sums_ref[pl.ds(first, 128), lanes] + out_rows_product(row_ref, 2, h, first, far)
+            half_out[pl.ds(first, 128), lanes] = total.astype(bf16)
         return carry
 
     lax.fori_loop(0, DH // 128, part, 0)
     sent_out[...] = half_out[pl.ds(pl.multiple_of((1 - core) * HALF, HALF), HALF), :]
 
 
-def out_grads_kernel(place_ref, mine_ref, other_ref, grad_ref, row_ref, c0, c1, c2, c3, grads):
+def packed_kernel(place_ref, mine_ref, other_ref, w0, w1, w2_top, w2_low, w3, packed, hidden, w2):
+    core = place_ref[1]
+    half = KEY_ROWS // 2 * KEY_COLS
+    part = D // 4
+    w2[:192, :] = w2_top[:, : 3 * HALF]
+    w2[192:, :] = w2_low[:, : 3 * HALF]
+    for source, side in ((mine_ref, core), (other_ref, 1 - core)):
+        own_at = pl.multiple_of((1 - side) * 6 * KEY_COLS, KEY_COLS)
+        for r in range(8):
+            to = pl.ds(pl.multiple_of((side * 8 + r) * SIDE, SIDE), SIDE)
+            hidden[to, :] = source[pl.ds(own_at + r * KEY_COLS, SIDE), :]
+
+        def project(t, carry, source=source, side=side):
+            rows = pl.ds(pl.multiple_of(t * 112, 112), 112)
+            to = pl.ds(pl.multiple_of(side * half + t * 112, 112), 112)
+            total = jnp.dot(source[rows, :part], w0[:, : 3 * HALF], preferred_element_type=f32)
+            for k, ref in ((1, w1), (2, w2), (3, w3)):
+                total += jnp.dot(
+                    source[rows, k * part : (k + 1) * part], ref[:, : 3 * HALF], preferred_element_type=f32
+                )
+            packed[to, :] = total.astype(bf16)
+            return carry
+
+        lax.fori_loop(0, 4, project, 0)
+
+
+def out_grads_kernel(place_ref, mine_ref, other_ref, grad_ref, row_ref, c0, c1, c2, c3):
     core = place_ref[1]
     over = (((0,), (0,)), ((), ()))
-    for attn, side in ((mine_ref, core), (other_ref, 1 - core)):
-        for h in range(2):
-            to = pl.ds(pl.multiple_of(h * DH + side * HALF, HALF), HALF)
-            grads[to, :] = lax.dot_general(
-                attn[...], grad_ref[:, h * HALF : (h + 1) * HALF], over, preferred_element_type=f32
-            ).astype(bf16)
-    lane = lax.broadcasted_iota(jnp.int32, (LANE, LANE), 1).astype(f32)
+    part = D // 4
+    inner = lax.broadcasted_iota(jnp.int32, (part, HALF), 0) % 24
     for k, chunk in enumerate((c0, c1, c2, c3)):
-
-        def part(n, carry, k=k, chunk=chunk):
-            first = pl.multiple_of(n * LANE, LANE)
-            row = row_ref[:, pl.ds(k * 384 + first, LANE)].astype(f32)
-            row = jnp.transpose(jnp.broadcast_to(row, (LANE, LANE)))
-            order = jnp.concatenate([one_hot(lane + m * LANE == row) for m in range(2 * DH // LANE)], axis=1)
-            chunk[pl.ds(first, LANE), :] = jnp.dot(order, grads[...], preferred_element_type=f32).astype(bf16)
-            return carry
-
-        lax.fori_loop(0, 3, part, 0)
-
-
-def grad_hidden_kernel(place_ref, grads_ref, w0, w1, w2, w3, feature_ref, mine_out, sent_out, rel):
+        row = row_ref[:, k * part : (k + 1) * part]
+        row = jnp.where(row < DH, row, row - DH)
+        picked = jnp.zeros((2 * LANE, part), f32)
+        for attn, side in ((mine_ref, core), (other_ref, 1 - core)):
+            order = one_hot(lax.broadcasted_iota(jnp.int32, (HALF, part), 0) + side * HALF == row)
+            picked += jnp.dot(attn[...], order, preferred_element_type=f32)
+        picked = picked.astype(bf16)
+        first = lax.dot_general(picked, grad_ref[:, :HALF], over, preferred_element_type=f32)
+        second = lax.dot_general(picked, grad_ref[:, HALF:], over, preferred_element_type=f32)
+        chunk[...] = jnp.where(inner < 12, first, second).astype(bf16)
+
+
+def grad_hidden_kernel(place_ref, grads_ref, w0, w1, w2_top, w2_low, w3, feature_ref, mine_out, sent_out, rel):
     core = place_ref[1]
     contract = (((1,), (1,)), ((), ()))
-    for k, ref in enumerate((w0, w1, w2, w3)):
+    far = jnp.concatenate([w2_top[:, : 3 * HALF], w2_low[:, : 3 * HALF]], axis=0)
+    for k, chunk in enumerate((w0[:, : 3 * HALF], w1[:, : 3 * HALF], far, w3[:, : 3 * HALF])):
         rel[:, k * 384 : (k + 1) * 384] = lax.dot_general(
-            grads_ref[...], ref[...], contract, preferred_element_type=f32
+            grads_ref[...], chunk, contract, preferred_element_type=f32
         ).astype(bf16)
 
     def part(n, carry):
@@ -290,9 +339,9 @@
 
 
 def layer_kernel(
-    place_ref, mine_ref, other_ref, w0, w1, w2, w3, amine_ref, aother_ref, gmine_ref, gother_ref, rmine_ref, rother_ref,
+    place_ref, packed, hidden, amine_ref, aother_ref, gmine_ref, gother_ref, rmine_ref, rother_ref,
     attn_out, grads_out, c0, c1, c2, c3, grad_own,
-    packed, hidden, grad_attn, dk, dv, attn, dq, tissue, lines_f32,
+    grad_attn, dk, dv, attn, dq, tissue, lines_f32,
 ):
     base, core, column = place_ref[0], place_ref[1], place_ref[2]
     width = 2 * QUERY_COLS
@@ -301,30 +350,10 @@
     half_q = QUERY_ROWS // 2 * QUERY_COLS
     contract = (((1,), (1,)), ((), ()))
     over = (((0,), (0,)), ((), ()))
-    chunks = (w0, w1, w2, w3)
     part = D // 4
 
     dk[...] = jnp.zeros_like(dk)
     dv[...] = jnp.zeros_like(dv)
-
-    for source, side in ((mine_ref, core), (other_ref, 1 - core)):
-        own_at = pl.multiple_of((1 - side) * 6 * KEY_COLS, KEY_COLS)
-        for r in range(8):
-            to = pl.ds(pl.multiple_of((side * 8 + r) * SIDE, SIDE), SIDE)
-            hidden[to, :] = source[pl.ds(own_at + r * KEY_COLS, SIDE), :]
-
-        def project(t, carry, source=source, side=side):
-            rows = pl.ds(pl.multiple_of(t * 112, 112), 112)
-            to = pl.ds(pl.multiple_of(side * half + t * 112, 112), 112)
-            total = jnp.dot(source[rows, :part], w0[...], preferred_element_type=f32)
-            for k in range(1, 4):
-                total += jnp.dot(
-                    source[rows, k * part : (k + 1) * part], chunks[k][...], preferred_element_type=f32
-                )
-            packed[to, :] = total.astype(bf16)
-            return carry
-
-        lax.fori_loop(0, 4, project, 0)
 
     mine_lanes = pl.ds(pl.multiple_of(core * DH, DH), DH)
     other_lanes = pl.ds(pl.multiple_of((1 - core) * DH, DH), DH)
@@ -435,8 +464,6 @@
         arrays,
         [((SIDE * SIDE, HALF), bf16), ((SIDE * SIDE, 3 * HALF), bf16)] + [((D // 4, 3 * HALF), bf16)] * 4 + [((SIDE * SIDE, DH), bf16)],
         [
-            ((keys, 3 * HALF), bf16),
-            ((SIDE * SIDE, D), bf16),
             ((queries, HALF), f32),
             ((keys, HALF), f32),
             ((keys, HALF), f32),
@@ -484,6 +511,9 @@
     shard_first, shard_second = shard(first, project_out[:, :DH]), shard(second, project_out[:, DH:])
     mine = jnp.where(core == 0, shard_first, shard_second)
     theirs = jnp.where(core == 0, shard_second, shard_first)
+    other = swap_cores(theirs)
+    here = {"x": x, "y": y, "z": z}
+    feature_line, row_line = orders(core, here, lax.broadcasted_iota(jnp.int32, (1, D), 1))
     flat_tiles, flat_grad = tiles.reshape(tokens, D), grad_layer.reshape(tokens, D)
     live = jnp.broadcast_to(tissue.reshape(tokens, 1).astype(f32), (tokens, LANE))
     own_hidden, own_grad, sent = on_chip(
@@ -492,15 +522,16 @@
         [flat_tiles, flat_grad, live],
         [((tokens, WIDE), bf16), ((tokens, WIDE), bf16), ((144, WIDE), bf16)],
     )
-    here = {"x": x, "y": y, "z": z}
-    feature_line, row_line = orders(core, here, lax.broadcasted_iota(jnp.int32, (1, D), 1))
-
-    other, got = swap_cores(theirs), row_neighbour(sent)
-    other, got, feature_line, row_line = lax.optimization_barrier((other, got, feature_line, row_line))
     block_in = by_core(core, mine[:, : 3 * HALF], other[:, : 3 * HALF], 0)
     mine_out, other_out = mine[:, 3 * HALF :].reshape(2, 6, HALF), other[:, 3 * HALF :].reshape(2, 6, HALF)
     block_out = by_core(core, mine_out, other_out, 1).reshape(24, HALF)
     block = jnp.concatenate([block_in, block_out], axis=1)
+    block, sent, feature_line, row_line = lax.optimization_barrier((block, sent, feature_line, row_line))
+
+    parts = gather_stage(block, 0)
+    got = row_neighbour(sent)
+    *parts, got = lax.optimization_barrier((*parts, got))
+    block = jnp.concatenate(parts, axis=0)
     a, b, to_right, to_left = on_chip(
         columns_kernel,
         place,
@@ -509,36 +540,43 @@
     )
     block, to_right, to_left = lax.optimization_barrier((block, to_right, to_left))
 
-    parts = gather_stage(block, 0)
+    parts = gather_stage(block, 1)
     left, right = col_neighbour(to_right, 1), col_neighbour(to_left, -1)
-    *parts, left, right = lax.optimization_barrier((*parts, left, right))
+    block = lax.optimization_barrier(jnp.concatenate(parts, axis=0))
+
+    near, back = gather_ring(block)
     wide_a, wide_b = on_chip(
         widen_kernel, place, [a, b, left, right], [((14 * KEY_COLS, WIDE), bf16), ((12 * QUERY_COLS, WIDE), bf16)]
     )
-    block, wide_a, wide_b = lax.optimization_barrier((jnp.concatenate(parts, axis=0), wide_a, wide_b))
-
-    parts = gather_stage(block, 1)
     other_a, other_b = swap_cores(wide_a), swap_cores(wide_b)
-    *parts, other_a, other_b = lax.optimization_barrier((*parts, other_a, other_b))
-    block_out = jnp.concatenate([part[:, 3 * HALF :] for part in parts], axis=0)
-    block_in = jnp.concatenate([part[:, : 3 * HALF] for part in parts], axis=0)
-    block_out, block_in = lax.optimization_barrier((block_out, block_in))
-
-    rows_out = gather_stage(block_out, 2)
-    weights = gather_stage(block_in, 2)
     permuted = [((14 * KEY_COLS, D), bf16)]
     (hidden_mine,) = on_chip(permute_kernel, place, [wide_a, feature_line], permuted)
     (hidden_other,) = on_chip(permute_kernel, place, [other_a, feature_line], permuted)
 
+    hidden_mine, near, back = lax.optimization_barrier((hidden_mine, near, back))
+    weights = [block, near, *relay_ring(near, back), back]
+    hidden_other, row_line = lax.optimization_barrier((hidden_other, row_line))
+    (near_rows,) = on_chip(near_rows_kernel, place, [block, near, back, row_line], [((DH, DH), f32)])
     half_out, sent_rows = on_chip(
-        out_rows_kernel, place, rows_out + [row_line], [((DH, DH), bf16), ((HALF, DH), bf16)]
+        out_rows_kernel,
+        place,
+        [near_rows, weights[2], weights[3], row_line],
+        [((DH, DH), bf16), ((HALF, DH), bf16)],
     )
     other_rows = swap_cores(sent_rows)
+    packed, hidden = on_chip(
+        packed_kernel,
+        place,
+        [hidden_mine, hidden_other, *weights],
+        [((KEY_ROWS * KEY_COLS, 3 * HALF), bf16), ((SIDE * SIDE, D), bf16)],
+        [((D // 4, 3 * HALF), bf16)],
+    )
 
     attention, grad_packed, *chunks_in, grad_own = layer(
-        place, hidden_mine, hidden_other, *weights, wide_a, other_a, wide_b, other_b, half_out, other_rows
-    )
-    total_in = scatter_stage(chunks_in, 2)
+        place, packed, hidden, wide_a, other_a, wide_b, other_b, half_out, other_rows
+    )
+    axes = (STAGES[0][2], STAGES[1][2])
+    far, near, back = shifted(chunks_in[2], axes, 2), shifted(chunks_in[1], axes, 3), shifted(chunks_in[3], axes, 1)
 
     attention_other = swap_cores(attention)
     hidden_kept, hidden_sent = on_chip(
@@ -554,12 +592,16 @@
         place,
         [attention, attention_other, grad_own, row_line],
         [((D // 4, HALF), bf16)] * 4,
-        [((2 * DH, HALF), bf16)],
     )
     projected, projected_sent = on_chip(
         project_kernel, place, [attention, attention_other, half_out], [((tokens, DH), f32)] * 2
     )
-    total = jnp.concatenate([total_in, scatter_stage(chunks_out, 2)], axis=1).astype(bf16)
+    far_out, near_out = shifted(chunks_out[2], axes, 2), shifted(chunks_out[1], axes, 3)
+    total_in, back_out = lax.optimization_barrier((chunks_in[0].astype(f32) + near.astype(f32), chunks_out[3]))
+    back_out = shifted(back_out, axes, 1)
+    total_in = total_in + (far.astype(f32) + back.astype(f32))
+    total_out = (chunks_out[0].astype(f32) + near_out.astype(f32)) + (far_out.astype(f32) + back_out.astype(f32))
+    total = jnp.concatenate([total_in, total_out], axis=1).astype(bf16)
     total, hidden_kept, hidden_sent, projected, projected_sent = lax.optimization_barrier(
         (total, hidden_kept, hidden_sent, projected, projected_sent)
     )
@@ -570,7 +612,6 @@
         [flat_tiles, flat_grad, live, projected, swap_cores(projected_sent), hidden_kept, swap_cores(hidden_sent)],
         [((tokens, D), bf16)] * 2,
     )
-    total, layer_out, grad_tiles = lax.optimization_barrier((total, layer_out, grad_tiles))
     total = scatter_stage([total[k * 24 : (k + 1) * 24] for k in range(4)], 0)
 
     sums_in = total[:, : 3 * HALF].reshape(2, 12, 3 * HALF)
@@ -578,6 +619,7 @@
     sums = jnp.concatenate([sums_in, sums_out], axis=2)
     kept = jnp.where(core == 0, sums[0], sums[1])
     gotten = swap_cores(jnp.where(core == 0, sums[1], sums[0]))
+    gotten, layer_out, grad_tiles = lax.optimization_barrier((gotten, layer_out, grad_tiles))
     grad_project_in = by_core(
         core, kept[:, : 3 * HALF].reshape(12, 3, 1, HALF), gotten[:, : 3 * HALF].reshape(12, 3, 1, HALF), 2
     ).reshape(12, 3 * DH)

time: 170 us -> 156 us (0.918)
  waiting for transfers between devices: 63.6 us -> 41.3 us
  starting transfers between devices: 47.6 us -> 56.1 us
    ppermute x24 -> x22, waiting for transfers between devices: 58.9 us -> 41.3 us  [shifted(): return lax.ppermute(value, AXES, stage_pairs(axes, shift))]
    ppermute x24 -> x22, starting transfers between devices: 33.5 us -> 41.7 us  [shifted(): return lax.ppermute(value, AXES, stage_pairs(axes, shift))]
    ppermute x8, starting transfers between devices: 4.99 us -> 7.92 us  [swap_cores(): return lax.ppermute(value, 'c', [(0, 1), (1, 0)])]
    ppermute x1, waiting for transfers between devices: 2.93 us -> 0.01 us  [row_neighbour(): lax.ppermute(value, ('zh', 'y', 'c'), [(a, b) for a, b in pairs if 0 <= b...]
    ppermute x8, waiting for transfers between devices: 1.75 us -> 0.02 us  [swap_cores(): return lax.ppermute(value, 'c', [(0, 1), (1, 0)])]
    pallas_call x11 -> x13, Pallas kernels: 49.2 us -> 48 us  [on_chip(): pl.pallas_call(kernel, out_shape=tuple((jax.ShapeDtypeStruct(shape, kind)...]
  transfers between devices with their start and end apart: 35 -> 33, of which waited for: 20 -> 17; matrix products, arithmetic and copies ran while one was open for 2% -> 2% of each run, Pallas kernels for 15% -> 22%
where the time goes in v1:
time: 156 us
  starting transfers between devices  56.1 us (36%)
  Pallas kernels  48 us (31%)
  waiting for transfers between devices  41.3 us (26%)
  local copies, waits for them, and re-layouts  5.35 us (3%)
  other arithmetic  3.53 us (2%)
    pallas_call x13, Pallas kernels, on_chip(): pl.pallas_call(kernel, out_shape=tuple((jax.ShapeDtypeStruct(shape, kind)...  48 us
    ppermute x22, starting transfers between devices, shifted(): return lax.ppermute(value, AXES, stage_pairs(axes, shift))  41.7 us
    ppermute x22, waiting for transfers between devices, shifted(): return lax.ppermute(value, AXES, stage_pairs(axes, shift))  41.3 us
    ppermute x8, starting transfers between devices, swap_cores(): return lax.ppermute(value, 'c', [(0, 1), (1, 0)])  7.92 us
    ppermute x2, starting transfers between devices, col_neighbour(): lax.ppermute(value, ('zl', 'x'), [(a, b) for a, b in pairs if 0 <= b < 8])  3.27 us
    ppermute x1, starting transfers between devices, row_neighbour(): lax.ppermute(value, ('zh', 'y', 'c'), [(a, b) for a, b in pairs if 0 <= b...  3.2 us
  transfers between devices with their start and end apart: 33, of which 17 were waited for; matrix products, arithmetic and copies ran while one was open for 2% of the time, Pallas kernels for 22%

profile of v1, /device:TPU:1, one launch (start us, length us, event | category | flops | bytes accessed | tf_op | source)
XLA Modules:
  0.0 155.6 jit_solution(13275576203394683695)
XLA Ops:
  8.6 3.2 %collective-permute-start.4 = (bf16[144,1664]{1,0:T(8,128)(2,1)S(1)}, bf16[144,1664]{1,0:T(8,128)(2,1)S(1)}, u32[]{:S(2)}, u32[]{:S(2)}) collective-permute-start(bf16[144,1664]{1,0:T(8,128)(2,1)S(1)} %get-tuple-element.68), channel_id=1, source_target_pairs={{8,16},{16,8},{24,32},{32,24},{40,48},{48,40},{56,64},{64,56},{72,... | collective-permute-start | bytes 1437704 | tf_op jit(solution)/shard_map/ppermute | solution.py:60
  11.9 2.5 %collective-permute-start.3 = (bf16[24,1536]{1,0:T(8,128)(2,1)S(1)}, bf16[24,1536]{1,0:T(8,128)(2,1)S(1)}, u32[]{:S(2)}, u32[]{:S(2)}) collective-permute-start(bf16[24,1536]{1,0:T(8,128)(2,1)S(1)} %pad_maximum_fusion.3), channel_id=1, source_target_pairs={{0,68},{8,11},{4,0},{12,15},{64,4},{72,75},{68,64},{76,79},{16,84}... | collective-permute-start | bytes 221192 | tf_op jit(solution)/shard_map/ppermute | solution.py:51
  15.8 3.4 %collective-permute-done.2 = bf16[24,1536]{1,0:T(8,128)(2,1)S(1)} collective-permute-done((bf16[24,1536]{1,0:T(8,128)(2,1)S(1)}, bf16[24,1536]{1,0:T(8,128)(2,1)S(1)}, u32[]{:S(2)}, u32[]{:S(2)}) %collective-permute-start.2) | collective-permute-done | bytes 73760 | tf_op jit(solution)/shard_map/ppermute | solution.py:51
  20.7 4.1 %collective-permute-start.9 = (bf16[96,1536]{1,0:T(8,128)(2,1)S(1)}, bf16[96,1536]{1,0:T(8,128)(2,1)S(1)}, u32[]{:S(2)}, u32[]{:S(2)}) collective-permute-start(bf16[96,1536]{1,0:T(8,128)(2,1)S(1)} %pad_maximum_fusion.2), channel_id=1, source_target_pairs={{0,48},{8,76},{4,52},{12,8},{64,112},{72,12},{68,116},{76,72},{16,... | collective-permute-start | bytes 884744 | tf_op jit(solution)/shard_map/ppermute | solution.py:51
  28.9 2.8 %collective-permute-done.9 = bf16[96,1536]{1,0:T(8,128)(2,1)S(1)} collective-permute-done((bf16[96,1536]{1,0:T(8,128)(2,1)S(1)}, bf16[96,1536]{1,0:T(8,128)(2,1)S(1)}, u32[]{:S(2)}, u32[]{:S(2)}) %collective-permute-start.9) | collective-permute-done | bytes 294944 | tf_op jit(solution)/shard_map/ppermute | solution.py:51
  32.1 3.1 %collective-permute-done.7 = bf16[96,1536]{1,0:T(8,128)(2,1)S(1)} collective-permute-done((bf16[96,1536]{1,0:T(8,128)(2,1)S(1)}, bf16[96,1536]{1,0:T(8,128)(2,1)S(1)}, u32[]{:S(2)}, u32[]{:S(2)}) %collective-permute-start.7) | collective-permute-done | bytes 294944 | tf_op jit(solution)/shard_map/ppermute | solution.py:51
  35.2 12.8 %collective-permute-start.11 = (bf16[384,1536]{1,0:T(8,128)(2,1)S(1)}, bf16[384,1536]{1,0:T(8,128)(2,1)S(1)}, u32[]{:S(2)}, u32[]{:S(2)}) collective-permute-start(bf16[384,1536]{1,0:T(8,128)(2,1)S(1)} %pad_maximum_fusion.w0.r0), channel_id=1, source_target_pairs={{0,3},{8,56},{4,7},{12,60},{64,67},{72,120},{68,71},{76,124},{16,1... | collective-permute-start | bytes 3538952 | tf_op jit(solution)/shard_map/ppermute | solution.py:51
  48.8 3.7 %shard_map.87.mine_ref = bf16[448,1536]{1,0:T(8,128)(2,1)S(1)} custom-call(s32[3]{0:T(128)S(1)} %pad_add_fusion.place_ref, bf16[448,1664]{1,0:T(8,128)(2,1)S(1)} %get-tuple-element.80.tokens_ref.amine_ref, s32[1,1536]{1,0:T(1,128)S(1)} %get-tuple-element.81.feature_ref), custom_call_target="tpu_custom_call" | custom-call | flops 1000 | bytes 1000 | tf_op jit(solution)/shard_map/pallas_call | solution.py:104
  52.5 8.6 %collective-permute-done.11.w3.r3 = bf16[384,1536]{1,0:T(8,128)(2,1)S(1)} collective-permute-done((bf16[384,1536]{1,0:T(8,128)(2,1)S(1)}, bf16[384,1536]{1,0:T(8,128)(2,1)S(1)}, u32[]{:S(2)}, u32[]{:S(2)}) %collective-permute-start.11) | collective-permute-done | bytes 1179680 | tf_op jit(solution)/shard_map/ppermute | solution.py:51
  61.1 3.1 %collective-permute-done.10.w1.r1 = bf16[384,1536]{1,0:T(8,128)(2,1)S(1)} collective-permute-done((bf16[384,1536]{1,0:T(8,128)(2,1)S(1)}, bf16[384,1536]{1,0:T(8,128)(2,1)S(1)}, u32[]{:S(2)}, u32[]{:S(2)}) %collective-permute-start.10) | collective-permute-done | bytes 1179680 | tf_op jit(solution)/shard_map/ppermute | solution.py:51
  65.9 3.7 %shard_map.88.other_ref = bf16[448,1536]{1,0:T(8,128)(2,1)S(1)} custom-call(s32[3]{0:T(128)S(1)} %pad_add_fusion.place_ref, bf16[448,1664]{1,0:T(8,128)(2,1)S(1)} %collective-permute-done.12.tokens_ref.aother_ref, s32[1,1536]{1,0:T(1,128)S(1)} %get-tuple-element.81.feature_ref), custom_call_target="tpu_custom_call" | custom-call | flops 1000 | bytes 1000 | tf_op jit(solution)/shard_map/pallas_call | solution.py:104
  69.6 3.7 %shard_map.90.sums_ref = f32[768,768]{1,0:T(8,128)S(1)} custom-call(s32[3]{0:T(128)S(1)} %pad_add_fusion.place_ref, bf16[384,1536]{1,0:T(8,128)(2,1)S(1)} %pad_maximum_fusion.w0.r0, bf16[384,1536]{1,0:T(8,128)(2,1)S(1)} %collective-permute-done.10.w1.r1, bf16[384,1536]{1,0:T(8,128)(2,1)S(1)} %collective-permute-done.11.w3.r3, ...), custom_call_target="tpu_custom_call" | custom-call | flops 1000 | bytes 1000 | tf_op jit(solution)/shard_map/pallas_call | solution.py:104
  74.4 2.3 %shard_map.91 = (bf16[768,768]{1,0:T(8,128)(2,1)S(1)}, bf16[384,768]{1,0:T(8,128)(2,1)S(1)}) custom-call(s32[3]{0:T(128)S(1)} %pad_add_fusion.place_ref, f32[768,768]{1,0:T(8,128)S(1)} %shard_map.90.sums_ref, bf16[192,1536]{1,0:T(8,128)(2,1)S(1)} %collective-permute-done.13.w2_top.r2_top, bf16[192,1536]{1,0:T(8,128)(2,1)S(1)} %collective-permute-done.14.w2_low.r2_low, ...), custom_call_target="tpu_custom_call" | custom-call | flops 1000 | bytes 1000 | tf_op jit(solution)/shard_map/pallas_call | solution.py:104
  77.0 7.1 %shard_map.89 = (bf16[896,1152]{1,0:T(8,128)(2,1)S(1)}, bf16[256,1536]{1,0:T(8,128)(2,1)S(1)}) custom-call(s32[3]{0:T(128)S(1)} %pad_add_fusion.place_ref, bf16[448,1536]{1,0:T(8,128)(2,1)S(1)} %shard_map.87.mine_ref, bf16[448,1536]{1,0:T(8,128)(2,1)S(1)} %shard_map.88.other_ref, bf16[384,1536]{1,0:T(8,128)(2,1)S(1)} %pad_maximum_fusion.w0.r0, ...), custom_call_target="tpu_custom_call" | custom-call | flops 1000 | bytes 1000 | tf_op jit(solution)/shard_map/pallas_call | solution.py:104
  84.1 12.6 %shard_map.92 = (bf16[256,384]{1,0:T(8,128)(2,1)S(1)}, bf16[256,1152]{1,0:T(8,128)(2,1)S(1)}, bf16[384,1152]{1,0:T(8,128)(2,1)S(1)}, bf16[384,1152]{1,0:T(8,128)...) custom-call(s32[3]{0:T(128)S(1)} %pad_add_fusion.place_ref, ...), custom_call_target="tpu_custom_call" | custom-call | flops 1000 | bytes 1000 | tf_op jit(solution)/shard_map/pallas_call | solution.py:104
  99.4 5.9 %shard_map.93 = (bf16[128,1536]{1,0:T(8,128)(2,1)S(1)}, bf16[128,1536]{1,0:T(8,128)(2,1)S(1)}) custom-call(s32[3]{0:T(128)S(1)} %pad_add_fusion.place_ref, bf16[256,1152]{1,0:T(8,128)(2,1)S(1)} %get-tuple-element.97.grads_ref, bf16[384,1536]{1,0:T(8,128)(2,1)S(1)} %pad_maximum_fusion.w0.r0, bf16[384,1536]{1,0:T(8,128)(2,1)S(1)} %collective-permute-done.10.w1.r1, ...), custom_call_target="tpu_custom_call" | custom-call | flops 1000 | bytes 1000 | tf_op jit(solution)/shard_map/pallas_call | solution.py:104
  106.4 3.3 %shard_map.94 = (bf16[384,384]{1,0:T(8,128)(2,1)S(1)}, bf16[384,384]{1,0:T(8,128)(2,1)S(1)}, bf16[384,384]{1,0:T(8,128)(2,1)S(1)}, bf16[384,384]{1,0:T(8,128)(2,1)S(1)}) custom-call(s32[3]{0:T(128)S(1)} %pad_add_fusion.place_ref, bf16[256,384]{1,0:T(8,128)(2,1)S(1)} %get-tuple-element.96.mine_ref, bf16[256,384]{1,0:T(8,128)(2,1)S(1)} %collective-permute-done.18.other_ref, ...), custom_call_target="tpu_custom_call" | custom-call | flops 1000 | bytes 1000 | tf_op jit(solution)/shard_map/pallas_call | solution.py:104
  112.6 6.4 %collective-permute-start.23 = (bf16[384,384]{1,0:T(8,128)(2,1)S(1)}, bf16[384,384]{1,0:T(8,128)(2,1)S(1)}, u32[]{:S(2)}, u32[]{:S(2)}) collective-permute-start(bf16[384,384]{1,0:T(8,128)(2,1)S(1)} %get-tuple-element.109), channel_id=1, source_target_pairs={{0,1},{8,24},{4,5},{12,28},{64,65},{72,88},{68,69},{76,92},{16,17}... | collective-permute-start | bytes 884744 | tf_op jit(solution)/shard_map/ppermute | solution.py:51
  121.7 2.2 %collective-permute-done.22 = bf16[384,384]{1,0:T(8,128)(2,1)S(1)} collective-permute-done((bf16[384,384]{1,0:T(8,128)(2,1)S(1)}, bf16[384,384]{1,0:T(8,128)(2,1)S(1)}, u32[]{:S(2)}, u32[]{:S(2)}) %collective-permute-start.22) | collective-permute-done | bytes 294944 | tf_op jit(solution)/shard_map/ppermute | solution.py:51
  124.0 3.1 %collective-permute-done.23 = bf16[384,384]{1,0:T(8,128)(2,1)S(1)} collective-permute-done((bf16[384,384]{1,0:T(8,128)(2,1)S(1)}, bf16[384,384]{1,0:T(8,128)(2,1)S(1)}, u32[]{:S(2)}, u32[]{:S(2)}) %collective-permute-start.23) | collective-permute-done | bytes 294944 | tf_op jit(solution)/shard_map/ppermute | solution.py:51
  127.4 4.2 %collective-permute-start.24 = (bf16[96,1536]{1,0:T(8,128)(2,1)S(1)}, bf16[96,1536]{1,0:T(8,128)(2,1)S(1)}, u32[]{:S(2)}, u32[]{:S(2)}) collective-permute-start(bf16[96,1536]{1,0:T(8,128)(2,1)S(1)} %get-tuple-element.126), channel_id=1, source_target_pairs={{0,48},{8,76},{4,52},{12,8},{64,112},{72,12},{68,116},{76,72},{16,... | collective-permute-start | bytes 884744 | tf_op jit(solution)/shard_map/ppermute | solution.py:51
  135.2 6.3 %collective-permute-done.26 = bf16[96,1536]{1,0:T(8,128)(2,1)S(1)} collective-permute-done((bf16[96,1536]{1,0:T(8,128)(2,1)S(1)}, bf16[96,1536]{1,0:T(8,128)(2,1)S(1)}, u32[]{:S(2)}, u32[]{:S(2)}) %collective-permute-start.26) | collective-permute-done | bytes 294944 | tf_op jit(solution)/shard_map/ppermute | solution.py:51
  143.9 2.4 %collective-permute-start.31 = (f32[128,768]{1,0:T(8,128)S(1)}, f32[128,768]{1,0:T(8,128)S(1)}, u32[]{:S(2)}, u32[]{:S(2)}) collective-permute-start(f32[128,768]{1,0:T(8,128)S(1)} %get-tuple-element.116), channel_id=1, source_target_pairs={{0,8},{8,0},{1,9},{9,1},{2,10},{10,2},{3,11},{11,3},{4,12},{12,4},... | collective-permute-start | bytes 1179656 | tf_op jit(solution)/shard_map/ppermute | solution.py:55
  148.7 3.1 %collective-permute-start.30 = (f32[12,1536]{1,0:T(8,128)}, f32[12,1536]{1,0:T(8,128)S(1)}, u32[]{:S(2)}, u32[]{:S(2)}) collective-permute-start(f32[12,1536]{1,0:T(8,128)} %get-tuple-element.133), channel_id=1, source_target_pairs={{0,8},{8,0},{1,9},{9,1},{2,10},{10,2},{3,11},{11,3},{4,12},{12,4},... | collective-permute-start | bytes 221192 | tf_op jit(solution)/shard_map/ppermute | solution.py:55
  (123 shorter events, 40.8 us)
Async XLA Ops:
  8.6 11.3 %collective-permute-start.4 = (bf16[144,1664]{1,0:T(8,128)(2,1)S(1)}, bf16[144,1664]{1,0:T(8,128)(2,1)S(1)}, u32[]{:S(2)}, u32[]{:S(2)}) collective-permute-start(bf16[144,1664]{1,0:T(8,128)(2,1)S(1)} %get-tuple-element.68), channel_id=1, source_target_pairs={{8,16},{16,8},{24,32},{32,24},{40,48},{48,40},{56,64},{64,56},{72,... | collective-permute-start | bytes 1437704 | tf_op jit(solution)/shard_map/ppermute | solution.py:60
  20.7 10.9 %collective-permute-start.9 = (bf16[96,1536]{1,0:T(8,128)(2,1)S(1)}, bf16[96,1536]{1,0:T(8,128)(2,1)S(1)}, u32[]{:S(2)}, u32[]{:S(2)}) collective-permute-start(bf16[96,1536]{1,0:T(8,128)(2,1)S(1)} %pad_maximum_fusion.2), channel_id=1, source_target_pairs={{0,48},{8,76},{4,52},{12,8},{64,112},{72,12},{68,116},{76,72},{16,... | collective-permute-start | bytes 884744 | tf_op jit(solution)/shard_map/ppermute | solution.py:51
  24.9 7.2 %collective-permute-start.8 = (bf16[96,1536]{1,0:T(8,128)(2,1)S(1)}, bf16[96,1536]{1,0:T(8,128)(2,1)S(1)}, u32[]{:S(2)}, u32[]{:S(2)}) collective-permute-start(bf16[96,1536]{1,0:T(8,128)(2,1)S(1)} %pad_maximum_fusion.2), channel_id=1, source_target_pairs={{0,32},{8,72},{4,36},{12,76},{64,96},{72,8},{68,100},{76,12},{16,4... | collective-permute-start | bytes 884744 | tf_op jit(solution)/shard_map/ppermute | solution.py:51
  24.9 10.2 %collective-permute-start.7 = (bf16[96,1536]{1,0:T(8,128)(2,1)S(1)}, bf16[96,1536]{1,0:T(8,128)(2,1)S(1)}, u32[]{:S(2)}, u32[]{:S(2)}) collective-permute-start(bf16[96,1536]{1,0:T(8,128)(2,1)S(1)} %pad_maximum_fusion.2), channel_id=1, source_target_pairs={{0,16},{8,12},{4,20},{12,72},{64,80},{72,76},{68,84},{76,8},{16,32... | collective-permute-start | bytes 884744 | tf_op jit(solution)/shard_map/ppermute | solution.py:51
  25.6 22.4 %collective-permute-start.5 = (bf16[160,1664]{1,0:T(8,128)(2,1)S(1)}, bf16[160,1664]{1,0:T(8,128)(2,1)S(1)}, u32[]{:S(2)}, u32[]{:S(2)}) collective-permute-start(bf16[160,1664]{1,0:T(8,128)(2,1)S(1)} %get-tuple-element.78), channel_id=1, source_target_pairs={{0,1},{1,2},{2,3},{3,4},{4,5},{5,6},{6,7},{8,9},{9,10},{10,11},{11... | collective-permute-start | bytes 1597448 | tf_op jit(solution)/shard_map/ppermute | solution.py:65
  27.6 20.4 %collective-permute-start.6 = (bf16[160,1664]{1,0:T(8,128)(2,1)S(1)}, bf16[160,1664]{1,0:T(8,128)(2,1)S(1)}, u32[]{:S(2)}, u32[]{:S(2)}) collective-permute-start(bf16[160,1664]{1,0:T(8,128)(2,1)S(1)} %get-tuple-element.79), channel_id=1, source_target_pairs={{1,0},{2,1},{3,2},{4,3},{5,4},{6,5},{7,6},{9,8},{10,9},{11,10},{12... | collective-permute-start | bytes 1597448 | tf_op jit(solution)/shard_map/ppermute | solution.py:65
  35.2 25.9 %collective-permute-start.11 = (bf16[384,1536]{1,0:T(8,128)(2,1)S(1)}, bf16[384,1536]{1,0:T(8,128)(2,1)S(1)}, u32[]{:S(2)}, u32[]{:S(2)}) collective-permute-start(bf16[384,1536]{1,0:T(8,128)(2,1)S(1)} %pad_maximum_fusion.w0.r0), channel_id=1, source_target_pairs={{0,3},{8,56},{4,7},{12,60},{64,67},{72,120},{68,71},{76,124},{16,1... | collective-permute-start | bytes 3538952 | tf_op jit(solution)/shard_map/ppermute | solution.py:51
  48.0 16.3 %collective-permute-start.10 = (bf16[384,1536]{1,0:T(8,128)(2,1)S(1)}, bf16[384,1536]{1,0:T(8,128)(2,1)S(1)}, u32[]{:S(2)}, u32[]{:S(2)}) collective-permute-start(bf16[384,1536]{1,0:T(8,128)(2,1)S(1)} %pad_maximum_fusion.w0.r0), channel_id=1, source_target_pairs={{0,1},{8,24},{4,5},{12,28},{64,65},{72,88},{68,69},{76,92},{16,17}... | collective-permute-start | bytes 3538952 | tf_op jit(solution)/shard_map/ppermute | solution.py:51
  48.7 17.1 %collective-permute-start.12 = (bf16[448,1664]{1,0:T(8,128)(2,1)S(1)}, bf16[448,1664]{1,0:T(8,128)(2,1)S(1)}, u32[]{:S(2)}, u32[]{:S(2)}) collective-permute-start(bf16[448,1664]{1,0:T(8,128)(2,1)S(1)} %get-tuple-element.80.tokens_ref.amine_ref), channel_id=1, source_target_pairs={{0,8},{8,0},{1,9},{9,1},{2,10},{10,2},{3,11},{11,3},{4,12},{12,4},... | collective-permute-start | bytes 4472840 | tf_op jit(solution)/shard_map/ppermute | solution.py:55
  64.3 9.0 %collective-permute-start.14 = (bf16[192,1536]{1,0:T(8,128)(2,1)S(1)}, bf16[192,1536]{1,0:T(8,128)(2,1)S(1)}, u32[]{:S(2)}, u32[]{:S(2)}) collective-permute-start(bf16[192,1536]{1,0:T(8,128)(2,1)S(1)} %slice.89), channel_id=1, source_target_pairs={{0,3},{8,56},{4,7},{12,60},{64,67},{72,120},{68,71},{76,124},{16,1... | collective-permute-start | bytes 1769480 | tf_op jit(solution)/shard_map/ppermute | solution.py:51
  64.4 10.0 %collective-permute-start.13 = (bf16[192,1536]{1,0:T(8,128)(2,1)S(1)}, bf16[192,1536]{1,0:T(8,128)(2,1)S(1)}, u32[]{:S(2)}, u32[]{:S(2)}) collective-permute-start(bf16[192,1536]{1,0:T(8,128)(2,1)S(1)} %slice.88), channel_id=1, source_target_pairs={{0,1},{8,24},{4,5},{12,28},{64,65},{72,88},{68,69},{76,92},{16,17}... | collective-permute-start | bytes 1769480 | tf_op jit(solution)/shard_map/ppermute | solution.py:51
  65.9 18.3 %collective-permute-start.15 = (bf16[288,1664]{1,0:T(8,128)(2,1)S(1)}, bf16[288,1664]{1,0:T(8,128)(2,1)S(1)}, u32[]{:S(2)}, u32[]{:S(2)}) collective-permute-start(bf16[288,1664]{1,0:T(8,128)(2,1)S(1)} %get-tuple-element.90.gmine_ref), channel_id=1, source_target_pairs={{0,8},{8,0},{1,9},{9,1},{2,10},{10,2},{3,11},{11,3},{4,12},{12,4},... | collective-permute-start | bytes 2875400 | tf_op jit(solution)/shard_map/ppermute | solution.py:55
  76.7 7.4 %collective-permute-start.16 = (bf16[384,768]{1,0:T(8,128)(2,1)S(1)}, bf16[384,768]{1,0:T(8,128)(2,1)S(1)}, u32[]{:S(2)}, u32[]{:S(2)}) collective-permute-start(bf16[384,768]{1,0:T(8,128)(2,1)S(1)} %get-tuple-element.93), channel_id=1, source_target_pairs={{0,8},{8,0},{1,9},{9,1},{2,10},{10,2},{3,11},{11,3},{4,12},{12,4},... | collective-permute-start | bytes 1769480 | tf_op jit(solution)/shard_map/ppermute | solution.py:55
  96.8 15.6 %collective-permute-start.17 = (bf16[384,1152]{1,0:T(8,128)(2,1)S(1)}, bf16[384,1152]{1,0:T(8,128)(2,1)S(1)}, u32[]{:S(2)}, u32[]{:S(2)}) collective-permute-start(bf16[384,1152]{1,0:T(8,128)(2,1)S(1)} %get-tuple-element.95), channel_id=1, source_target_pairs={{0,3},{8,56},{4,7},{12,60},{64,67},{72,120},{68,71},{76,124},{16,1... | collective-permute-start | bytes 2654216 | tf_op jit(solution)/shard_map/ppermute | solution.py:51
  97.6 21.4 %collective-permute-start.19 = (bf16[384,1152]{1,0:T(8,128)(2,1)S(1)}, bf16[384,1152]{1,0:T(8,128)(2,1)S(1)}, u32[]{:S(2)}, u32[]{:S(2)}) collective-permute-start(bf16[384,1152]{1,0:T(8,128)(2,1)S(1)} %get-tuple-element.104), channel_id=1, source_target_pairs={{0,2},{8,40},{4,6},{12,44},{64,66},{72,104},{68,70},{76,108},{16,1... | collective-permute-start | bytes 2654216 | tf_op jit(solution)/shard_map/ppermute | solution.py:51
  98.8 21.9 %collective-permute-start.20 = (bf16[384,1152]{1,0:T(8,128)(2,1)S(1)}, bf16[384,1152]{1,0:T(8,128)(2,1)S(1)}, u32[]{:S(2)}, u32[]{:S(2)}) collective-permute-start(bf16[384,1152]{1,0:T(8,128)(2,1)S(1)} %get-tuple-element.105), channel_id=1, source_target_pairs={{0,1},{8,24},{4,5},{12,28},{64,65},{72,88},{68,69},{76,92},{16,17}... | collective-permute-start | bytes 2654216 | tf_op jit(solution)/shard_map/ppermute | solution.py:51
  98.8 6.5 %collective-permute-start.18 = (bf16[256,384]{1,0:T(8,128)(2,1)S(1)}, bf16[256,384]{1,0:T(8,128)(2,1)S(1)}, u32[]{:S(2)}, u32[]{:S(2)}) collective-permute-start(bf16[256,384]{1,0:T(8,128)(2,1)S(1)} %get-tuple-element.96.mine_ref), channel_id=1, source_target_pairs={{0,8},{8,0},{1,9},{9,1},{2,10},{10,2},{3,11},{11,3},{4,12},{12,4},... | collective-permute-start | bytes 589832 | tf_op jit(solution)/shard_map/ppermute | solution.py:55
  109.7 12.0 %collective-permute-start.21 = (bf16[384,384]{1,0:T(8,128)(2,1)S(1)}, bf16[384,384]{1,0:T(8,128)(2,1)S(1)}, u32[]{:S(2)}, u32[]{:S(2)}) collective-permute-start(bf16[384,384]{1,0:T(8,128)(2,1)S(1)} %get-tuple-element.107), channel_id=1, source_target_pairs={{0,3},{8,56},{4,7},{12,60},{64,67},{72,120},{68,71},{76,124},{16,1... | collective-permute-start | bytes 884744 | tf_op jit(solution)/shard_map/ppermute | solution.py:51
  111.9 12.1 %collective-permute-start.22 = (bf16[384,384]{1,0:T(8,128)(2,1)S(1)}, bf16[384,384]{1,0:T(8,128)(2,1)S(1)}, u32[]{:S(2)}, u32[]{:S(2)}) collective-permute-start(bf16[384,384]{1,0:T(8,128)(2,1)S(1)} %get-tuple-element.108), channel_id=1, source_target_pairs={{0,2},{8,40},{4,6},{12,44},{64,66},{72,104},{68,70},{76,108},{16,1... | collective-permute-start | bytes 884744 | tf_op jit(solution)/shard_map/ppermute | solution.py:51
  112.6 14.5 %collective-permute-start.23 = (bf16[384,384]{1,0:T(8,128)(2,1)S(1)}, bf16[384,384]{1,0:T(8,128)(2,1)S(1)}, u32[]{:S(2)}, u32[]{:S(2)}) collective-permute-start(bf16[384,384]{1,0:T(8,128)(2,1)S(1)} %get-tuple-element.109), channel_id=1, source_target_pairs={{0,1},{8,24},{4,5},{12,28},{64,65},{72,88},{68,69},{76,92},{16,17}... | collective-permute-start | bytes 884744 | tf_op jit(solution)/shard_map/ppermute | solution.py:51
  127.4 7.8 %collective-permute-start.24 = (bf16[96,1536]{1,0:T(8,128)(2,1)S(1)}, bf16[96,1536]{1,0:T(8,128)(2,1)S(1)}, u32[]{:S(2)}, u32[]{:S(2)}) collective-permute-start(bf16[96,1536]{1,0:T(8,128)(2,1)S(1)} %get-tuple-element.126), channel_id=1, source_target_pairs={{0,48},{8,76},{4,52},{12,8},{64,112},{72,12},{68,116},{76,72},{16,... | collective-permute-start | bytes 884744 | tf_op jit(solution)/shard_map/ppermute | solution.py:51
  131.5 9.9 %collective-permute-start.26 = (bf16[96,1536]{1,0:T(8,128)(2,1)S(1)}, bf16[96,1536]{1,0:T(8,128)(2,1)S(1)}, u32[]{:S(2)}, u32[]{:S(2)}) collective-permute-start(bf16[96,1536]{1,0:T(8,128)(2,1)S(1)} %get-tuple-element.127), channel_id=1, source_target_pairs={{0,16},{8,12},{4,20},{12,72},{64,80},{72,76},{68,84},{76,8},{16,32... | collective-permute-start | bytes 884744 | tf_op jit(solution)/shard_map/ppermute | solution.py:51
  131.6 9.9 %collective-permute-start.25 = (bf16[96,1536]{1,0:T(8,128)(2,1)S(1)}, bf16[96,1536]{1,0:T(8,128)(2,1)S(1)}, u32[]{:S(2)}, u32[]{:S(2)}) collective-permute-start(bf16[96,1536]{1,0:T(8,128)(2,1)S(1)} %get-tuple-element.128), channel_id=1, source_target_pairs={{0,32},{8,72},{4,36},{12,76},{64,96},{72,8},{68,100},{76,12},{16,4... | collective-permute-start | bytes 884744 | tf_op jit(solution)/shard_map/ppermute | solution.py:51
  143.9 8.1 %collective-permute-start.31 = (f32[128,768]{1,0:T(8,128)S(1)}, f32[128,768]{1,0:T(8,128)S(1)}, u32[]{:S(2)}, u32[]{:S(2)}) collective-permute-start(f32[128,768]{1,0:T(8,128)S(1)} %get-tuple-element.116), channel_id=1, source_target_pairs={{0,8},{8,0},{1,9},{9,1},{2,10},{10,2},{3,11},{11,3},{4,12},{12,4},... | collective-permute-start | bytes 1179656 | tf_op jit(solution)/shard_map/ppermute | solution.py:55
  (13 other events, 86.9 us)

commit v2 on v1

--- a/solution.py
+++ b/solution.py
@@ -198,35 +198,44 @@
     lax.fori_loop(0, D // 256, part, 0)
 
 
-def out_rows_product(row_ref, part, h, first, chunk):
-    row = lax.broadcasted_iota(jnp.int32, (128, D // 4), 0) + (first + h * DH)
-    order = one_hot(row == row_ref[:, part * 384 : (part + 1) * 384])
+def out_rows_product(row_ref, part, first, chunk):
+    row = row_ref[:, part * 384 : (part + 1) * 384]
+    row = jnp.where(row < DH, row, row - DH)
+    order = one_hot(lax.broadcasted_iota(jnp.int32, (128, D // 4), 0) + first == row)
     return jnp.dot(order, chunk, preferred_element_type=f32)
 
 
-def near_rows_kernel(place_ref, r0, r1, r3, row_ref, sums_out):
+def by_half(chunk):
+    upper = lax.broadcasted_iota(jnp.int32, chunk.shape, 0) % 24 < 12
+    chunk = chunk.astype(f32)
+    halves = [jnp.where(upper, chunk, 0.0), jnp.where(upper, 0.0, chunk)]
+    return jnp.concatenate(halves, axis=1).astype(bf16)
+
+
+def near_rows_kernel(place_ref, r0, r1, r3, row_ref, sums_out, halves):
+    for i, ref in enumerate((r0, r1, r3)):
+        halves[i, :, :] = by_half(ref[:, 3 * HALF :])
+
     def part(n, carry):
         first = pl.multiple_of(n * 128, 128)
-        for h in range(2):
-            total = out_rows_product(row_ref, 0, h, first, r0[:, 3 * HALF :])
-            total += out_rows_product(row_ref, 1, h, first, r1[:, 3 * HALF :])
-            total += out_rows_product(row_ref, 3, h, first, r3[:, 3 * HALF :])
-            sums_out[pl.ds(first, 128), h * HALF : (h + 1) * HALF] = total
+        total = out_rows_product(row_ref, 0, first, halves[0])
+        total += out_rows_product(row_ref, 1, first, halves[1])
+        total += out_rows_product(row_ref, 3, first, halves[2])
+        sums_out[pl.ds(first, 128), :] = total
         return carry
 
     lax.fori_loop(0, DH // 128, part, 0)
 
 
-def out_rows_kernel(place_ref, sums_ref, r2_top, r2_low, row_ref, half_out, sent_out):
+def out_rows_kernel(place_ref, sums_ref, r2_top, r2_low, row_ref, half_out, sent_out, halves):
     core = place_ref[1]
-    far = jnp.concatenate([r2_top[:, 3 * HALF :], r2_low[:, 3 * HALF :]], axis=0)
+    halves[:192, :] = by_half(r2_top[:, 3 * HALF :])
+    halves[192:, :] = by_half(r2_low[:, 3 * HALF :])
 
     def part(n, carry):
         first = pl.multiple_of(n * 128, 128)
-        for h in range(2):
-            lanes = slice(h * HALF, (h + 1) * HALF)
-            total = sums_ref[pl.ds(first, 128), lanes] + out_rows_product(row_ref, 2, h, first, far)
-            half_out[pl.ds(first, 128), lanes] = total.astype(bf16)
+        rows = pl.ds(first, 128)
+        half_out[rows, :] = (sums_ref[rows, :] + out_rows_product(row_ref, 2, first, halves[...])).astype(bf16)
         return carry
 
     lax.fori_loop(0, DH // 128, part, 0)
@@ -246,8 +255,8 @@
             hidden[to, :] = source[pl.ds(own_at + r * KEY_COLS, SIDE), :]
 
         def project(t, carry, source=source, side=side):
-            rows = pl.ds(pl.multiple_of(t * 112, 112), 112)
-            to = pl.ds(pl.multiple_of(side * half + t * 112, 112), 112)
+            rows = pl.ds(pl.multiple_of(t * 224, 224), 224)
+            to = pl.ds(pl.multiple_of(side * half + t * 224, 224), 224)
             total = jnp.dot(source[rows, :part], w0[:, : 3 * HALF], preferred_element_type=f32)
             for k, ref in ((1, w1), (2, w2), (3, w3)):
                 total += jnp.dot(
@@ -256,7 +265,7 @@
             packed[to, :] = total.astype(bf16)
             return carry
 
-        lax.fori_loop(0, 4, project, 0)
+        lax.fori_loop(0, 2, project, 0)
 
 
 def out_grads_kernel(place_ref, mine_ref, other_ref, grad_ref, row_ref, c0, c1, c2, c3):
@@ -441,7 +450,7 @@
             dk[keys_at, lanes[g]] += key_sum[g]
         return carry
 
-    lax.fori_loop(0, QUERY_ROWS // 2, block, 0)
+    lax.fori_loop(0, QUERY_ROWS // 2, block, 0, unroll=True)
     for r in range(SIDE):
         own = pl.ds(r * SIDE, SIDE)
         at_query = pl.ds((r + 3) * QUERY_COLS, SIDE)
@@ -556,12 +565,13 @@
     hidden_mine, near, back = lax.optimization_barrier((hidden_mine, near, back))
     weights = [block, near, *relay_ring(near, back), back]
     hidden_other, row_line = lax.optimization_barrier((hidden_other, row_line))
-    (near_rows,) = on_chip(near_rows_kernel, place, [block, near, back, row_line], [((DH, DH), f32)])
+    (near_rows,) = on_chip(near_rows_kernel, place, [block, near, back, row_line], [((DH, DH), f32)], [((3, D // 4, DH), bf16)])
     half_out, sent_rows = on_chip(
         out_rows_kernel,
         place,
         [near_rows, weights[2], weights[3], row_line],
         [((DH, DH), bf16), ((HALF, DH), bf16)],
+        [((D // 4, DH), bf16)],
     )
     other_rows = swap_cores(sent_rows)
     packed, hidden = on_chip(

time: 156 us -> 153 us (0.981)
  Pallas kernels: 48 us -> 45.2 us
    pallas_call x13, Pallas kernels: 48 us -> 45.2 us  [on_chip(): pl.pallas_call(kernel, out_shape=tuple((jax.ShapeDtypeStruct(shape, kind)...]
where the time goes in v2:
time: 153 us
  starting transfers between devices  55.9 us (37%)
  Pallas kernels  45.2 us (30%)
  waiting for transfers between devices  41.6 us (27%)
  local copies, waits for them, and re-layouts  5.35 us (3%)
  other arithmetic  3.53 us (2%)
    pallas_call x13, Pallas kernels, on_chip(): pl.pallas_call(kernel, out_shape=tuple((jax.ShapeDtypeStruct(shape, kind)...  45.2 us
    ppermute x22, starting transfers between devices, shifted(): return lax.ppermute(value, AXES, stage_pairs(axes, shift))  41.6 us
    ppermute x22, waiting for transfers between devices, shifted(): return lax.ppermute(value, AXES, stage_pairs(axes, shift))  41.5 us
    ppermute x8, starting transfers between devices, swap_cores(): return lax.ppermute(value, 'c', [(0, 1), (1, 0)])  7.89 us
    ppermute x2, starting transfers between devices, col_neighbour(): lax.ppermute(value, ('zl', 'x'), [(a, b) for a, b in pairs if 0 <= b < 8])  3.27 us
    ppermute x1, starting transfers between devices, row_neighbour(): lax.ppermute(value, ('zh', 'y', 'c'), [(a, b) for a, b in pairs if 0 <= b...  3.2 us
  transfers between devices with their start and end apart: 33, of which 17 were waited for; matrix products, arithmetic and copies ran while one was open for 2% of the time, Pallas kernels for 22%

profile of v2, /device:TPU:1, one launch (start us, length us, event | category | flops | bytes accessed | tf_op | source)
XLA Modules:
  0.0 152.8 jit_solution(11881634745509625635)
XLA Ops:
  8.6 3.2 %collective-permute-start.4 = (bf16[144,1664]{1,0:T(8,128)(2,1)S(1)}, bf16[144,1664]{1,0:T(8,128)(2,1)S(1)}, u32[]{:S(2)}, u32[]{:S(2)}) collective-permute-start(bf16[144,1664]{1,0:T(8,128)(2,1)S(1)} %get-tuple-element.68), channel_id=1, source_target_pairs={{8,16},{16,8},{24,32},{32,24},{40,48},{48,40},{56,64},{64,56},{72,... | collective-permute-start | bytes 1437704 | tf_op jit(solution)/shard_map/ppermute | solution.py:60
  11.9 2.5 %collective-permute-start.3 = (bf16[24,1536]{1,0:T(8,128)(2,1)S(1)}, bf16[24,1536]{1,0:T(8,128)(2,1)S(1)}, u32[]{:S(2)}, u32[]{:S(2)}) collective-permute-start(bf16[24,1536]{1,0:T(8,128)(2,1)S(1)} %pad_maximum_fusion.3), channel_id=1, source_target_pairs={{0,68},{8,11},{4,0},{12,15},{64,4},{72,75},{68,64},{76,79},{16,84}... | collective-permute-start | bytes 221192 | tf_op jit(solution)/shard_map/ppermute | solution.py:51
  15.8 3.4 %collective-permute-done.2 = bf16[24,1536]{1,0:T(8,128)(2,1)S(1)} collective-permute-done((bf16[24,1536]{1,0:T(8,128)(2,1)S(1)}, bf16[24,1536]{1,0:T(8,128)(2,1)S(1)}, u32[]{:S(2)}, u32[]{:S(2)}) %collective-permute-start.2) | collective-permute-done | bytes 73760 | tf_op jit(solution)/shard_map/ppermute | solution.py:51
  20.7 4.1 %collective-permute-start.9 = (bf16[96,1536]{1,0:T(8,128)(2,1)S(1)}, bf16[96,1536]{1,0:T(8,128)(2,1)S(1)}, u32[]{:S(2)}, u32[]{:S(2)}) collective-permute-start(bf16[96,1536]{1,0:T(8,128)(2,1)S(1)} %pad_maximum_fusion.2), channel_id=1, source_target_pairs={{0,48},{8,76},{4,52},{12,8},{64,112},{72,12},{68,116},{76,72},{16,... | collective-permute-start | bytes 884744 | tf_op jit(solution)/shard_map/ppermute | solution.py:51
  28.9 2.8 %collective-permute-done.9 = bf16[96,1536]{1,0:T(8,128)(2,1)S(1)} collective-permute-done((bf16[96,1536]{1,0:T(8,128)(2,1)S(1)}, bf16[96,1536]{1,0:T(8,128)(2,1)S(1)}, u32[]{:S(2)}, u32[]{:S(2)}) %collective-permute-start.9) | collective-permute-done | bytes 294944 | tf_op jit(solution)/shard_map/ppermute | solution.py:51
  32.1 3.1 %collective-permute-done.7 = bf16[96,1536]{1,0:T(8,128)(2,1)S(1)} collective-permute-done((bf16[96,1536]{1,0:T(8,128)(2,1)S(1)}, bf16[96,1536]{1,0:T(8,128)(2,1)S(1)}, u32[]{:S(2)}, u32[]{:S(2)}) %collective-permute-start.7) | collective-permute-done | bytes 294944 | tf_op jit(solution)/shard_map/ppermute | solution.py:51
  35.2 12.8 %collective-permute-start.11 = (bf16[384,1536]{1,0:T(8,128)(2,1)S(1)}, bf16[384,1536]{1,0:T(8,128)(2,1)S(1)}, u32[]{:S(2)}, u32[]{:S(2)}) collective-permute-start(bf16[384,1536]{1,0:T(8,128)(2,1)S(1)} %pad_maximum_fusion.w0.r0), channel_id=1, source_target_pairs={{0,3},{8,56},{4,7},{12,60},{64,67},{72,120},{68,71},{76,124},{16,1... | collective-permute-start | bytes 3538952 | tf_op jit(solution)/shard_map/ppermute | solution.py:51
  48.8 3.7 %shard_map.87.mine_ref = bf16[448,1536]{1,0:T(8,128)(2,1)S(1)} custom-call(s32[3]{0:T(128)S(1)} %pad_add_fusion.place_ref, bf16[448,1664]{1,0:T(8,128)(2,1)S(1)} %get-tuple-element.80.tokens_ref.amine_ref, s32[1,1536]{1,0:T(1,128)S(1)} %get-tuple-element.81.feature_ref), custom_call_target="tpu_custom_call" | custom-call | flops 1000 | bytes 1000 | tf_op jit(solution)/shard_map/pallas_call | solution.py:104
  52.5 8.6 %collective-permute-done.11.w3.r3 = bf16[384,1536]{1,0:T(8,128)(2,1)S(1)} collective-permute-done((bf16[384,1536]{1,0:T(8,128)(2,1)S(1)}, bf16[384,1536]{1,0:T(8,128)(2,1)S(1)}, u32[]{:S(2)}, u32[]{:S(2)}) %collective-permute-start.11) | collective-permute-done | bytes 1179680 | tf_op jit(solution)/shard_map/ppermute | solution.py:51
  61.1 3.1 %collective-permute-done.10.w1.r1 = bf16[384,1536]{1,0:T(8,128)(2,1)S(1)} collective-permute-done((bf16[384,1536]{1,0:T(8,128)(2,1)S(1)}, bf16[384,1536]{1,0:T(8,128)(2,1)S(1)}, u32[]{:S(2)}, u32[]{:S(2)}) %collective-permute-start.10) | collective-permute-done | bytes 1179680 | tf_op jit(solution)/shard_map/ppermute | solution.py:51
  65.9 3.7 %shard_map.88.other_ref = bf16[448,1536]{1,0:T(8,128)(2,1)S(1)} custom-call(s32[3]{0:T(128)S(1)} %pad_add_fusion.place_ref, bf16[448,1664]{1,0:T(8,128)(2,1)S(1)} %collective-permute-done.12.tokens_ref.aother_ref, s32[1,1536]{1,0:T(1,128)S(1)} %get-tuple-element.81.feature_ref), custom_call_target="tpu_custom_call" | custom-call | flops 1000 | bytes 1000 | tf_op jit(solution)/shard_map/pallas_call | solution.py:104
  69.6 3.7 %shard_map.90.sums_ref = f32[768,768]{1,0:T(8,128)S(1)} custom-call(s32[3]{0:T(128)S(1)} %pad_add_fusion.place_ref, bf16[384,1536]{1,0:T(8,128)(2,1)S(1)} %pad_maximum_fusion.w0.r0, bf16[384,1536]{1,0:T(8,128)(2,1)S(1)} %collective-permute-done.10.w1.r1, bf16[384,1536]{1,0:T(8,128)(2,1)S(1)} %collective-permute-done.11.w3.r3, ...), custom_call_target="tpu_custom_call" | custom-call | flops 1000 | bytes 1000 | tf_op jit(solution)/shard_map/pallas_call | solution.py:104
  74.4 2.3 %shard_map.91 = (bf16[768,768]{1,0:T(8,128)(2,1)S(1)}, bf16[384,768]{1,0:T(8,128)(2,1)S(1)}) custom-call(s32[3]{0:T(128)S(1)} %pad_add_fusion.place_ref, f32[768,768]{1,0:T(8,128)S(1)} %shard_map.90.sums_ref, bf16[192,1536]{1,0:T(8,128)(2,1)S(1)} %collective-permute-done.13.w2_top.r2_top, bf16[192,1536]{1,0:T(8,128)(2,1)S(1)} %collective-permute-done.14.w2_low.r2_low, ...), custom_call_target="tpu_custom_call" | custom-call | flops 1000 | bytes 1000 | tf_op jit(solution)/shard_map/pallas_call | solution.py:104
  77.0 5.9 %shard_map.89 = (bf16[896,1152]{1,0:T(8,128)(2,1)S(1)}, bf16[256,1536]{1,0:T(8,128)(2,1)S(1)}) custom-call(s32[3]{0:T(128)S(1)} %pad_add_fusion.place_ref, bf16[448,1536]{1,0:T(8,128)(2,1)S(1)} %shard_map.87.mine_ref, bf16[448,1536]{1,0:T(8,128)(2,1)S(1)} %shard_map.88.other_ref, bf16[384,1536]{1,0:T(8,128)(2,1)S(1)} %pad_maximum_fusion.w0.r0, ...), custom_call_target="tpu_custom_call" | custom-call | flops 1000 | bytes 1000 | tf_op jit(solution)/shard_map/pallas_call | solution.py:104
  82.9 11.1 %shard_map.92 = (bf16[256,384]{1,0:T(8,128)(2,1)S(1)}, bf16[256,1152]{1,0:T(8,128)(2,1)S(1)}, bf16[384,1152]{1,0:T(8,128)(2,1)S(1)}, bf16[384,1152]{1,0:T(8,128)...) custom-call(s32[3]{0:T(128)S(1)} %pad_add_fusion.place_ref, ...), custom_call_target="tpu_custom_call" | custom-call | flops 1000 | bytes 1000 | tf_op jit(solution)/shard_map/pallas_call | solution.py:104
  96.6 5.9 %shard_map.93 = (bf16[128,1536]{1,0:T(8,128)(2,1)S(1)}, bf16[128,1536]{1,0:T(8,128)(2,1)S(1)}) custom-call(s32[3]{0:T(128)S(1)} %pad_add_fusion.place_ref, bf16[256,1152]{1,0:T(8,128)(2,1)S(1)} %get-tuple-element.97.grads_ref, bf16[384,1536]{1,0:T(8,128)(2,1)S(1)} %pad_maximum_fusion.w0.r0, bf16[384,1536]{1,0:T(8,128)(2,1)S(1)} %collective-permute-done.10.w1.r1, ...), custom_call_target="tpu_custom_call" | custom-call | flops 1000 | bytes 1000 | tf_op jit(solution)/shard_map/pallas_call | solution.py:104
  103.6 3.3 %shard_map.94 = (bf16[384,384]{1,0:T(8,128)(2,1)S(1)}, bf16[384,384]{1,0:T(8,128)(2,1)S(1)}, bf16[384,384]{1,0:T(8,128)(2,1)S(1)}, bf16[384,384]{1,0:T(8,128)(2,1)S(1)}) custom-call(s32[3]{0:T(128)S(1)} %pad_add_fusion.place_ref, bf16[256,384]{1,0:T(8,128)(2,1)S(1)} %get-tuple-element.96.mine_ref, bf16[256,384]{1,0:T(8,128)(2,1)S(1)} %collective-permute-done.18.other_ref, ...), custom_call_target="tpu_custom_call" | custom-call | flops 1000 | bytes 1000 | tf_op jit(solution)/shard_map/pallas_call | solution.py:104
  109.8 6.4 %collective-permute-start.23 = (bf16[384,384]{1,0:T(8,128)(2,1)S(1)}, bf16[384,384]{1,0:T(8,128)(2,1)S(1)}, u32[]{:S(2)}, u32[]{:S(2)}) collective-permute-start(bf16[384,384]{1,0:T(8,128)(2,1)S(1)} %get-tuple-element.109), channel_id=1, source_target_pairs={{0,1},{8,24},{4,5},{12,28},{64,65},{72,88},{68,69},{76,92},{16,17}... | collective-permute-start | bytes 884744 | tf_op jit(solution)/shard_map/ppermute | solution.py:51
  121.2 3.1 %collective-permute-done.23 = bf16[384,384]{1,0:T(8,128)(2,1)S(1)} collective-permute-done((bf16[384,384]{1,0:T(8,128)(2,1)S(1)}, bf16[384,384]{1,0:T(8,128)(2,1)S(1)}, u32[]{:S(2)}, u32[]{:S(2)}) %collective-permute-start.23) | collective-permute-done | bytes 294944 | tf_op jit(solution)/shard_map/ppermute | solution.py:51
  124.6 4.2 %collective-permute-start.24 = (bf16[96,1536]{1,0:T(8,128)(2,1)S(1)}, bf16[96,1536]{1,0:T(8,128)(2,1)S(1)}, u32[]{:S(2)}, u32[]{:S(2)}) collective-permute-start(bf16[96,1536]{1,0:T(8,128)(2,1)S(1)} %get-tuple-element.126), channel_id=1, source_target_pairs={{0,48},{8,76},{4,52},{12,8},{64,112},{72,12},{68,116},{76,72},{16,... | collective-permute-start | bytes 884744 | tf_op jit(solution)/shard_map/ppermute | solution.py:51
  130.0 2.4 %collective-permute-done.24 = bf16[96,1536]{1,0:T(8,128)(2,1)S(1)} collective-permute-done((bf16[96,1536]{1,0:T(8,128)(2,1)S(1)}, bf16[96,1536]{1,0:T(8,128)(2,1)S(1)}, u32[]{:S(2)}, u32[]{:S(2)}) %collective-permute-start.24) | collective-permute-done | bytes 294944 | tf_op jit(solution)/shard_map/ppermute | solution.py:51
  132.4 6.3 %collective-permute-done.26 = bf16[96,1536]{1,0:T(8,128)(2,1)S(1)} collective-permute-done((bf16[96,1536]{1,0:T(8,128)(2,1)S(1)}, bf16[96,1536]{1,0:T(8,128)(2,1)S(1)}, u32[]{:S(2)}, u32[]{:S(2)}) %collective-permute-start.26) | collective-permute-done | bytes 294944 | tf_op jit(solution)/shard_map/ppermute | solution.py:51
  141.1 2.3 %collective-permute-start.31 = (f32[128,768]{1,0:T(8,128)S(1)}, f32[128,768]{1,0:T(8,128)S(1)}, u32[]{:S(2)}, u32[]{:S(2)}) collective-permute-start(f32[128,768]{1,0:T(8,128)S(1)} %get-tuple-element.116), channel_id=1, source_target_pairs={{0,8},{8,0},{1,9},{9,1},{2,10},{10,2},{3,11},{11,3},{4,12},{12,4},... | collective-permute-start | bytes 1179656 | tf_op jit(solution)/shard_map/ppermute | solution.py:55
  146.0 3.1 %collective-permute-start.30 = (f32[12,1536]{1,0:T(8,128)}, f32[12,1536]{1,0:T(8,128)S(1)}, u32[]{:S(2)}, u32[]{:S(2)}) collective-permute-start(f32[12,1536]{1,0:T(8,128)} %get-tuple-element.133), channel_id=1, source_target_pairs={{0,8},{8,0},{1,9},{9,1},{2,10},{10,2},{3,11},{11,3},{4,12},{12,4},... | collective-permute-start | bytes 221192 | tf_op jit(solution)/shard_map/ppermute | solution.py:55
  (123 shorter events, 40.6 us)
Async XLA Ops:
  8.6 11.3 %collective-permute-start.4 = (bf16[144,1664]{1,0:T(8,128)(2,1)S(1)}, bf16[144,1664]{1,0:T(8,128)(2,1)S(1)}, u32[]{:S(2)}, u32[]{:S(2)}) collective-permute-start(bf16[144,1664]{1,0:T(8,128)(2,1)S(1)} %get-tuple-element.68), channel_id=1, source_target_pairs={{8,16},{16,8},{24,32},{32,24},{40,48},{48,40},{56,64},{64,56},{72,... | collective-permute-start | bytes 1437704 | tf_op jit(solution)/shard_map/ppermute | solution.py:60
  20.7 10.9 %collective-permute-start.9 = (bf16[96,1536]{1,0:T(8,128)(2,1)S(1)}, bf16[96,1536]{1,0:T(8,128)(2,1)S(1)}, u32[]{:S(2)}, u32[]{:S(2)}) collective-permute-start(bf16[96,1536]{1,0:T(8,128)(2,1)S(1)} %pad_maximum_fusion.2), channel_id=1, source_target_pairs={{0,48},{8,76},{4,52},{12,8},{64,112},{72,12},{68,116},{76,72},{16,... | collective-permute-start | bytes 884744 | tf_op jit(solution)/shard_map/ppermute | solution.py:51
  24.9 7.2 %collective-permute-start.8 = (bf16[96,1536]{1,0:T(8,128)(2,1)S(1)}, bf16[96,1536]{1,0:T(8,128)(2,1)S(1)}, u32[]{:S(2)}, u32[]{:S(2)}) collective-permute-start(bf16[96,1536]{1,0:T(8,128)(2,1)S(1)} %pad_maximum_fusion.2), channel_id=1, source_target_pairs={{0,32},{8,72},{4,36},{12,76},{64,96},{72,8},{68,100},{76,12},{16,4... | collective-permute-start | bytes 884744 | tf_op jit(solution)/shard_map/ppermute | solution.py:51
  24.9 10.2 %collective-permute-start.7 = (bf16[96,1536]{1,0:T(8,128)(2,1)S(1)}, bf16[96,1536]{1,0:T(8,128)(2,1)S(1)}, u32[]{:S(2)}, u32[]{:S(2)}) collective-permute-start(bf16[96,1536]{1,0:T(8,128)(2,1)S(1)} %pad_maximum_fusion.2), channel_id=1, source_target_pairs={{0,16},{8,12},{4,20},{12,72},{64,80},{72,76},{68,84},{76,8},{16,32... | collective-permute-start | bytes 884744 | tf_op jit(solution)/shard_map/ppermute | solution.py:51
  25.6 22.4 %collective-permute-start.5 = (bf16[160,1664]{1,0:T(8,128)(2,1)S(1)}, bf16[160,1664]{1,0:T(8,128)(2,1)S(1)}, u32[]{:S(2)}, u32[]{:S(2)}) collective-permute-start(bf16[160,1664]{1,0:T(8,128)(2,1)S(1)} %get-tuple-element.78), channel_id=1, source_target_pairs={{0,1},{1,2},{2,3},{3,4},{4,5},{5,6},{6,7},{8,9},{9,10},{10,11},{11... | collective-permute-start | bytes 1597448 | tf_op jit(solution)/shard_map/ppermute | solution.py:65
  27.6 20.4 %collective-permute-start.6 = (bf16[160,1664]{1,0:T(8,128)(2,1)S(1)}, bf16[160,1664]{1,0:T(8,128)(2,1)S(1)}, u32[]{:S(2)}, u32[]{:S(2)}) collective-permute-start(bf16[160,1664]{1,0:T(8,128)(2,1)S(1)} %get-tuple-element.79), channel_id=1, source_target_pairs={{1,0},{2,1},{3,2},{4,3},{5,4},{6,5},{7,6},{9,8},{10,9},{11,10},{12... | collective-permute-start | bytes 1597448 | tf_op jit(solution)/shard_map/ppermute | solution.py:65
  35.2 25.9 %collective-permute-start.11 = (bf16[384,1536]{1,0:T(8,128)(2,1)S(1)}, bf16[384,1536]{1,0:T(8,128)(2,1)S(1)}, u32[]{:S(2)}, u32[]{:S(2)}) collective-permute-start(bf16[384,1536]{1,0:T(8,128)(2,1)S(1)} %pad_maximum_fusion.w0.r0), channel_id=1, source_target_pairs={{0,3},{8,56},{4,7},{12,60},{64,67},{72,120},{68,71},{76,124},{16,1... | collective-permute-start | bytes 3538952 | tf_op jit(solution)/shard_map/ppermute | solution.py:51
  48.0 16.3 %collective-permute-start.10 = (bf16[384,1536]{1,0:T(8,128)(2,1)S(1)}, bf16[384,1536]{1,0:T(8,128)(2,1)S(1)}, u32[]{:S(2)}, u32[]{:S(2)}) collective-permute-start(bf16[384,1536]{1,0:T(8,128)(2,1)S(1)} %pad_maximum_fusion.w0.r0), channel_id=1, source_target_pairs={{0,1},{8,24},{4,5},{12,28},{64,65},{72,88},{68,69},{76,92},{16,17}... | collective-permute-start | bytes 3538952 | tf_op jit(solution)/shard_map/ppermute | solution.py:51
  48.7 17.1 %collective-permute-start.12 = (bf16[448,1664]{1,0:T(8,128)(2,1)S(1)}, bf16[448,1664]{1,0:T(8,128)(2,1)S(1)}, u32[]{:S(2)}, u32[]{:S(2)}) collective-permute-start(bf16[448,1664]{1,0:T(8,128)(2,1)S(1)} %get-tuple-element.80.tokens_ref.amine_ref), channel_id=1, source_target_pairs={{0,8},{8,0},{1,9},{9,1},{2,10},{10,2},{3,11},{11,3},{4,12},{12,4},... | collective-permute-start | bytes 4472840 | tf_op jit(solution)/shard_map/ppermute | solution.py:55
  64.3 9.0 %collective-permute-start.14 = (bf16[192,1536]{1,0:T(8,128)(2,1)S(1)}, bf16[192,1536]{1,0:T(8,128)(2,1)S(1)}, u32[]{:S(2)}, u32[]{:S(2)}) collective-permute-start(bf16[192,1536]{1,0:T(8,128)(2,1)S(1)} %slice.89), channel_id=1, source_target_pairs={{0,3},{8,56},{4,7},{12,60},{64,67},{72,120},{68,71},{76,124},{16,1... | collective-permute-start | bytes 1769480 | tf_op jit(solution)/shard_map/ppermute | solution.py:51
  64.4 10.0 %collective-permute-start.13 = (bf16[192,1536]{1,0:T(8,128)(2,1)S(1)}, bf16[192,1536]{1,0:T(8,128)(2,1)S(1)}, u32[]{:S(2)}, u32[]{:S(2)}) collective-permute-start(bf16[192,1536]{1,0:T(8,128)(2,1)S(1)} %slice.88), channel_id=1, source_target_pairs={{0,1},{8,24},{4,5},{12,28},{64,65},{72,88},{68,69},{76,92},{16,17}... | collective-permute-start | bytes 1769480 | tf_op jit(solution)/shard_map/ppermute | solution.py:51
  65.9 17.0 %collective-permute-start.15 = (bf16[288,1664]{1,0:T(8,128)(2,1)S(1)}, bf16[288,1664]{1,0:T(8,128)(2,1)S(1)}, u32[]{:S(2)}, u32[]{:S(2)}) collective-permute-start(bf16[288,1664]{1,0:T(8,128)(2,1)S(1)} %get-tuple-element.90.gmine_ref), channel_id=1, source_target_pairs={{0,8},{8,0},{1,9},{9,1},{2,10},{10,2},{3,11},{11,3},{4,12},{12,4},... | collective-permute-start | bytes 2875400 | tf_op jit(solution)/shard_map/ppermute | solution.py:55
  76.7 6.2 %collective-permute-start.16 = (bf16[384,768]{1,0:T(8,128)(2,1)S(1)}, bf16[384,768]{1,0:T(8,128)(2,1)S(1)}, u32[]{:S(2)}, u32[]{:S(2)}) collective-permute-start(bf16[384,768]{1,0:T(8,128)(2,1)S(1)} %get-tuple-element.93), channel_id=1, source_target_pairs={{0,8},{8,0},{1,9},{9,1},{2,10},{10,2},{3,11},{11,3},{4,12},{12,4},... | collective-permute-start | bytes 1769480 | tf_op jit(solution)/shard_map/ppermute | solution.py:55
  94.0 15.6 %collective-permute-start.17 = (bf16[384,1152]{1,0:T(8,128)(2,1)S(1)}, bf16[384,1152]{1,0:T(8,128)(2,1)S(1)}, u32[]{:S(2)}, u32[]{:S(2)}) collective-permute-start(bf16[384,1152]{1,0:T(8,128)(2,1)S(1)} %get-tuple-element.95), channel_id=1, source_target_pairs={{0,3},{8,56},{4,7},{12,60},{64,67},{72,120},{68,71},{76,124},{16,1... | collective-permute-start | bytes 2654216 | tf_op jit(solution)/shard_map/ppermute | solution.py:51
  94.7 21.4 %collective-permute-start.19 = (bf16[384,1152]{1,0:T(8,128)(2,1)S(1)}, bf16[384,1152]{1,0:T(8,128)(2,1)S(1)}, u32[]{:S(2)}, u32[]{:S(2)}) collective-permute-start(bf16[384,1152]{1,0:T(8,128)(2,1)S(1)} %get-tuple-element.104), channel_id=1, source_target_pairs={{0,2},{8,40},{4,6},{12,44},{64,66},{72,104},{68,70},{76,108},{16,1... | collective-permute-start | bytes 2654216 | tf_op jit(solution)/shard_map/ppermute | solution.py:51
  96.0 21.9 %collective-permute-start.20 = (bf16[384,1152]{1,0:T(8,128)(2,1)S(1)}, bf16[384,1152]{1,0:T(8,128)(2,1)S(1)}, u32[]{:S(2)}, u32[]{:S(2)}) collective-permute-start(bf16[384,1152]{1,0:T(8,128)(2,1)S(1)} %get-tuple-element.105), channel_id=1, source_target_pairs={{0,1},{8,24},{4,5},{12,28},{64,65},{72,88},{68,69},{76,92},{16,17}... | collective-permute-start | bytes 2654216 | tf_op jit(solution)/shard_map/ppermute | solution.py:51
  96.0 6.5 %collective-permute-start.18 = (bf16[256,384]{1,0:T(8,128)(2,1)S(1)}, bf16[256,384]{1,0:T(8,128)(2,1)S(1)}, u32[]{:S(2)}, u32[]{:S(2)}) collective-permute-start(bf16[256,384]{1,0:T(8,128)(2,1)S(1)} %get-tuple-element.96.mine_ref), channel_id=1, source_target_pairs={{0,8},{8,0},{1,9},{9,1},{2,10},{10,2},{3,11},{11,3},{4,12},{12,4},... | collective-permute-start | bytes 589832 | tf_op jit(solution)/shard_map/ppermute | solution.py:55
  106.9 12.0 %collective-permute-start.21 = (bf16[384,384]{1,0:T(8,128)(2,1)S(1)}, bf16[384,384]{1,0:T(8,128)(2,1)S(1)}, u32[]{:S(2)}, u32[]{:S(2)}) collective-permute-start(bf16[384,384]{1,0:T(8,128)(2,1)S(1)} %get-tuple-element.107), channel_id=1, source_target_pairs={{0,3},{8,56},{4,7},{12,60},{64,67},{72,120},{68,71},{76,124},{16,1... | collective-permute-start | bytes 884744 | tf_op jit(solution)/shard_map/ppermute | solution.py:51
  109.1 12.1 %collective-permute-start.22 = (bf16[384,384]{1,0:T(8,128)(2,1)S(1)}, bf16[384,384]{1,0:T(8,128)(2,1)S(1)}, u32[]{:S(2)}, u32[]{:S(2)}) collective-permute-start(bf16[384,384]{1,0:T(8,128)(2,1)S(1)} %get-tuple-element.108), channel_id=1, source_target_pairs={{0,2},{8,40},{4,6},{12,44},{64,66},{72,104},{68,70},{76,108},{16,1... | collective-permute-start | bytes 884744 | tf_op jit(solution)/shard_map/ppermute | solution.py:51
  109.8 14.4 %collective-permute-start.23 = (bf16[384,384]{1,0:T(8,128)(2,1)S(1)}, bf16[384,384]{1,0:T(8,128)(2,1)S(1)}, u32[]{:S(2)}, u32[]{:S(2)}) collective-permute-start(bf16[384,384]{1,0:T(8,128)(2,1)S(1)} %get-tuple-element.109), channel_id=1, source_target_pairs={{0,1},{8,24},{4,5},{12,28},{64,65},{72,88},{68,69},{76,92},{16,17}... | collective-permute-start | bytes 884744 | tf_op jit(solution)/shard_map/ppermute | solution.py:51
  124.6 7.9 %collective-permute-start.24 = (bf16[96,1536]{1,0:T(8,128)(2,1)S(1)}, bf16[96,1536]{1,0:T(8,128)(2,1)S(1)}, u32[]{:S(2)}, u32[]{:S(2)}) collective-permute-start(bf16[96,1536]{1,0:T(8,128)(2,1)S(1)} %get-tuple-element.126), channel_id=1, source_target_pairs={{0,48},{8,76},{4,52},{12,8},{64,112},{72,12},{68,116},{76,72},{16,... | collective-permute-start | bytes 884744 | tf_op jit(solution)/shard_map/ppermute | solution.py:51
  128.8 9.9 %collective-permute-start.26 = (bf16[96,1536]{1,0:T(8,128)(2,1)S(1)}, bf16[96,1536]{1,0:T(8,128)(2,1)S(1)}, u32[]{:S(2)}, u32[]{:S(2)}) collective-permute-start(bf16[96,1536]{1,0:T(8,128)(2,1)S(1)} %get-tuple-element.127), channel_id=1, source_target_pairs={{0,16},{8,12},{4,20},{12,72},{64,80},{72,76},{68,84},{76,8},{16,32... | collective-permute-start | bytes 884744 | tf_op jit(solution)/shard_map/ppermute | solution.py:51
  128.8 9.9 %collective-permute-start.25 = (bf16[96,1536]{1,0:T(8,128)(2,1)S(1)}, bf16[96,1536]{1,0:T(8,128)(2,1)S(1)}, u32[]{:S(2)}, u32[]{:S(2)}) collective-permute-start(bf16[96,1536]{1,0:T(8,128)(2,1)S(1)} %get-tuple-element.128), channel_id=1, source_target_pairs={{0,32},{8,72},{4,36},{12,76},{64,96},{72,8},{68,100},{76,12},{16,4... | collective-permute-start | bytes 884744 | tf_op jit(solution)/shard_map/ppermute | solution.py:51
  141.1 8.0 %collective-permute-start.31 = (f32[128,768]{1,0:T(8,128)S(1)}, f32[128,768]{1,0:T(8,128)S(1)}, u32[]{:S(2)}, u32[]{:S(2)}) collective-permute-start(f32[128,768]{1,0:T(8,128)S(1)} %get-tuple-element.116), channel_id=1, source_target_pairs={{0,8},{8,0},{1,9},{9,1},{2,10},{10,2},{3,11},{11,3},{4,12},{12,4},... | collective-permute-start | bytes 1179656 | tf_op jit(solution)/shard_map/ppermute | solution.py:55
  (13 other events, 86.9 us)

commit v3 on v2

--- a/solution.py
+++ b/solution.py
@@ -189,19 +189,19 @@
 
 def permute_kernel(place_ref, tokens_ref, feature_ref, out):
     def part(n, carry):
-        lanes = pl.ds(pl.multiple_of(n * 256, 256), 256)
-        feature = lax.broadcasted_iota(jnp.int32, (D, 256), 0)
+        lanes = pl.ds(pl.multiple_of(n * 512, 512), 512)
+        feature = lax.broadcasted_iota(jnp.int32, (D, 512), 0)
         order = one_hot(feature == feature_ref[:, lanes])
         out[:, lanes] = jnp.dot(tokens_ref[:, :D], order, preferred_element_type=f32).astype(bf16)
         return carry
 
-    lax.fori_loop(0, D // 256, part, 0)
+    lax.fori_loop(0, D // 512, part, 0)
 
 
 def out_rows_product(row_ref, part, first, chunk):
     row = row_ref[:, part * 384 : (part + 1) * 384]
     row = jnp.where(row < DH, row, row - DH)
-    order = one_hot(lax.broadcasted_iota(jnp.int32, (128, D // 4), 0) + first == row)
+    order = one_hot(lax.broadcasted_iota(jnp.int32, (768, D // 4), 0) + first == row)
     return jnp.dot(order, chunk, preferred_element_type=f32)
 
 
@@ -217,14 +217,14 @@
         halves[i, :, :] = by_half(ref[:, 3 * HALF :])
 
     def part(n, carry):
-        first = pl.multiple_of(n * 128, 128)
+        first = pl.multiple_of(n * 768, 768)
         total = out_rows_product(row_ref, 0, first, halves[0])
         total += out_rows_product(row_ref, 1, first, halves[1])
         total += out_rows_product(row_ref, 3, first, halves[2])
-        sums_out[pl.ds(first, 128), :] = total
+        sums_out[pl.ds(first, 768), :] = total
         return carry
 
-    lax.fori_loop(0, DH // 128, part, 0)
+    lax.fori_loop(0, DH // 768, part, 0)
 
 
 def out_rows_kernel(place_ref, sums_ref, r2_top, r2_low, row_ref, half_out, sent_out, halves):
@@ -233,12 +233,12 @@
     halves[192:, :] = by_half(r2_low[:, 3 * HALF :])
 
     def part(n, carry):
-        first = pl.multiple_of(n * 128, 128)
-        rows = pl.ds(first, 128)
+        first = pl.multiple_of(n * 768, 768)
+        rows = pl.ds(first, 768)
         half_out[rows, :] = (sums_ref[rows, :] + out_rows_product(row_ref, 2, first, halves[...])).astype(bf16)
         return carry
 
-    lax.fori_loop(0, DH // 128, part, 0)
+    lax.fori_loop(0, DH // 768, part, 0)
     sent_out[...] = half_out[pl.ds(pl.multiple_of((1 - core) * HALF, HALF), HALF), :]
 
 
@@ -246,26 +246,19 @@
     core = place_ref[1]
     half = KEY_ROWS // 2 * KEY_COLS
     part = D // 4
-    w2[:192, :] = w2_top[:, : 3 * HALF]
-    w2[192:, :] = w2_low[:, : 3 * HALF]
+    w2[:part, :] = w0[:, : 3 * HALF]
+    w2[part : 2 * part, :] = w1[:, : 3 * HALF]
+    w2[2 * part : 2 * part + 192, :] = w2_top[:, : 3 * HALF]
+    w2[2 * part + 192 : 3 * part, :] = w2_low[:, : 3 * HALF]
+    w2[3 * part :, :] = w3[:, : 3 * HALF]
     for source, side in ((mine_ref, core), (other_ref, 1 - core)):
         own_at = pl.multiple_of((1 - side) * 6 * KEY_COLS, KEY_COLS)
         for r in range(8):
             to = pl.ds(pl.multiple_of((side * 8 + r) * SIDE, SIDE), SIDE)
             hidden[to, :] = source[pl.ds(own_at + r * KEY_COLS, SIDE), :]
 
-        def project(t, carry, source=source, side=side):
-            rows = pl.ds(pl.multiple_of(t * 224, 224), 224)
-            to = pl.ds(pl.multiple_of(side * half + t * 224, 224), 224)
-            total = jnp.dot(source[rows, :part], w0[:, : 3 * HALF], preferred_element_type=f32)
-            for k, ref in ((1, w1), (2, w2), (3, w3)):
-                total += jnp.dot(
-                    source[rows, k * part : (k + 1) * part], ref[:, : 3 * HALF], preferred_element_type=f32
-                )
-            packed[to, :] = total.astype(bf16)
-            return carry
-
-        lax.fori_loop(0, 2, project, 0)
+        to = pl.ds(pl.multiple_of(side * half, half), half)
+        packed[to, :] = jnp.dot(source[...], w2[...], preferred_element_type=f32).astype(bf16)
 
 
 def out_grads_kernel(place_ref, mine_ref, other_ref, grad_ref, row_ref, c0, c1, c2, c3):
@@ -300,9 +293,9 @@
         feature = lax.broadcasted_iota(jnp.int32, (256, D), 0) + first
         order = one_hot(feature == feature_ref[...])
         lanes = pl.ds(first, 256)
-        for side, out in ((core, mine_out), (1 - core, sent_out)):
-            rows = rel[pl.ds(pl.multiple_of(side * 128, 128), 128), :]
-            out[:, lanes] = lax.dot_general(rows, order, contract, preferred_element_type=f32).astype(bf16)
+        both = lax.dot_general(rel[...], order, contract, preferred_element_type=f32)
+        mine_out[:, lanes] = jnp.where(core == 0, both[:128], both[128:]).astype(bf16)
+        sent_out[:, lanes] = jnp.where(core == 0, both[128:], both[:128]).astype(bf16)
         return carry
 
     lax.fori_loop(0, D // 256, part, 0)
@@ -579,7 +572,7 @@
         place,
         [hidden_mine, hidden_other, *weights],
         [((KEY_ROWS * KEY_COLS, 3 * HALF), bf16), ((SIDE * SIDE, D), bf16)],
-        [((D // 4, 3 * HALF), bf16)],
+        [((D, 3 * HALF), bf16)],
     )
 
     attention, grad_packed, *chunks_in, grad_own = layer(

time: 153 us -> 151 us (0.987)
  Pallas kernels: 45.2 us -> 39.3 us
  starting transfers between devices: 55.9 us -> 57.8 us
    pallas_call x13, Pallas kernels: 45.2 us -> 39.3 us  [on_chip(): pl.pallas_call(kernel, out_shape=tuple((jax.ShapeDtypeStruct(shape, kind)...]
    ppermute x22, starting transfers between devices: 41.6 us -> 43.5 us  [shifted(): return lax.ppermute(value, AXES, stage_pairs(axes, shift))]
    ppermute x22, waiting for transfers between devices: 41.5 us -> 43.1 us  [shifted(): return lax.ppermute(value, AXES, stage_pairs(axes, shift))]
  transfers between devices with their start and end apart: 33 -> 33, of which waited for: 17 -> 18; matrix products, arithmetic and copies ran while one was open for 2% -> 2% of each run, Pallas kernels for 22% -> 18%
where the time goes in v3:
time: 151 us; the launch traced here: 150 us
  starting transfers between devices  57.8 us (38%)
  waiting for transfers between devices  43.1 us (29%)
  Pallas kernels  39.3 us (26%)
  local copies, waits for them, and re-layouts  5.35 us (4%)
  other arithmetic  3.53 us (2%)
    ppermute x22, starting transfers between devices, shifted(): return lax.ppermute(value, AXES, stage_pairs(axes, shift))  43.5 us
    ppermute x22, waiting for transfers between devices, shifted(): return lax.ppermute(value, AXES, stage_pairs(axes, shift))  43.1 us
    pallas_call x13, Pallas kernels, on_chip(): pl.pallas_call(kernel, out_shape=tuple((jax.ShapeDtypeStruct(shape, kind)...  39.3 us
    ppermute x8, starting transfers between devices, swap_cores(): return lax.ppermute(value, 'c', [(0, 1), (1, 0)])  7.87 us
    ppermute x2, starting transfers between devices, col_neighbour(): lax.ppermute(value, ('zl', 'x'), [(a, b) for a, b in pairs if 0 <= b < 8])  3.27 us
    ppermute x1, starting transfers between devices, row_neighbour(): lax.ppermute(value, ('zh', 'y', 'c'), [(a, b) for a, b in pairs if 0 <= b...  3.2 us
  transfers between devices with their start and end apart: 33, of which 18 were waited for; matrix products, arithmetic and copies ran while one was open for 2% of the time, Pallas kernels for 18%

profile of v3, /device:TPU:1, one launch (start us, length us, event | category | flops | bytes accessed | tf_op | source)
XLA Modules:
  0.0 150.3 jit_solution(10164842717352414769)
XLA Ops:
  8.6 3.2 %collective-permute-start.4 = (bf16[144,1664]{1,0:T(8,128)(2,1)S(1)}, bf16[144,1664]{1,0:T(8,128)(2,1)S(1)}, u32[]{:S(2)}, u32[]{:S(2)}) collective-permute-start(bf16[144,1664]{1,0:T(8,128)(2,1)S(1)} %get-tuple-element.68), channel_id=1, source_target_pairs={{8,16},{16,8},{24,32},{32,24},{40,48},{48,40},{56,64},{64,56},{72,... | collective-permute-start | bytes 1437704 | tf_op jit(solution)/shard_map/ppermute | solution.py:60
  11.9 2.5 %collective-permute-start.3 = (bf16[24,1536]{1,0:T(8,128)(2,1)S(1)}, bf16[24,1536]{1,0:T(8,128)(2,1)S(1)}, u32[]{:S(2)}, u32[]{:S(2)}) collective-permute-start(bf16[24,1536]{1,0:T(8,128)(2,1)S(1)} %pad_maximum_fusion.3), channel_id=1, source_target_pairs={{0,68},{8,11},{4,0},{12,15},{64,4},{72,75},{68,64},{76,79},{16,84}... | collective-permute-start | bytes 221192 | tf_op jit(solution)/shard_map/ppermute | solution.py:51
  15.8 3.4 %collective-permute-done.2 = bf16[24,1536]{1,0:T(8,128)(2,1)S(1)} collective-permute-done((bf16[24,1536]{1,0:T(8,128)(2,1)S(1)}, bf16[24,1536]{1,0:T(8,128)(2,1)S(1)}, u32[]{:S(2)}, u32[]{:S(2)}) %collective-permute-start.2) | collective-permute-done | bytes 73760 | tf_op jit(solution)/shard_map/ppermute | solution.py:51
  20.7 4.1 %collective-permute-start.9 = (bf16[96,1536]{1,0:T(8,128)(2,1)S(1)}, bf16[96,1536]{1,0:T(8,128)(2,1)S(1)}, u32[]{:S(2)}, u32[]{:S(2)}) collective-permute-start(bf16[96,1536]{1,0:T(8,128)(2,1)S(1)} %pad_maximum_fusion.2), channel_id=1, source_target_pairs={{0,48},{8,76},{4,52},{12,8},{64,112},{72,12},{68,116},{76,72},{16,... | collective-permute-start | bytes 884744 | tf_op jit(solution)/shard_map/ppermute | solution.py:51
  28.9 2.8 %collective-permute-done.9 = bf16[96,1536]{1,0:T(8,128)(2,1)S(1)} collective-permute-done((bf16[96,1536]{1,0:T(8,128)(2,1)S(1)}, bf16[96,1536]{1,0:T(8,128)(2,1)S(1)}, u32[]{:S(2)}, u32[]{:S(2)}) %collective-permute-start.9) | collective-permute-done | bytes 294944 | tf_op jit(solution)/shard_map/ppermute | solution.py:51
  32.1 3.1 %collective-permute-done.7 = bf16[96,1536]{1,0:T(8,128)(2,1)S(1)} collective-permute-done((bf16[96,1536]{1,0:T(8,128)(2,1)S(1)}, bf16[96,1536]{1,0:T(8,128)(2,1)S(1)}, u32[]{:S(2)}, u32[]{:S(2)}) %collective-permute-start.7) | collective-permute-done | bytes 294944 | tf_op jit(solution)/shard_map/ppermute | solution.py:51
  35.2 12.8 %collective-permute-start.11 = (bf16[384,1536]{1,0:T(8,128)(2,1)S(1)}, bf16[384,1536]{1,0:T(8,128)(2,1)S(1)}, u32[]{:S(2)}, u32[]{:S(2)}) collective-permute-start(bf16[384,1536]{1,0:T(8,128)(2,1)S(1)} %pad_maximum_fusion.w0.r0), channel_id=1, source_target_pairs={{0,3},{8,56},{4,7},{12,60},{64,67},{72,120},{68,71},{76,124},{16,1... | collective-permute-start | bytes 3538952 | tf_op jit(solution)/shard_map/ppermute | solution.py:51
  48.8 3.2 %shard_map.87.mine_ref = bf16[448,1536]{1,0:T(8,128)(2,1)S(1)} custom-call(s32[3]{0:T(128)S(1)} %pad_add_fusion.place_ref, bf16[448,1664]{1,0:T(8,128)(2,1)S(1)} %get-tuple-element.80.tokens_ref.amine_ref, s32[1,1536]{1,0:T(1,128)S(1)} %get-tuple-element.81.feature_ref), custom_call_target="tpu_custom_call" | custom-call | flops 1000 | bytes 1000 | tf_op jit(solution)/shard_map/pallas_call | solution.py:104
  52.0 9.1 %collective-permute-done.11.w3.r3 = bf16[384,1536]{1,0:T(8,128)(2,1)S(1)} collective-permute-done((bf16[384,1536]{1,0:T(8,128)(2,1)S(1)}, bf16[384,1536]{1,0:T(8,128)(2,1)S(1)}, u32[]{:S(2)}, u32[]{:S(2)}) %collective-permute-start.11) | collective-permute-done | bytes 1179680 | tf_op jit(solution)/shard_map/ppermute | solution.py:51
  61.1 3.1 %collective-permute-done.10.w1.r1 = bf16[384,1536]{1,0:T(8,128)(2,1)S(1)} collective-permute-done((bf16[384,1536]{1,0:T(8,128)(2,1)S(1)}, bf16[384,1536]{1,0:T(8,128)(2,1)S(1)}, u32[]{:S(2)}, u32[]{:S(2)}) %collective-permute-start.10) | collective-permute-done | bytes 1179680 | tf_op jit(solution)/shard_map/ppermute | solution.py:51
  65.9 3.2 %shard_map.88.other_ref = bf16[448,1536]{1,0:T(8,128)(2,1)S(1)} custom-call(s32[3]{0:T(128)S(1)} %pad_add_fusion.place_ref, bf16[448,1664]{1,0:T(8,128)(2,1)S(1)} %collective-permute-done.12.tokens_ref.aother_ref, s32[1,1536]{1,0:T(1,128)S(1)} %get-tuple-element.81.feature_ref), custom_call_target="tpu_custom_call" | custom-call | flops 1000 | bytes 1000 | tf_op jit(solution)/shard_map/pallas_call | solution.py:104
  69.1 2.6 %shard_map.90.sums_ref = f32[768,768]{1,0:T(8,128)S(1)} custom-call(s32[3]{0:T(128)S(1)} %pad_add_fusion.place_ref, bf16[384,1536]{1,0:T(8,128)(2,1)S(1)} %pad_maximum_fusion.w0.r0, bf16[384,1536]{1,0:T(8,128)(2,1)S(1)} %collective-permute-done.10.w1.r1, bf16[384,1536]{1,0:T(8,128)(2,1)S(1)} %collective-permute-done.11.w3.r3, ...), custom_call_target="tpu_custom_call" | custom-call | flops 1000 | bytes 1000 | tf_op jit(solution)/shard_map/pallas_call | solution.py:104
  76.1 4.4 %shard_map.89 = (bf16[896,1152]{1,0:T(8,128)(2,1)S(1)}, bf16[256,1536]{1,0:T(8,128)(2,1)S(1)}) custom-call(s32[3]{0:T(128)S(1)} %pad_add_fusion.place_ref, bf16[448,1536]{1,0:T(8,128)(2,1)S(1)} %shard_map.87.mine_ref, bf16[448,1536]{1,0:T(8,128)(2,1)S(1)} %shard_map.88.other_ref, bf16[384,1536]{1,0:T(8,128)(2,1)S(1)} %pad_maximum_fusion.w0.r0, ...), custom_call_target="tpu_custom_call" | custom-call | flops 1000 | bytes 1000 | tf_op jit(solution)/shard_map/pallas_call | solution.py:104
  80.5 11.1 %shard_map.92 = (bf16[256,384]{1,0:T(8,128)(2,1)S(1)}, bf16[256,1152]{1,0:T(8,128)(2,1)S(1)}, bf16[384,1152]{1,0:T(8,128)(2,1)S(1)}, bf16[384,1152]{1,0:T(8,128)...) custom-call(s32[3]{0:T(128)S(1)} %pad_add_fusion.place_ref, ...), custom_call_target="tpu_custom_call" | custom-call | flops 1000 | bytes 1000 | tf_op jit(solution)/shard_map/pallas_call | solution.py:104
  94.2 4.5 %shard_map.93 = (bf16[128,1536]{1,0:T(8,128)(2,1)S(1)}, bf16[128,1536]{1,0:T(8,128)(2,1)S(1)}) custom-call(s32[3]{0:T(128)S(1)} %pad_add_fusion.place_ref, bf16[256,1152]{1,0:T(8,128)(2,1)S(1)} %get-tuple-element.97.grads_ref, bf16[384,1536]{1,0:T(8,128)(2,1)S(1)} %pad_maximum_fusion.w0.r0, bf16[384,1536]{1,0:T(8,128)(2,1)S(1)} %collective-permute-done.10.w1.r1, ...), custom_call_target="tpu_custom_call" | custom-call | flops 1000 | bytes 1000 | tf_op jit(solution)/shard_map/pallas_call | solution.py:104
  99.8 3.3 %shard_map.94 = (bf16[384,384]{1,0:T(8,128)(2,1)S(1)}, bf16[384,384]{1,0:T(8,128)(2,1)S(1)}, bf16[384,384]{1,0:T(8,128)(2,1)S(1)}, bf16[384,384]{1,0:T(8,128)(2,1)S(1)}) custom-call(s32[3]{0:T(128)S(1)} %pad_add_fusion.place_ref, bf16[256,384]{1,0:T(8,128)(2,1)S(1)} %get-tuple-element.96.mine_ref, bf16[256,384]{1,0:T(8,128)(2,1)S(1)} %collective-permute-done.18.other_ref, ...), custom_call_target="tpu_custom_call" | custom-call | flops 1000 | bytes 1000 | tf_op jit(solution)/shard_map/pallas_call | solution.py:104
  103.1 2.2 %collective-permute-start.21 = (bf16[384,384]{1,0:T(8,128)(2,1)S(1)}, bf16[384,384]{1,0:T(8,128)(2,1)S(1)}, u32[]{:S(2)}, u32[]{:S(2)}) collective-permute-start(bf16[384,384]{1,0:T(8,128)(2,1)S(1)} %get-tuple-element.107), channel_id=1, source_target_pairs={{0,3},{8,56},{4,7},{12,60},{64,67},{72,120},{68,71},{76,124},{16,1... | collective-permute-start | bytes 884744 | tf_op jit(solution)/shard_map/ppermute | solution.py:51
  106.0 7.7 %collective-permute-start.23 = (bf16[384,384]{1,0:T(8,128)(2,1)S(1)}, bf16[384,384]{1,0:T(8,128)(2,1)S(1)}, u32[]{:S(2)}, u32[]{:S(2)}) collective-permute-start(bf16[384,384]{1,0:T(8,128)(2,1)S(1)} %get-tuple-element.109), channel_id=1, source_target_pairs={{0,1},{8,24},{4,5},{12,28},{64,65},{72,88},{68,69},{76,92},{16,17}... | collective-permute-start | bytes 884744 | tf_op jit(solution)/shard_map/ppermute | solution.py:51
  118.2 3.1 %collective-permute-done.23 = bf16[384,384]{1,0:T(8,128)(2,1)S(1)} collective-permute-done((bf16[384,384]{1,0:T(8,128)(2,1)S(1)}, bf16[384,384]{1,0:T(8,128)(2,1)S(1)}, u32[]{:S(2)}, u32[]{:S(2)}) %collective-permute-start.23) | collective-permute-done | bytes 294944 | tf_op jit(solution)/shard_map/ppermute | solution.py:51
  121.6 4.8 %collective-permute-start.24 = (bf16[96,1536]{1,0:T(8,128)(2,1)S(1)}, bf16[96,1536]{1,0:T(8,128)(2,1)S(1)}, u32[]{:S(2)}, u32[]{:S(2)}) collective-permute-start(bf16[96,1536]{1,0:T(8,128)(2,1)S(1)} %get-tuple-element.126), channel_id=1, source_target_pairs={{0,48},{8,76},{4,52},{12,8},{64,112},{72,12},{68,116},{76,72},{16,... | collective-permute-start | bytes 884744 | tf_op jit(solution)/shard_map/ppermute | solution.py:51
  127.6 2.4 %collective-permute-done.24 = bf16[96,1536]{1,0:T(8,128)(2,1)S(1)} collective-permute-done((bf16[96,1536]{1,0:T(8,128)(2,1)S(1)}, bf16[96,1536]{1,0:T(8,128)(2,1)S(1)}, u32[]{:S(2)}, u32[]{:S(2)}) %collective-permute-start.24) | collective-permute-done | bytes 294944 | tf_op jit(solution)/shard_map/ppermute | solution.py:51
  130.0 6.3 %collective-permute-done.26 = bf16[96,1536]{1,0:T(8,128)(2,1)S(1)} collective-permute-done((bf16[96,1536]{1,0:T(8,128)(2,1)S(1)}, bf16[96,1536]{1,0:T(8,128)(2,1)S(1)}, u32[]{:S(2)}, u32[]{:S(2)}) %collective-permute-start.26) | collective-permute-done | bytes 294944 | tf_op jit(solution)/shard_map/ppermute | solution.py:51
  138.7 2.3 %collective-permute-start.31 = (f32[128,768]{1,0:T(8,128)S(1)}, f32[128,768]{1,0:T(8,128)S(1)}, u32[]{:S(2)}, u32[]{:S(2)}) collective-permute-start(f32[128,768]{1,0:T(8,128)S(1)} %get-tuple-element.116), channel_id=1, source_target_pairs={{0,8},{8,0},{1,9},{9,1},{2,10},{10,2},{3,11},{11,3},{4,12},{12,4},... | collective-permute-start | bytes 1179656 | tf_op jit(solution)/shard_map/ppermute | solution.py:55
  143.5 3.1 %collective-permute-start.30 = (f32[12,1536]{1,0:T(8,128)}, f32[12,1536]{1,0:T(8,128)S(1)}, u32[]{:S(2)}, u32[]{:S(2)}) collective-permute-start(f32[12,1536]{1,0:T(8,128)} %get-tuple-element.133), channel_id=1, source_target_pairs={{0,8},{8,0},{1,9},{9,1},{2,10},{10,2},{3,11},{11,3},{4,12},{12,4},... | collective-permute-start | bytes 221192 | tf_op jit(solution)/shard_map/ppermute | solution.py:55
  (123 shorter events, 40.9 us)
Async XLA Ops:
  2.8 5.7 %collective-permute-start = (bf16[12,1536]{1,0:T(8,128)(2,1)S(1)}, bf16[12,1536]{1,0:T(8,128)(2,1)S(1)}, u32[]{:S(2)}, u32[]{:S(2)}) collective-permute-start(bf16[12,1536]{1,0:T(8,128)(2,1)S(1)} %get-tuple-element.135), channel_id=1, source_target_pairs={{0,8},{8,0},{1,9},{9,1},{2,10},{10,2},{3,11},{11,3},{4,12},{12,4},... | collective-permute-start | bytes 110600 | tf_op jit(solution)/shard_map/ppermute | solution.py:55
  8.6 11.3 %collective-permute-start.4 = (bf16[144,1664]{1,0:T(8,128)(2,1)S(1)}, bf16[144,1664]{1,0:T(8,128)(2,1)S(1)}, u32[]{:S(2)}, u32[]{:S(2)}) collective-permute-start(bf16[144,1664]{1,0:T(8,128)(2,1)S(1)} %get-tuple-element.68), channel_id=1, source_target_pairs={{8,16},{16,8},{24,32},{32,24},{40,48},{48,40},{56,64},{64,56},{72,... | collective-permute-start | bytes 1437704 | tf_op jit(solution)/shard_map/ppermute | solution.py:60
  20.7 10.9 %collective-permute-start.9 = (bf16[96,1536]{1,0:T(8,128)(2,1)S(1)}, bf16[96,1536]{1,0:T(8,128)(2,1)S(1)}, u32[]{:S(2)}, u32[]{:S(2)}) collective-permute-start(bf16[96,1536]{1,0:T(8,128)(2,1)S(1)} %pad_maximum_fusion.2), channel_id=1, source_target_pairs={{0,48},{8,76},{4,52},{12,8},{64,112},{72,12},{68,116},{76,72},{16,... | collective-permute-start | bytes 884744 | tf_op jit(solution)/shard_map/ppermute | solution.py:51
  24.9 7.2 %collective-permute-start.8 = (bf16[96,1536]{1,0:T(8,128)(2,1)S(1)}, bf16[96,1536]{1,0:T(8,128)(2,1)S(1)}, u32[]{:S(2)}, u32[]{:S(2)}) collective-permute-start(bf16[96,1536]{1,0:T(8,128)(2,1)S(1)} %pad_maximum_fusion.2), channel_id=1, source_target_pairs={{0,32},{8,72},{4,36},{12,76},{64,96},{72,8},{68,100},{76,12},{16,4... | collective-permute-start | bytes 884744 | tf_op jit(solution)/shard_map/ppermute | solution.py:51
  24.9 10.2 %collective-permute-start.7 = (bf16[96,1536]{1,0:T(8,128)(2,1)S(1)}, bf16[96,1536]{1,0:T(8,128)(2,1)S(1)}, u32[]{:S(2)}, u32[]{:S(2)}) collective-permute-start(bf16[96,1536]{1,0:T(8,128)(2,1)S(1)} %pad_maximum_fusion.2), channel_id=1, source_target_pairs={{0,16},{8,12},{4,20},{12,72},{64,80},{72,76},{68,84},{76,8},{16,32... | collective-permute-start | bytes 884744 | tf_op jit(solution)/shard_map/ppermute | solution.py:51
  25.6 22.4 %collective-permute-start.5 = (bf16[160,1664]{1,0:T(8,128)(2,1)S(1)}, bf16[160,1664]{1,0:T(8,128)(2,1)S(1)}, u32[]{:S(2)}, u32[]{:S(2)}) collective-permute-start(bf16[160,1664]{1,0:T(8,128)(2,1)S(1)} %get-tuple-element.78), channel_id=1, source_target_pairs={{0,1},{1,2},{2,3},{3,4},{4,5},{5,6},{6,7},{8,9},{9,10},{10,11},{11... | collective-permute-start | bytes 1597448 | tf_op jit(solution)/shard_map/ppermute | solution.py:65
  27.6 20.4 %collective-permute-start.6 = (bf16[160,1664]{1,0:T(8,128)(2,1)S(1)}, bf16[160,1664]{1,0:T(8,128)(2,1)S(1)}, u32[]{:S(2)}, u32[]{:S(2)}) collective-permute-start(bf16[160,1664]{1,0:T(8,128)(2,1)S(1)} %get-tuple-element.79), channel_id=1, source_target_pairs={{1,0},{2,1},{3,2},{4,3},{5,4},{6,5},{7,6},{9,8},{10,9},{11,10},{12... | collective-permute-start | bytes 1597448 | tf_op jit(solution)/shard_map/ppermute | solution.py:65
  35.2 25.9 %collective-permute-start.11 = (bf16[384,1536]{1,0:T(8,128)(2,1)S(1)}, bf16[384,1536]{1,0:T(8,128)(2,1)S(1)}, u32[]{:S(2)}, u32[]{:S(2)}) collective-permute-start(bf16[384,1536]{1,0:T(8,128)(2,1)S(1)} %pad_maximum_fusion.w0.r0), channel_id=1, source_target_pairs={{0,3},{8,56},{4,7},{12,60},{64,67},{72,120},{68,71},{76,124},{16,1... | collective-permute-start | bytes 3538952 | tf_op jit(solution)/shard_map/ppermute | solution.py:51
  48.0 16.3 %collective-permute-start.10 = (bf16[384,1536]{1,0:T(8,128)(2,1)S(1)}, bf16[384,1536]{1,0:T(8,128)(2,1)S(1)}, u32[]{:S(2)}, u32[]{:S(2)}) collective-permute-start(bf16[384,1536]{1,0:T(8,128)(2,1)S(1)} %pad_maximum_fusion.w0.r0), channel_id=1, source_target_pairs={{0,1},{8,24},{4,5},{12,28},{64,65},{72,88},{68,69},{76,92},{16,17}... | collective-permute-start | bytes 3538952 | tf_op jit(solution)/shard_map/ppermute | solution.py:51
  48.7 17.1 %collective-permute-start.12 = (bf16[448,1664]{1,0:T(8,128)(2,1)S(1)}, bf16[448,1664]{1,0:T(8,128)(2,1)S(1)}, u32[]{:S(2)}, u32[]{:S(2)}) collective-permute-start(bf16[448,1664]{1,0:T(8,128)(2,1)S(1)} %get-tuple-element.80.tokens_ref.amine_ref), channel_id=1, source_target_pairs={{0,8},{8,0},{1,9},{9,1},{2,10},{10,2},{3,11},{11,3},{4,12},{12,4},... | collective-permute-start | bytes 4472840 | tf_op jit(solution)/shard_map/ppermute | solution.py:55
  64.3 8.8 %collective-permute-start.14 = (bf16[192,1536]{1,0:T(8,128)(2,1)S(1)}, bf16[192,1536]{1,0:T(8,128)(2,1)S(1)}, u32[]{:S(2)}, u32[]{:S(2)}) collective-permute-start(bf16[192,1536]{1,0:T(8,128)(2,1)S(1)} %slice.89), channel_id=1, source_target_pairs={{0,3},{8,56},{4,7},{12,60},{64,67},{72,120},{68,71},{76,124},{16,1... | collective-permute-start | bytes 1769480 | tf_op jit(solution)/shard_map/ppermute | solution.py:51
  64.4 10.0 %collective-permute-start.13 = (bf16[192,1536]{1,0:T(8,128)(2,1)S(1)}, bf16[192,1536]{1,0:T(8,128)(2,1)S(1)}, u32[]{:S(2)}, u32[]{:S(2)}) collective-permute-start(bf16[192,1536]{1,0:T(8,128)(2,1)S(1)} %slice.88), channel_id=1, source_target_pairs={{0,1},{8,24},{4,5},{12,28},{64,65},{72,88},{68,69},{76,92},{16,17}... | collective-permute-start | bytes 1769480 | tf_op jit(solution)/shard_map/ppermute | solution.py:51
  65.9 14.6 %collective-permute-start.15 = (bf16[288,1664]{1,0:T(8,128)(2,1)S(1)}, bf16[288,1664]{1,0:T(8,128)(2,1)S(1)}, u32[]{:S(2)}, u32[]{:S(2)}) collective-permute-start(bf16[288,1664]{1,0:T(8,128)(2,1)S(1)} %get-tuple-element.90.gmine_ref), channel_id=1, source_target_pairs={{0,8},{8,0},{1,9},{9,1},{2,10},{10,2},{3,11},{11,3},{4,12},{12,4},... | collective-permute-start | bytes 2875400 | tf_op jit(solution)/shard_map/ppermute | solution.py:55
  91.6 14.3 %collective-permute-start.17 = (bf16[384,1152]{1,0:T(8,128)(2,1)S(1)}, bf16[384,1152]{1,0:T(8,128)(2,1)S(1)}, u32[]{:S(2)}, u32[]{:S(2)}) collective-permute-start(bf16[384,1152]{1,0:T(8,128)(2,1)S(1)} %get-tuple-element.95), channel_id=1, source_target_pairs={{0,3},{8,56},{4,7},{12,60},{64,67},{72,120},{68,71},{76,124},{16,1... | collective-permute-start | bytes 2654216 | tf_op jit(solution)/shard_map/ppermute | solution.py:51
  91.7 22.1 %collective-permute-start.19 = (bf16[384,1152]{1,0:T(8,128)(2,1)S(1)}, bf16[384,1152]{1,0:T(8,128)(2,1)S(1)}, u32[]{:S(2)}, u32[]{:S(2)}) collective-permute-start(bf16[384,1152]{1,0:T(8,128)(2,1)S(1)} %get-tuple-element.104), channel_id=1, source_target_pairs={{0,2},{8,40},{4,6},{12,44},{64,66},{72,104},{68,70},{76,108},{16,1... | collective-permute-start | bytes 2654216 | tf_op jit(solution)/shard_map/ppermute | solution.py:51
  93.6 21.3 %collective-permute-start.20 = (bf16[384,1152]{1,0:T(8,128)(2,1)S(1)}, bf16[384,1152]{1,0:T(8,128)(2,1)S(1)}, u32[]{:S(2)}, u32[]{:S(2)}) collective-permute-start(bf16[384,1152]{1,0:T(8,128)(2,1)S(1)} %get-tuple-element.105), channel_id=1, source_target_pairs={{0,1},{8,24},{4,5},{12,28},{64,65},{72,88},{68,69},{76,92},{16,17}... | collective-permute-start | bytes 2654216 | tf_op jit(solution)/shard_map/ppermute | solution.py:51
  103.1 13.4 %collective-permute-start.21 = (bf16[384,384]{1,0:T(8,128)(2,1)S(1)}, bf16[384,384]{1,0:T(8,128)(2,1)S(1)}, u32[]{:S(2)}, u32[]{:S(2)}) collective-permute-start(bf16[384,384]{1,0:T(8,128)(2,1)S(1)} %get-tuple-element.107), channel_id=1, source_target_pairs={{0,3},{8,56},{4,7},{12,60},{64,67},{72,120},{68,71},{76,124},{16,1... | collective-permute-start | bytes 884744 | tf_op jit(solution)/shard_map/ppermute | solution.py:51
  105.3 12.8 %collective-permute-start.22 = (bf16[384,384]{1,0:T(8,128)(2,1)S(1)}, bf16[384,384]{1,0:T(8,128)(2,1)S(1)}, u32[]{:S(2)}, u32[]{:S(2)}) collective-permute-start(bf16[384,384]{1,0:T(8,128)(2,1)S(1)} %get-tuple-element.108), channel_id=1, source_target_pairs={{0,2},{8,40},{4,6},{12,44},{64,66},{72,104},{68,70},{76,108},{16,1... | collective-permute-start | bytes 884744 | tf_op jit(solution)/shard_map/ppermute | solution.py:51
  106.0 15.2 %collective-permute-start.23 = (bf16[384,384]{1,0:T(8,128)(2,1)S(1)}, bf16[384,384]{1,0:T(8,128)(2,1)S(1)}, u32[]{:S(2)}, u32[]{:S(2)}) collective-permute-start(bf16[384,384]{1,0:T(8,128)(2,1)S(1)} %get-tuple-element.109), channel_id=1, source_target_pairs={{0,1},{8,24},{4,5},{12,28},{64,65},{72,88},{68,69},{76,92},{16,17}... | collective-permute-start | bytes 884744 | tf_op jit(solution)/shard_map/ppermute | solution.py:51
  121.6 8.4 %collective-permute-start.24 = (bf16[96,1536]{1,0:T(8,128)(2,1)S(1)}, bf16[96,1536]{1,0:T(8,128)(2,1)S(1)}, u32[]{:S(2)}, u32[]{:S(2)}) collective-permute-start(bf16[96,1536]{1,0:T(8,128)(2,1)S(1)} %get-tuple-element.126), channel_id=1, source_target_pairs={{0,48},{8,76},{4,52},{12,8},{64,112},{72,12},{68,116},{76,72},{16,... | collective-permute-start | bytes 884744 | tf_op jit(solution)/shard_map/ppermute | solution.py:51
  126.3 9.9 %collective-permute-start.26 = (bf16[96,1536]{1,0:T(8,128)(2,1)S(1)}, bf16[96,1536]{1,0:T(8,128)(2,1)S(1)}, u32[]{:S(2)}, u32[]{:S(2)}) collective-permute-start(bf16[96,1536]{1,0:T(8,128)(2,1)S(1)} %get-tuple-element.127), channel_id=1, source_target_pairs={{0,16},{8,12},{4,20},{12,72},{64,80},{72,76},{68,84},{76,8},{16,32... | collective-permute-start | bytes 884744 | tf_op jit(solution)/shard_map/ppermute | solution.py:51
  126.3 9.9 %collective-permute-start.25 = (bf16[96,1536]{1,0:T(8,128)(2,1)S(1)}, bf16[96,1536]{1,0:T(8,128)(2,1)S(1)}, u32[]{:S(2)}, u32[]{:S(2)}) collective-permute-start(bf16[96,1536]{1,0:T(8,128)(2,1)S(1)} %get-tuple-element.128), channel_id=1, source_target_pairs={{0,32},{8,72},{4,36},{12,76},{64,96},{72,8},{68,100},{76,12},{16,4... | collective-permute-start | bytes 884744 | tf_op jit(solution)/shard_map/ppermute | solution.py:51
  138.7 8.0 %collective-permute-start.31 = (f32[128,768]{1,0:T(8,128)S(1)}, f32[128,768]{1,0:T(8,128)S(1)}, u32[]{:S(2)}, u32[]{:S(2)}) collective-permute-start(f32[128,768]{1,0:T(8,128)S(1)} %get-tuple-element.116), channel_id=1, source_target_pairs={{0,8},{8,0},{1,9},{9,1},{2,10},{10,2},{3,11},{11,3},{4,12},{12,4},... | collective-permute-start | bytes 1179656 | tf_op jit(solution)/shard_map/ppermute | solution.py:55
  141.0 5.7 %collective-permute-start.32 = (bf16[128,1536]{1,0:T(8,128)(2,1)S(1)}, bf16[128,1536]{1,0:T(8,128)(2,1)S(1)}, u32[]{:S(2)}, u32[]{:S(2)}) collective-permute-start(bf16[128,1536]{1,0:T(8,128)(2,1)S(1)} %get-tuple-element.118), channel_id=1, source_target_pairs={{0,8},{8,0},{1,9},{9,1},{2,10},{10,2},{3,11},{11,3},{4,12},{12,4},... | collective-permute-start | bytes 1179656 | tf_op jit(solution)/shard_map/ppermute | solution.py:55
  (13 other events, 85.2 us)

commit v4 on v3

--- a/solution.py
+++ b/solution.py
@@ -299,6 +299,31 @@
         return carry
 
     lax.fori_loop(0, D // 256, part, 0)
+
+
+def last_sum_kernel(place_ref, own_ref, near_ref, far_ref, back_ref, kept_out, sent_out):
+    first = place_ref[1] == 0
+    total = (own_ref[...].astype(f32) + near_ref[...].astype(f32)) + (
+        far_ref[...].astype(f32) + back_ref[...].astype(f32)
+    )
+    left, right = total[:, : 3 * HALF], total[:, 3 * HALF :]
+    lefts = (left[:12], left[12:])
+    rights = [jnp.concatenate([right[6 * i : 6 * i + 6], right[12 + 6 * i : 18 + 6 * i]], axis=0) for i in range(2)]
+    for out, mine in ((kept_out, first), (sent_out, jnp.logical_not(first))):
+        out[:, : 3 * HALF] = jnp.where(mine, lefts[0], lefts[1])
+        out[:, 3 * HALF :] = jnp.where(mine, rights[0], rights[1])
+
+
+def unpack_kernel(place_ref, kept_ref, got_ref, in_out, out_out):
+    first = place_ref[1] == 0
+    kept, got = kept_ref[...], got_ref[...]
+    for half, value in enumerate((jnp.where(first, kept, got), jnp.where(first, got, kept))):
+        for t in range(3):
+            lanes = slice(t * DH + half * HALF, t * DH + half * HALF + HALF)
+            in_out[:, lanes] = value[:, t * HALF : (t + 1) * HALF]
+        for h in range(2):
+            lanes = slice(half * DH + h * HALF, half * DH + h * HALF + HALF)
+            out_out[:, lanes] = value[6 * h : 6 * h + 6, 3 * HALF :]
 
 
 def project_kernel(place_ref, mine_ref, other_ref, half_ref, mine_out, sent_out):
@@ -615,20 +640,15 @@
         [flat_tiles, flat_grad, live, projected, swap_cores(projected_sent), hidden_kept, swap_cores(hidden_sent)],
         [((tokens, D), bf16)] * 2,
     )
-    total = scatter_stage([total[k * 24 : (k + 1) * 24] for k in range(4)], 0)
-
-    sums_in = total[:, : 3 * HALF].reshape(2, 12, 3 * HALF)
-    sums_out = total[:, 3 * HALF :].reshape(2, 2, 6, HALF).transpose(1, 0, 2, 3).reshape(2, 12, HALF)
-    sums = jnp.concatenate([sums_in, sums_out], axis=2)
-    kept = jnp.where(core == 0, sums[0], sums[1])
-    gotten = swap_cores(jnp.where(core == 0, sums[1], sums[0]))
+    axes = (STAGES[0][0], STAGES[1][0])
+    own, to_near, to_far, to_back = [total[k * 24 : (k + 1) * 24] for k in range(4)]
+    parts = [own, shifted(to_near, axes, 3), shifted(to_far, axes, 2), shifted(to_back, axes, 1)]
+    kept, sent = on_chip(last_sum_kernel, place, parts, [((12, D), f32)] * 2)
+    gotten = swap_cores(sent)
     gotten, layer_out, grad_tiles = lax.optimization_barrier((gotten, layer_out, grad_tiles))
-    grad_project_in = by_core(
-        core, kept[:, : 3 * HALF].reshape(12, 3, 1, HALF), gotten[:, : 3 * HALF].reshape(12, 3, 1, HALF), 2
-    ).reshape(12, 3 * DH)
-    kept_out = kept[:, 3 * HALF :].reshape(2, 6, HALF).transpose(1, 0, 2).reshape(6, DH)
-    gotten_out = gotten[:, 3 * HALF :].reshape(2, 6, HALF).transpose(1, 0, 2).reshape(6, DH)
-    grad_project_out = by_core(core, kept_out, gotten_out, 1)
+    grad_project_in, grad_project_out = on_chip(
+        unpack_kernel, place, [kept, gotten], [((12, 3 * DH), f32), ((6, D), f32)]
+    )
 
     return (
         layer_out.reshape(8, SIDE, D),

time: 151 us -> 150 us (level)
  Pallas kernels: 39.3 us -> 41.1 us
  starting transfers between devices: 57.8 us -> 56.1 us
    ppermute x8, starting transfers between devices: 7.87 us -> 5.69 us  [swap_cores(): return lax.ppermute(value, 'c', [(0, 1), (1, 0)])]
    pallas_call x13 -> x15, Pallas kernels: 39.3 us -> 41.1 us  [on_chip(): pl.pallas_call(kernel, out_shape=tuple((jax.ShapeDtypeStruct(shape, kind)...]
  transfers between devices with their start and end apart: 33 -> 33, of which waited for: 18 -> 18; matrix products, arithmetic and copies ran while one was open for 2% -> 1% of each run, Pallas kernels for 18% -> 19%
where the time goes in v4:
time: 150 us; the launch traced here: 149 us
  starting transfers between devices  56.1 us (37%)
  waiting for transfers between devices  44.3 us (30%)
  Pallas kernels  41.1 us (27%)
  local copies, waits for them, and re-layouts  4.4 us (3%)
  other arithmetic  2.16 us (1%)
    ppermute x22, waiting for transfers between devices, shifted(): return lax.ppermute(value, AXES, stage_pairs(axes, shift))  44.3 us
    ppermute x22, starting transfers between devices, shifted(): return lax.ppermute(value, AXES, stage_pairs(axes, shift))  44 us
    pallas_call x15, Pallas kernels, on_chip(): pl.pallas_call(kernel, out_shape=tuple((jax.ShapeDtypeStruct(shape, kind)...  41.1 us
    ppermute x8, starting transfers between devices, swap_cores(): return lax.ppermute(value, 'c', [(0, 1), (1, 0)])  5.69 us
    ppermute x2, starting transfers between devices, col_neighbour(): lax.ppermute(value, ('zl', 'x'), [(a, b) for a, b in pairs if 0 <= b < 8])  3.27 us
    ppermute x1, starting transfers between devices, row_neighbour(): lax.ppermute(value, ('zh', 'y', 'c'), [(a, b) for a, b in pairs if 0 <= b...  3.2 us
  transfers between devices with their start and end apart: 33, of which 18 were waited for; matrix products, arithmetic and copies ran while one was open for 1% of the time, Pallas kernels for 19%

profile of v4, /device:TPU:1, one launch (start us, length us, event | category | flops | bytes accessed | tf_op | source)
XLA Modules:
  0.0 149.3 jit_solution(15500475619016744728)
XLA Ops:
  8.6 3.2 %collective-permute-start.4 = (bf16[144,1664]{1,0:T(8,128)(2,1)S(1)}, bf16[144,1664]{1,0:T(8,128)(2,1)S(1)}, u32[]{:S(2)}, u32[]{:S(2)}) collective-permute-start(bf16[144,1664]{1,0:T(8,128)(2,1)S(1)} %get-tuple-element.72), channel_id=1, source_target_pairs={{8,16},{16,8},{24,32},{32,24},{40,48},{48,40},{56,64},{64,56},{72,... | collective-permute-start | bytes 1437704 | tf_op jit(solution)/shard_map/ppermute | solution.py:60
  11.9 2.5 %collective-permute-start.3 = (bf16[24,1536]{1,0:T(8,128)(2,1)S(1)}, bf16[24,1536]{1,0:T(8,128)(2,1)S(1)}, u32[]{:S(2)}, u32[]{:S(2)}) collective-permute-start(bf16[24,1536]{1,0:T(8,128)(2,1)S(1)} %pad_maximum_fusion.3), channel_id=1, source_target_pairs={{0,68},{8,11},{4,0},{12,15},{64,4},{72,75},{68,64},{76,79},{16,84}... | collective-permute-start | bytes 221192 | tf_op jit(solution)/shard_map/ppermute | solution.py:51
  15.8 3.4 %collective-permute-done.2 = bf16[24,1536]{1,0:T(8,128)(2,1)S(1)} collective-permute-done((bf16[24,1536]{1,0:T(8,128)(2,1)S(1)}, bf16[24,1536]{1,0:T(8,128)(2,1)S(1)}, u32[]{:S(2)}, u32[]{:S(2)}) %collective-permute-start.2) | collective-permute-done | bytes 73760 | tf_op jit(solution)/shard_map/ppermute | solution.py:51
  20.7 4.1 %collective-permute-start.9 = (bf16[96,1536]{1,0:T(8,128)(2,1)S(1)}, bf16[96,1536]{1,0:T(8,128)(2,1)S(1)}, u32[]{:S(2)}, u32[]{:S(2)}) collective-permute-start(bf16[96,1536]{1,0:T(8,128)(2,1)S(1)} %pad_maximum_fusion.2), channel_id=1, source_target_pairs={{0,48},{8,76},{4,52},{12,8},{64,112},{72,12},{68,116},{76,72},{16,... | collective-permute-start | bytes 884744 | tf_op jit(solution)/shard_map/ppermute | solution.py:51
  28.9 2.8 %collective-permute-done.9 = bf16[96,1536]{1,0:T(8,128)(2,1)S(1)} collective-permute-done((bf16[96,1536]{1,0:T(8,128)(2,1)S(1)}, bf16[96,1536]{1,0:T(8,128)(2,1)S(1)}, u32[]{:S(2)}, u32[]{:S(2)}) %collective-permute-start.9) | collective-permute-done | bytes 294944 | tf_op jit(solution)/shard_map/ppermute | solution.py:51
  32.1 3.1 %collective-permute-done.7 = bf16[96,1536]{1,0:T(8,128)(2,1)S(1)} collective-permute-done((bf16[96,1536]{1,0:T(8,128)(2,1)S(1)}, bf16[96,1536]{1,0:T(8,128)(2,1)S(1)}, u32[]{:S(2)}, u32[]{:S(2)}) %collective-permute-start.7) | collective-permute-done | bytes 294944 | tf_op jit(solution)/shard_map/ppermute | solution.py:51
  35.2 12.8 %collective-permute-start.11 = (bf16[384,1536]{1,0:T(8,128)(2,1)S(1)}, bf16[384,1536]{1,0:T(8,128)(2,1)S(1)}, u32[]{:S(2)}, u32[]{:S(2)}) collective-permute-start(bf16[384,1536]{1,0:T(8,128)(2,1)S(1)} %pad_maximum_fusion.w0.r0), channel_id=1, source_target_pairs={{0,3},{8,56},{4,7},{12,60},{64,67},{72,120},{68,71},{76,124},{16,1... | collective-permute-start | bytes 3538952 | tf_op jit(solution)/shard_map/ppermute | solution.py:51
  48.8 3.2 %shard_map.87.mine_ref = bf16[448,1536]{1,0:T(8,128)(2,1)S(1)} custom-call(s32[3]{0:T(128)S(1)} %pad_add_fusion.place_ref, bf16[448,1664]{1,0:T(8,128)(2,1)S(1)} %get-tuple-element.84.tokens_ref.amine_ref, s32[1,1536]{1,0:T(1,128)S(1)} %get-tuple-element.85.feature_ref), custom_call_target="tpu_custom_call" | custom-call | flops 1000 | bytes 1000 | tf_op jit(solution)/shard_map/pallas_call | solution.py:104
  52.0 9.1 %collective-permute-done.11.w3.r3 = bf16[384,1536]{1,0:T(8,128)(2,1)S(1)} collective-permute-done((bf16[384,1536]{1,0:T(8,128)(2,1)S(1)}, bf16[384,1536]{1,0:T(8,128)(2,1)S(1)}, u32[]{:S(2)}, u32[]{:S(2)}) %collective-permute-start.11) | collective-permute-done | bytes 1179680 | tf_op jit(solution)/shard_map/ppermute | solution.py:51
  61.1 3.1 %collective-permute-done.10.w1.r1 = bf16[384,1536]{1,0:T(8,128)(2,1)S(1)} collective-permute-done((bf16[384,1536]{1,0:T(8,128)(2,1)S(1)}, bf16[384,1536]{1,0:T(8,128)(2,1)S(1)}, u32[]{:S(2)}, u32[]{:S(2)}) %collective-permute-start.10) | collective-permute-done | bytes 1179680 | tf_op jit(solution)/shard_map/ppermute | solution.py:51
  65.9 3.2 %shard_map.88.other_ref = bf16[448,1536]{1,0:T(8,128)(2,1)S(1)} custom-call(s32[3]{0:T(128)S(1)} %pad_add_fusion.place_ref, bf16[448,1664]{1,0:T(8,128)(2,1)S(1)} %collective-permute-done.12.tokens_ref.aother_ref, s32[1,1536]{1,0:T(1,128)S(1)} %get-tuple-element.85.feature_ref), custom_call_target="tpu_custom_call" | custom-call | flops 1000 | bytes 1000 | tf_op jit(solution)/shard_map/pallas_call | solution.py:104
  69.1 2.6 %shard_map.90.sums_ref = f32[768,768]{1,0:T(8,128)S(1)} custom-call(s32[3]{0:T(128)S(1)} %pad_add_fusion.place_ref, bf16[384,1536]{1,0:T(8,128)(2,1)S(1)} %pad_maximum_fusion.w0.r0, bf16[384,1536]{1,0:T(8,128)(2,1)S(1)} %collective-permute-done.10.w1.r1, bf16[384,1536]{1,0:T(8,128)(2,1)S(1)} %collective-permute-done.11.w3.r3, ...), custom_call_target="tpu_custom_call" | custom-call | flops 1000 | bytes 1000 | tf_op jit(solution)/shard_map/pallas_call | solution.py:104
  76.1 4.4 %shard_map.89 = (bf16[896,1152]{1,0:T(8,128)(2,1)S(1)}, bf16[256,1536]{1,0:T(8,128)(2,1)S(1)}) custom-call(s32[3]{0:T(128)S(1)} %pad_add_fusion.place_ref, bf16[448,1536]{1,0:T(8,128)(2,1)S(1)} %shard_map.87.mine_ref, bf16[448,1536]{1,0:T(8,128)(2,1)S(1)} %shard_map.88.other_ref, bf16[384,1536]{1,0:T(8,128)(2,1)S(1)} %pad_maximum_fusion.w0.r0, ...), custom_call_target="tpu_custom_call" | custom-call | flops 1000 | bytes 1000 | tf_op jit(solution)/shard_map/pallas_call | solution.py:104
  80.5 11.1 %shard_map.92 = (bf16[256,384]{1,0:T(8,128)(2,1)S(1)}, bf16[256,1152]{1,0:T(8,128)(2,1)S(1)}, bf16[384,1152]{1,0:T(8,128)(2,1)S(1)}, bf16[384,1152]{1,0:T(8,128)...) custom-call(s32[3]{0:T(128)S(1)} %pad_add_fusion.place_ref, ...), custom_call_target="tpu_custom_call" | custom-call | flops 1000 | bytes 1000 | tf_op jit(solution)/shard_map/pallas_call | solution.py:104
  94.2 4.5 %shard_map.93 = (bf16[128,1536]{1,0:T(8,128)(2,1)S(1)}, bf16[128,1536]{1,0:T(8,128)(2,1)S(1)}) custom-call(s32[3]{0:T(128)S(1)} %pad_add_fusion.place_ref, bf16[256,1152]{1,0:T(8,128)(2,1)S(1)} %get-tuple-element.101.grads_ref, bf16[384,1536]{1,0:T(8,128)(2,1)S(1)} %pad_maximum_fusion.w0.r0, bf16[384,1536]{1,0:T(8,128)(2,1)S(1)} %collective-permute-done.10.w1.r1, ...), custom_call_target="tpu_custom_call" | custom-call | flops 1000 | bytes 1000 | tf_op jit(solution)/shard_map/pallas_call | solution.py:104
  99.9 3.3 %shard_map.94 = (bf16[384,384]{1,0:T(8,128)(2,1)S(1)}, bf16[384,384]{1,0:T(8,128)(2,1)S(1)}, bf16[384,384]{1,0:T(8,128)(2,1)S(1)}, bf16[384,384]{1,0:T(8,128)(2,1)S(1)}) custom-call(s32[3]{0:T(128)S(1)} %pad_add_fusion.place_ref, bf16[256,384]{1,0:T(8,128)(2,1)S(1)} %get-tuple-element.100.mine_ref, bf16[256,384]{1,0:T(8,128)(2,1)S(1)} %collective-permute-done.18.other_ref, ...), custom_call_target="tpu_custom_call" | custom-call | flops 1000 | bytes 1000 | tf_op jit(solution)/shard_map/pallas_call | solution.py:104
  103.2 2.2 %collective-permute-start.21 = (bf16[384,384]{1,0:T(8,128)(2,1)S(1)}, bf16[384,384]{1,0:T(8,128)(2,1)S(1)}, u32[]{:S(2)}, u32[]{:S(2)}) collective-permute-start(bf16[384,384]{1,0:T(8,128)(2,1)S(1)} %get-tuple-element.111), channel_id=1, source_target_pairs={{0,3},{8,56},{4,7},{12,60},{64,67},{72,120},{68,71},{76,124},{16,1... | collective-permute-start | bytes 884744 | tf_op jit(solution)/shard_map/ppermute | solution.py:51
  106.0 7.7 %collective-permute-start.23 = (bf16[384,384]{1,0:T(8,128)(2,1)S(1)}, bf16[384,384]{1,0:T(8,128)(2,1)S(1)}, u32[]{:S(2)}, u32[]{:S(2)}) collective-permute-start(bf16[384,384]{1,0:T(8,128)(2,1)S(1)} %get-tuple-element.113), channel_id=1, source_target_pairs={{0,1},{8,24},{4,5},{12,28},{64,65},{72,88},{68,69},{76,92},{16,17}... | collective-permute-start | bytes 884744 | tf_op jit(solution)/shard_map/ppermute | solution.py:51
  118.2 3.1 %collective-permute-done.23 = bf16[384,384]{1,0:T(8,128)(2,1)S(1)} collective-permute-done((bf16[384,384]{1,0:T(8,128)(2,1)S(1)}, bf16[384,384]{1,0:T(8,128)(2,1)S(1)}, u32[]{:S(2)}, u32[]{:S(2)}) %collective-permute-start.23) | collective-permute-done | bytes 294944 | tf_op jit(solution)/shard_map/ppermute | solution.py:51
  121.6 4.8 %collective-permute-start.24 = (bf16[96,1536]{1,0:T(8,128)(2,1)S(1)}, bf16[96,1536]{1,0:T(8,128)(2,1)S(1)}, u32[]{:S(2)}, u32[]{:S(2)}) collective-permute-start(bf16[96,1536]{1,0:T(8,128)(2,1)S(1)} %get-tuple-element.134), channel_id=1, source_target_pairs={{0,48},{8,76},{4,52},{12,8},{64,112},{72,12},{68,116},{76,72},{16,... | collective-permute-start | bytes 884744 | tf_op jit(solution)/shard_map/ppermute | solution.py:51
  130.0 6.3 %collective-permute-done.26 = bf16[96,1536]{1,0:T(8,128)(2,1)S(1)} collective-permute-done((bf16[96,1536]{1,0:T(8,128)(2,1)S(1)}, bf16[96,1536]{1,0:T(8,128)(2,1)S(1)}, u32[]{:S(2)}, u32[]{:S(2)}) %collective-permute-start.26) | collective-permute-done | bytes 294944 | tf_op jit(solution)/shard_map/ppermute | solution.py:51
  136.6 2.1 %collective-permute-start.28 = (bf16[24,1536]{1,0:T(8,128)(2,1)S(1)}, bf16[24,1536]{1,0:T(8,128)(2,1)S(1)}, u32[]{:S(2)}, u32[]{:S(2)}) collective-permute-start(bf16[24,1536]{1,0:T(8,128)(2,1)S(1)} %get-tuple-element.138), channel_id=1, source_target_pairs={{0,64},{8,10},{4,68},{12,14},{64,0},{72,74},{68,4},{76,78},{16,80}... | collective-permute-start | bytes 221192 | tf_op jit(solution)/shard_map/ppermute | solution.py:51
  139.2 2.5 %collective-permute-done.29.back_ref = bf16[24,1536]{1,0:T(8,128)(2,1)S(1)} collective-permute-done((bf16[24,1536]{1,0:T(8,128)(2,1)S(1)}, bf16[24,1536]{1,0:T(8,128)(2,1)S(1)}, u32[]{:S(2)}, u32[]{:S(2)}) %collective-permute-start.29) | collective-permute-done | bytes 73760 | tf_op jit(solution)/shard_map/ppermute | solution.py:51
  143.2 2.8 %collective-permute-start.30 = (f32[12,1536]{1,0:T(8,128)S(1)}, f32[12,1536]{1,0:T(8,128)S(1)}, u32[]{:S(2)}, u32[]{:S(2)}) collective-permute-start(f32[12,1536]{1,0:T(8,128)S(1)} %get-tuple-element.119), channel_id=1, source_target_pairs={{0,8},{8,0},{1,9},{9,1},{2,10},{10,2},{3,11},{11,3},{4,12},{12,4},... | collective-permute-start | bytes 221192 | tf_op jit(solution)/shard_map/ppermute | solution.py:55
  (104 shorter events, 40.4 us)
Async XLA Ops:
  2.8 5.7 %collective-permute-start = (bf16[12,1536]{1,0:T(8,128)(2,1)S(1)}, bf16[12,1536]{1,0:T(8,128)(2,1)S(1)}, u32[]{:S(2)}, u32[]{:S(2)}) collective-permute-start(bf16[12,1536]{1,0:T(8,128)(2,1)S(1)} %get-tuple-element.142), channel_id=1, source_target_pairs={{0,8},{8,0},{1,9},{9,1},{2,10},{10,2},{3,11},{11,3},{4,12},{12,4},... | collective-permute-start | bytes 110600 | tf_op jit(solution)/shard_map/ppermute | solution.py:55
  8.6 11.3 %collective-permute-start.4 = (bf16[144,1664]{1,0:T(8,128)(2,1)S(1)}, bf16[144,1664]{1,0:T(8,128)(2,1)S(1)}, u32[]{:S(2)}, u32[]{:S(2)}) collective-permute-start(bf16[144,1664]{1,0:T(8,128)(2,1)S(1)} %get-tuple-element.72), channel_id=1, source_target_pairs={{8,16},{16,8},{24,32},{32,24},{40,48},{48,40},{56,64},{64,56},{72,... | collective-permute-start | bytes 1437704 | tf_op jit(solution)/shard_map/ppermute | solution.py:60
  20.7 10.9 %collective-permute-start.9 = (bf16[96,1536]{1,0:T(8,128)(2,1)S(1)}, bf16[96,1536]{1,0:T(8,128)(2,1)S(1)}, u32[]{:S(2)}, u32[]{:S(2)}) collective-permute-start(bf16[96,1536]{1,0:T(8,128)(2,1)S(1)} %pad_maximum_fusion.2), channel_id=1, source_target_pairs={{0,48},{8,76},{4,52},{12,8},{64,112},{72,12},{68,116},{76,72},{16,... | collective-permute-start | bytes 884744 | tf_op jit(solution)/shard_map/ppermute | solution.py:51
  24.9 7.2 %collective-permute-start.8 = (bf16[96,1536]{1,0:T(8,128)(2,1)S(1)}, bf16[96,1536]{1,0:T(8,128)(2,1)S(1)}, u32[]{:S(2)}, u32[]{:S(2)}) collective-permute-start(bf16[96,1536]{1,0:T(8,128)(2,1)S(1)} %pad_maximum_fusion.2), channel_id=1, source_target_pairs={{0,32},{8,72},{4,36},{12,76},{64,96},{72,8},{68,100},{76,12},{16,4... | collective-permute-start | bytes 884744 | tf_op jit(solution)/shard_map/ppermute | solution.py:51
  24.9 10.2 %collective-permute-start.7 = (bf16[96,1536]{1,0:T(8,128)(2,1)S(1)}, bf16[96,1536]{1,0:T(8,128)(2,1)S(1)}, u32[]{:S(2)}, u32[]{:S(2)}) collective-permute-start(bf16[96,1536]{1,0:T(8,128)(2,1)S(1)} %pad_maximum_fusion.2), channel_id=1, source_target_pairs={{0,16},{8,12},{4,20},{12,72},{64,80},{72,76},{68,84},{76,8},{16,32... | collective-permute-start | bytes 884744 | tf_op jit(solution)/shard_map/ppermute | solution.py:51
  25.6 22.4 %collective-permute-start.5 = (bf16[160,1664]{1,0:T(8,128)(2,1)S(1)}, bf16[160,1664]{1,0:T(8,128)(2,1)S(1)}, u32[]{:S(2)}, u32[]{:S(2)}) collective-permute-start(bf16[160,1664]{1,0:T(8,128)(2,1)S(1)} %get-tuple-element.82), channel_id=1, source_target_pairs={{0,1},{1,2},{2,3},{3,4},{4,5},{5,6},{6,7},{8,9},{9,10},{10,11},{11... | collective-permute-start | bytes 1597448 | tf_op jit(solution)/shard_map/ppermute | solution.py:65
  27.6 20.4 %collective-permute-start.6 = (bf16[160,1664]{1,0:T(8,128)(2,1)S(1)}, bf16[160,1664]{1,0:T(8,128)(2,1)S(1)}, u32[]{:S(2)}, u32[]{:S(2)}) collective-permute-start(bf16[160,1664]{1,0:T(8,128)(2,1)S(1)} %get-tuple-element.83), channel_id=1, source_target_pairs={{1,0},{2,1},{3,2},{4,3},{5,4},{6,5},{7,6},{9,8},{10,9},{11,10},{12... | collective-permute-start | bytes 1597448 | tf_op jit(solution)/shard_map/ppermute | solution.py:65
  35.2 25.9 %collective-permute-start.11 = (bf16[384,1536]{1,0:T(8,128)(2,1)S(1)}, bf16[384,1536]{1,0:T(8,128)(2,1)S(1)}, u32[]{:S(2)}, u32[]{:S(2)}) collective-permute-start(bf16[384,1536]{1,0:T(8,128)(2,1)S(1)} %pad_maximum_fusion.w0.r0), channel_id=1, source_target_pairs={{0,3},{8,56},{4,7},{12,60},{64,67},{72,120},{68,71},{76,124},{16,1... | collective-permute-start | bytes 3538952 | tf_op jit(solution)/shard_map/ppermute | solution.py:51
  48.0 16.3 %collective-permute-start.10 = (bf16[384,1536]{1,0:T(8,128)(2,1)S(1)}, bf16[384,1536]{1,0:T(8,128)(2,1)S(1)}, u32[]{:S(2)}, u32[]{:S(2)}) collective-permute-start(bf16[384,1536]{1,0:T(8,128)(2,1)S(1)} %pad_maximum_fusion.w0.r0), channel_id=1, source_target_pairs={{0,1},{8,24},{4,5},{12,28},{64,65},{72,88},{68,69},{76,92},{16,17}... | collective-permute-start | bytes 3538952 | tf_op jit(solution)/shard_map/ppermute | solution.py:51
  48.7 17.1 %collective-permute-start.12 = (bf16[448,1664]{1,0:T(8,128)(2,1)S(1)}, bf16[448,1664]{1,0:T(8,128)(2,1)S(1)}, u32[]{:S(2)}, u32[]{:S(2)}) collective-permute-start(bf16[448,1664]{1,0:T(8,128)(2,1)S(1)} %get-tuple-element.84.tokens_ref.amine_ref), channel_id=1, source_target_pairs={{0,8},{8,0},{1,9},{9,1},{2,10},{10,2},{3,11},{11,3},{4,12},{12,4},... | collective-permute-start | bytes 4472840 | tf_op jit(solution)/shard_map/ppermute | solution.py:55
  64.3 8.8 %collective-permute-start.14 = (bf16[192,1536]{1,0:T(8,128)(2,1)S(1)}, bf16[192,1536]{1,0:T(8,128)(2,1)S(1)}, u32[]{:S(2)}, u32[]{:S(2)}) collective-permute-start(bf16[192,1536]{1,0:T(8,128)(2,1)S(1)} %slice.63), channel_id=1, source_target_pairs={{0,3},{8,56},{4,7},{12,60},{64,67},{72,120},{68,71},{76,124},{16,1... | collective-permute-start | bytes 1769480 | tf_op jit(solution)/shard_map/ppermute | solution.py:51
  64.4 10.0 %collective-permute-start.13 = (bf16[192,1536]{1,0:T(8,128)(2,1)S(1)}, bf16[192,1536]{1,0:T(8,128)(2,1)S(1)}, u32[]{:S(2)}, u32[]{:S(2)}) collective-permute-start(bf16[192,1536]{1,0:T(8,128)(2,1)S(1)} %slice.62), channel_id=1, source_target_pairs={{0,1},{8,24},{4,5},{12,28},{64,65},{72,88},{68,69},{76,92},{16,17}... | collective-permute-start | bytes 1769480 | tf_op jit(solution)/shard_map/ppermute | solution.py:51
  65.9 14.6 %collective-permute-start.15 = (bf16[288,1664]{1,0:T(8,128)(2,1)S(1)}, bf16[288,1664]{1,0:T(8,128)(2,1)S(1)}, u32[]{:S(2)}, u32[]{:S(2)}) collective-permute-start(bf16[288,1664]{1,0:T(8,128)(2,1)S(1)} %get-tuple-element.94.gmine_ref), channel_id=1, source_target_pairs={{0,8},{8,0},{1,9},{9,1},{2,10},{10,2},{3,11},{11,3},{4,12},{12,4},... | collective-permute-start | bytes 2875400 | tf_op jit(solution)/shard_map/ppermute | solution.py:55
  91.6 14.3 %collective-permute-start.17 = (bf16[384,1152]{1,0:T(8,128)(2,1)S(1)}, bf16[384,1152]{1,0:T(8,128)(2,1)S(1)}, u32[]{:S(2)}, u32[]{:S(2)}) collective-permute-start(bf16[384,1152]{1,0:T(8,128)(2,1)S(1)} %get-tuple-element.99), channel_id=1, source_target_pairs={{0,3},{8,56},{4,7},{12,60},{64,67},{72,120},{68,71},{76,124},{16,1... | collective-permute-start | bytes 2654216 | tf_op jit(solution)/shard_map/ppermute | solution.py:51
  91.7 22.1 %collective-permute-start.19 = (bf16[384,1152]{1,0:T(8,128)(2,1)S(1)}, bf16[384,1152]{1,0:T(8,128)(2,1)S(1)}, u32[]{:S(2)}, u32[]{:S(2)}) collective-permute-start(bf16[384,1152]{1,0:T(8,128)(2,1)S(1)} %get-tuple-element.108), channel_id=1, source_target_pairs={{0,2},{8,40},{4,6},{12,44},{64,66},{72,104},{68,70},{76,108},{16,1... | collective-permute-start | bytes 2654216 | tf_op jit(solution)/shard_map/ppermute | solution.py:51
  93.6 21.3 %collective-permute-start.20 = (bf16[384,1152]{1,0:T(8,128)(2,1)S(1)}, bf16[384,1152]{1,0:T(8,128)(2,1)S(1)}, u32[]{:S(2)}, u32[]{:S(2)}) collective-permute-start(bf16[384,1152]{1,0:T(8,128)(2,1)S(1)} %get-tuple-element.109), channel_id=1, source_target_pairs={{0,1},{8,24},{4,5},{12,28},{64,65},{72,88},{68,69},{76,92},{16,17}... | collective-permute-start | bytes 2654216 | tf_op jit(solution)/shard_map/ppermute | solution.py:51
  103.2 13.4 %collective-permute-start.21 = (bf16[384,384]{1,0:T(8,128)(2,1)S(1)}, bf16[384,384]{1,0:T(8,128)(2,1)S(1)}, u32[]{:S(2)}, u32[]{:S(2)}) collective-permute-start(bf16[384,384]{1,0:T(8,128)(2,1)S(1)} %get-tuple-element.111), channel_id=1, source_target_pairs={{0,3},{8,56},{4,7},{12,60},{64,67},{72,120},{68,71},{76,124},{16,1... | collective-permute-start | bytes 884744 | tf_op jit(solution)/shard_map/ppermute | solution.py:51
  105.3 12.8 %collective-permute-start.22 = (bf16[384,384]{1,0:T(8,128)(2,1)S(1)}, bf16[384,384]{1,0:T(8,128)(2,1)S(1)}, u32[]{:S(2)}, u32[]{:S(2)}) collective-permute-start(bf16[384,384]{1,0:T(8,128)(2,1)S(1)} %get-tuple-element.112), channel_id=1, source_target_pairs={{0,2},{8,40},{4,6},{12,44},{64,66},{72,104},{68,70},{76,108},{16,1... | collective-permute-start | bytes 884744 | tf_op jit(solution)/shard_map/ppermute | solution.py:51
  106.0 15.2 %collective-permute-start.23 = (bf16[384,384]{1,0:T(8,128)(2,1)S(1)}, bf16[384,384]{1,0:T(8,128)(2,1)S(1)}, u32[]{:S(2)}, u32[]{:S(2)}) collective-permute-start(bf16[384,384]{1,0:T(8,128)(2,1)S(1)} %get-tuple-element.113), channel_id=1, source_target_pairs={{0,1},{8,24},{4,5},{12,28},{64,65},{72,88},{68,69},{76,92},{16,17}... | collective-permute-start | bytes 884744 | tf_op jit(solution)/shard_map/ppermute | solution.py:51
  121.6 8.4 %collective-permute-start.24 = (bf16[96,1536]{1,0:T(8,128)(2,1)S(1)}, bf16[96,1536]{1,0:T(8,128)(2,1)S(1)}, u32[]{:S(2)}, u32[]{:S(2)}) collective-permute-start(bf16[96,1536]{1,0:T(8,128)(2,1)S(1)} %get-tuple-element.134), channel_id=1, source_target_pairs={{0,48},{8,76},{4,52},{12,8},{64,112},{72,12},{68,116},{76,72},{16,... | collective-permute-start | bytes 884744 | tf_op jit(solution)/shard_map/ppermute | solution.py:51
  126.3 9.9 %collective-permute-start.26 = (bf16[96,1536]{1,0:T(8,128)(2,1)S(1)}, bf16[96,1536]{1,0:T(8,128)(2,1)S(1)}, u32[]{:S(2)}, u32[]{:S(2)}) collective-permute-start(bf16[96,1536]{1,0:T(8,128)(2,1)S(1)} %get-tuple-element.135), channel_id=1, source_target_pairs={{0,16},{8,12},{4,20},{12,72},{64,80},{72,76},{68,84},{76,8},{16,32... | collective-permute-start | bytes 884744 | tf_op jit(solution)/shard_map/ppermute | solution.py:51
  126.4 9.9 %collective-permute-start.25 = (bf16[96,1536]{1,0:T(8,128)(2,1)S(1)}, bf16[96,1536]{1,0:T(8,128)(2,1)S(1)}, u32[]{:S(2)}, u32[]{:S(2)}) collective-permute-start(bf16[96,1536]{1,0:T(8,128)(2,1)S(1)} %get-tuple-element.136), channel_id=1, source_target_pairs={{0,32},{8,72},{4,36},{12,76},{64,96},{72,8},{68,100},{76,12},{16,4... | collective-permute-start | bytes 884744 | tf_op jit(solution)/shard_map/ppermute | solution.py:51
  127.6 18.4 %collective-permute-start.31 = (f32[128,768]{1,0:T(8,128)S(1)}, f32[128,768]{1,0:T(8,128)S(1)}, u32[]{:S(2)}, u32[]{:S(2)}) collective-permute-start(f32[128,768]{1,0:T(8,128)S(1)} %get-tuple-element.121), channel_id=1, source_target_pairs={{0,8},{8,0},{1,9},{9,1},{2,10},{10,2},{3,11},{11,3},{4,12},{12,4},... | collective-permute-start | bytes 1179656 | tf_op jit(solution)/shard_map/ppermute | solution.py:55
  127.6 18.4 %collective-permute-start.32 = (bf16[128,1536]{1,0:T(8,128)(2,1)S(1)}, bf16[128,1536]{1,0:T(8,128)(2,1)S(1)}, u32[]{:S(2)}, u32[]{:S(2)}) collective-permute-start(bf16[128,1536]{1,0:T(8,128)(2,1)S(1)} %get-tuple-element.123), channel_id=1, source_target_pairs={{0,8},{8,0},{1,9},{9,1},{2,10},{10,2},{3,11},{11,3},{4,12},{12,4},... | collective-permute-start | bytes 1179656 | tf_op jit(solution)/shard_map/ppermute | solution.py:55
  (13 other events, 93.8 us)
